TPU v7x, 512 devices: a whole 4x8x8 slice. The times are simulated.
512 devices in a mesh: tok: 16 (over z, core), hid: 32 (over y, x).
Axes of the slice: x: 4, y: 8, z: 8, core: 2. Of those that a mesh axis runs over, the one named last changes fastest.
Arguments:
- activations: bfloat16 [2048, 4096], P('tok'), may hold values from -12 to 12
- cotangent: bfloat16 [2048, 8192], P('tok', 'hid'), may hold values from -0.0078125 to 0.0078125
- left_gram: float32 [32, 1024, 1024], P('hid', 'tok'), may hold values from -0.28125 to 30, as said below
- right_gram: float32 [32, 1024, 1024], P('hid', 'tok'), may hold values from -0.28125 to 30, as said below
- left_root: float32 [32, 1024, 1024], P('hid', 'tok'), may hold values from -0.0115625 to 1.21, as said below
- right_root: float32 [32, 1024, 1024], P('hid', 'tok'), may hold values from -0.0115625 to 1.21, as said below
Outputs:
- left_next: float32 [32, 1024, 1024], P('hid', 'tok')
- right_next: float32 [32, 1024, 1024], P('hid', 'tok')
- left_refined: float32 [32, 1024, 1024], P('hid', 'tok')
- right_refined: float32 [32, 1024, 1024], P('hid', 'tok')
- update: float32 [4, 1024, 8192], P(None, 'tok', 'hid')
Inputs may be any that keep to these rules, and one draw needn't show every extreme that they name: `left_gram`: every block is symmetric and positive definite. `right_gram`: every block is symmetric and positive definite. `left_root`: every block is symmetric. `right_root`: every block is symmetric.
All inputs are finite; a program needn't handle non-finite values.
Results may differ from a plain program's by a relative error of at most 0.019.
Values may be sent and summed in bfloat16 or wider, within the bound.
No kernel may reach another device: no remote copies, remote signals or barrier semaphores. Data moves between devices by JAX's collectives and lax.ppermute only.
A program may use at most 64 MiB of HBM per device.

v0:
```python
import jax
import jax.numpy as jnp
from jax import lax
from jax.sharding import PartitionSpec as P

BETA = 0.95
EPS = 1e-06


def partner(block, axis, bit):
    count = lax.axis_size(axis)
    route = []
    for low in range(count):
        high = low | 1 << bit
        if high != low and high < count:
            route += [(low, high), (high, low)]
    return lax.ppermute(block, axis, route)


def sent_together(arrays, axis, dim, along):
    widths = [a.shape[along] for a in arrays]
    both = jnp.concatenate(arrays, axis=along)
    whole = lax.all_gather(both, axis, axis=dim, tiled=True)
    return tuple(jnp.split(whole, [sum(widths[:k]) for k in range(1, len(widths))], axis=along))


def split_up(value, dim, length):
    lengths = value.shape
    parts = value.reshape(*lengths[:dim], length, lengths[dim] // length, *lengths[dim + 1 :])
    return jnp.moveaxis(parts, dim, 0)


def sent_and_summed(value, axis, dim):
    length = lax.axis_size(axis)
    parts = lax.all_to_all(split_up(value, dim, length), axis, 0, 0, tiled=True)
    return jnp.sum(parts.astype(jnp.float32), axis=0)


def sent_to_all(value, axis):
    copies = jnp.broadcast_to(value, (lax.axis_size(axis), *value.shape))
    return lax.all_to_all(copies, axis, split_axis=0, concat_axis=0, tiled=True)


def of_everyone(value, axis):
    everything = sent_to_all(value, axis)
    return jnp.sum(everything, axis=0)


def newton_rows(gram_rows, root_full, root_rows):
    product = gram_rows.astype(jnp.bfloat16)
    for repeat in range(4):
        product = jnp.einsum(
            "brk,bkc->brc", product, root_full, preferred_element_type=jnp.float32
        ).astype(jnp.bfloat16)
    final = jnp.einsum("brk,bkc->brc", product, root_full, preferred_element_type=jnp.float32)
    return (5.0 * root_rows - final) / 4.0


def butterfly(pieces, swapper):
    group_size = pieces.shape[0]
    position = lax.axis_index("hid") % group_size
    ordering = jnp.bitwise_xor(jnp.arange(group_size, dtype=jnp.int32), position)
    holding = jnp.take(pieces, ordering, axis=0)
    for bit_level in range(group_size.bit_length() - 1):
        stride = 1 << bit_level
        shaped = holding.reshape((group_size // (2 * stride), 2, stride) + holding.shape[1:])
        incoming = swapper(shaped[:, 1], bit_level)
        holding = jnp.stack([shaped[:, 0], incoming], axis=1).reshape(holding.shape)
    return jnp.take(holding, ordering, axis=0)


def swap_slabs(portion, bit_level):
    return partner(portion, "hid", bit_level)


def swap_updates(portion, bit_level):
    return partner(portion.astype(jnp.bfloat16), "hid", bit_level).astype(portion.dtype)


def make_folder(own_rows, root_low_rows, first_row):
    slab_rows = own_rows.shape[1]

    def absorb(running, portion, offset):
        column_slab = lax.dynamic_slice_in_dim(portion, first_row, slab_rows, 2)
        products = jnp.einsum("brk,bnk->brn", own_rows, portion, preferred_element_type=jnp.float32)
        right_rows = jnp.einsum(
            "bnr,bnk->brk", column_slab, portion, preferred_element_type=jnp.float32
        )
        left_applied = jnp.einsum(
            "brn,bnk->brk", root_low_rows, portion, preferred_element_type=jnp.float32
        )
        return (products, right_rows, left_applied)

    return absorb


def on_device(activations, cotangent, left_gram, right_gram, left_root, right_root):
    owned_blocks, slab_rows, block_size = left_gram.shape
    slab_width = cotangent.shape[1]
    group_size = block_size // slab_width
    block_rows = activations.shape[1] // block_size
    partial_value = jnp.einsum(
        "td,tc->dc", activations, cotangent, preferred_element_type=jnp.float32
    )
    partial_value = partial_value.reshape(block_rows, block_size, slab_width)
    first_row = lax.axis_index("tok") * slab_rows
    left_low = left_root.astype(jnp.bfloat16)
    right_low = right_root.astype(jnp.bfloat16)
    left_full, right_full = sent_together((left_low, right_low), "tok", 1, 0)
    empty = jnp.zeros((owned_blocks, slab_rows, block_size), jnp.float32)
    initial = (empty, empty, empty)
    summed = sent_and_summed(partial_value.astype(jnp.bfloat16), "tok", 1).astype(jnp.bfloat16)
    pieces = summed.reshape(group_size, owned_blocks, slab_rows, slab_width)
    arrived = butterfly(pieces, swap_slabs)
    own_rows = arrived.transpose(1, 2, 0, 3).reshape(owned_blocks, slab_rows, block_size)
    folder = make_folder(own_rows, left_low, first_row)
    left_cols, right_rows, left_applied = folder(
        initial, lax.all_gather(own_rows, "tok", axis=1, tiled=True), jnp.int32(0)
    )
    left_next = BETA * left_gram + left_cols
    right_next = BETA * right_gram + right_rows
    left_refined = newton_rows(left_next, left_full, left_root)
    right_refined = newton_rows(right_next, right_full, right_root)
    precond = jnp.einsum(
        "brk,bkc->brc",
        left_applied.astype(jnp.bfloat16),
        right_full,
        preferred_element_type=jnp.float32,
    )
    squares = of_everyone(jnp.sum(precond * precond, axis=(1, 2)), "tok")
    scale = jnp.sqrt(squares / (block_size * block_size) + EPS)
    scaled = precond / scale[:, None, None]
    outgoing = scaled.reshape(owned_blocks, slab_rows, group_size, slab_width).transpose(2, 0, 1, 3)
    returned = butterfly(outgoing, swap_updates)
    update = returned.reshape(block_rows, slab_rows, slab_width)
    return (left_next, right_next, left_refined, right_refined, update)


def solution(mesh):
    in_specs = (
        P("tok", None),
        P("tok", "hid"),
        P("hid", "tok", None),
        P("hid", "tok", None),
        P("hid", "tok", None),
        P("hid", "tok", None),
    )
    out_specs = (
        P("hid", "tok", None),
        P("hid", "tok", None),
        P("hid", "tok", None),
        P("hid", "tok", None),
        P(None, "tok", "hid"),
    )
    return jax.shard_map(
        on_device, mesh=mesh, in_specs=in_specs, out_specs=out_specs, check_vma=False
    )
```

profile of v0, /device:TPU:1, one launch (start us, length us, event | category | flops | bytes accessed | tf_op | source)
XLA Modules:
  0.0 204.0 jit_solution(1630706581589492874)
XLA Ops:
  7.2 1.0 convert_element_type.87
  10.0 1.6 convolution_convert_fusion
  11.6 1.5 copy.76
  13.1 11.8 %all-to-all-start = ((bf16[16,4,64,256]{3,2,1,0:T(8,128)(2,1)}), bf16[16,4,64,256]{3,2,1,0:T(8,128)(2,1)S(1)}, u32[]{:S(2)}, u32[]{:S(2)}) async-start(bf16[16,4,64,256]{3,2,1,0:T(8,128)(2,1)} %bitcast.152), calls=%async_computation | async-start | bytes 4194304 | tf_op jit(solution)/shard_map/all_to_all | solution.py:35
  25.0 65.2 %all-to-all-done = bf16[16,4,64,256]{3,2,1,0:T(8,128)(2,1)S(1)} async-done(((bf16[16,4,64,256]{3,2,1,0:T(8,128)(2,1)}), bf16[16,4,64,256]{3,2,1,0:T(8,128)(2,1)S(1)}, u32[]{:S(2)}, u32[]{:S(2)}) %all-to-all-start) | async-done | bytes 2097184 | tf_op jit(solution)/shard_map/all_to_all | solution.py:35
  91.2 3.1 %collective-permute-start = (bf16[2,1,1,64,256]{4,3,0,2,1:T(8,128)(2,1)S(1)}, bf16[2,1,1,64,256]{4,3,0,2,1:T(8,128)(2,1)S(1)}, u32[]{:S(2)}, u32[]{:S(2)}) collective-permute-start(bf16[2,1,1,64,256]{4,3,0,2,1:T(8,128)(2,1)S(1)} %get-tuple-element.12), channel_id=1, source_target_pairs={{0,1},{1,0},{2,3},{3,2},{4,5},{5,4},{6,7},{7,6},{8,9},{9,8},{10,11... | collective-permute-start | bytes 196616 | tf_op jit(solution)/shard_map/ppermute | solution.py:17
  94.4 2.4 %collective-permute-done = bf16[2,1,1,64,256]{4,3,0,2,1:T(8,128)(2,1)S(1)} collective-permute-done((bf16[2,1,1,64,256]{4,3,0,2,1:T(8,128)(2,1)S(1)}, bf16[2,1,1,64,256]{4,3,0,2,1:T(8,128)(2,1)S(1)}, u32[]{:S(2)}, u32[]{:S(2)}) %collective-permute-start) | collective-permute-done | bytes 65568 | tf_op jit(solution)/shard_map/ppermute | solution.py:17
  96.8 4.7 %collective-permute-start.1 = (bf16[1,2,1,64,256]{4,3,1,2,0:T(8,128)(2,1)S(1)}, bf16[1,2,1,64,256]{4,3,1,2,0:T(8,128)(2,1)S(1)}, u32[]{:S(2)}, u32[]{:S(2)}) collective-permute-start(bf16[1,2,1,64,256]{4,3,1,2,0:T(8,128)(2,1)S(1)} %get-tuple-element.10), channel_id=1, source_target_pairs={{0,2},{2,0},{1,3},{3,1},{4,6},{6,4},{5,7},{7,5},{8,10},{10,8},{9,1... | collective-permute-start | bytes 196616 | tf_op jit(solution)/shard_map/ppermute | solution.py:17
  101.5 1.9 collective-permute-done.1
  105.5 44.8 %all-gather.3.cloned.1.call-done = bf16[1,1024,1024]{2,1,0:T(8,128)(2,1)} async-done(((bf16[1,64,1024]{2,1,0:T(8,128)(2,1)}), bf16[1,1024,1024]{2,1,0:T(8,128)(2,1)}) %all-gather.3.cloned.1.call-update) | async-done | bytes 2097168 | tf_op jit(solution)/shard_map/all_gather | solution.py:118
  150.2 3.8 %multiply_reduce_fusion = (f32[]{:T(128)}, f32[64,1024]{1,0:T(8,128)S(1)}) fusion(bf16[2,1024,1024]{2,1,0:T(8,128)(2,1)} %all-gather.5.cloned.1.call-done, bf16[1,1024,1024]{2,1,0:T(8,128)(2,1)} %all-gather.3.cloned.1.call-done, bf16[1,64,1024]{2,1,0:T(8,128)(2,1)S(1)} %convert_element_type.87), kind=kOutput, calls=%fused_computation.42 | convolution fusion | flops 268632064 | bytes 4587524 | tf_op jit(solution)/shard_map/brk,bkc->brc/dot_general | solution.py:124
  154.1 1.2 broadcast_in_dim.22
  155.3 4.4 %all-to-all-start.1 = ((f32[16,1,1]{2,1,0:T(1,128)}), f32[16,1,1]{2,1,0:T(1,128)S(1)}, u32[]{:S(2)}, u32[]{:S(2)}) async-start(f32[16,1,1]{2,1,0:T(1,128)} %broadcast_in_dim.22), calls=%async_computation.1 | async-start | bytes 16384 | tf_op jit(solution)/shard_map/all_to_all | solution.py:41
  159.8 2.3 %fusion.16 = f32[1,64,1024]{2,1,0:T(8,128)} fusion(bf16[1,1024,1024]{2,1,0:T(8,128)(2,1)S(1)} %copy-done.1, s32[]{:T(128)S(6)} %select_n.42, f32[1,64,1024]{2,1,0:T(8,128)} %param.13), kind=kOutput, calls=%fused_computation.22 | convolution fusion | flops 134348800 | bytes 2883588 | tf_op jit(solution)/shard_map/bnr,bnk->brk/dot_general | solution.py:86
  162.0 3.1 %convolution_convert_fusion.3 = bf16[64,1024]{1,0:T(8,128)(2,1)S(1)} fusion(bf16[2,1024,1024]{2,1,0:T(8,128)(2,1)} %all-gather.5.cloned.1.call-done, f32[1,64,1024]{2,1,0:T(8,128)} %fusion.16), kind=kOutput, calls=%fused_computation.27 | convolution fusion | flops 268632064 | bytes 4587520 | tf_op jit(solution)/shard_map/brk,bkc->brc/dot_general | solution.py:52
  165.2 2.7 %convolution_convert_fusion.2 = bf16[64,1024]{1,0:T(8,128)(2,1)} fusion(bf16[64,1024]{1,0:T(8,128)(2,1)S(1)} %convolution_convert_fusion.3, bf16[2,1024,1024]{2,1,0:T(8,128)(2,1)} %all-gather.5.cloned.1.call-done), kind=kOutput, calls=%fused_computation.26 | convolution fusion | flops 134283264 | bytes 2359296 | tf_op jit(solution)/shard_map/brk,bkc->brc/dot_general | solution.py:52
  167.9 3.9 %fusion.13 = f32[1,64,1024]{2,1,0:T(8,128)} fusion(bf16[64,1024]{1,0:T(8,128)(2,1)} %convolution_convert_fusion.2, bf16[2,1024,1024]{2,1,0:T(8,128)(2,1)} %all-gather.5.cloned.1.call-done, f32[1,64,1024]{2,1,0:T(8,128)} %param.15), kind=kOutput, calls=%fused_computation.18 | convolution fusion | flops 268697600 | bytes 4849664 | tf_op jit(solution)/shard_map/brk,bkc->brc/dot_general | solution.py:55
  171.8 2.4 %fusion.19 = f32[1,64,1024]{2,1,0:T(8,128)} fusion(bf16[64,1024]{1,0:T(8,128)(2,1)S(1)} %bitcast.162, bf16[1,1024,1024]{2,1,0:T(8,128)(2,1)S(1)} %copy-done.1, f32[1,64,1024]{2,1,0:T(8,128)} %param.12), kind=kOutput, calls=%fused_computation.23 | convolution fusion | flops 134348800 | bytes 2752512 | tf_op jit(solution)/shard_map/brk,bnk->brn/dot_general | solution.py:85
  174.2 3.1 %convolution_convert_fusion.7 = bf16[64,1024]{1,0:T(8,128)(2,1)S(1)} fusion(bf16[2,1024,1024]{2,1,0:T(8,128)(2,1)} %all-gather.5.cloned.1.call-done, f32[1,64,1024]{2,1,0:T(8,128)} %fusion.19), kind=kOutput, calls=%fused_computation.31 | convolution fusion | flops 268632064 | bytes 4587520 | tf_op jit(solution)/shard_map/brk,bkc->brc/dot_general | solution.py:52
  177.4 2.1 %convolution_convert_fusion.6 = bf16[64,1024]{1,0:T(8,128)(2,1)S(1)} fusion(bf16[64,1024]{1,0:T(8,128)(2,1)S(1)} %convolution_convert_fusion.7, bf16[2,1024,1024]{2,1,0:T(8,128)(2,1)} %all-gather.5.cloned.1.call-done), kind=kOutput, calls=%fused_computation.30 | convolution fusion | flops 134283264 | bytes 2359296 | tf_op jit(solution)/shard_map/brk,bkc->brc/dot_general | solution.py:52
  181.7 3.1 %collective-permute-start.2 = (bf16[2,1,1,64,256]{4,3,0,2,1:T(8,128)(2,1)S(1)}, bf16[2,1,1,64,256]{4,3,0,2,1:T(8,128)(2,1)S(1)}, u32[]{:S(2)}, u32[]{:S(2)}) collective-permute-start(bf16[2,1,1,64,256]{4,3,0,2,1:T(8,128)(2,1)S(1)} %fusion.42), channel_id=1, source_target_pairs={{0,1},{1,0},{2,3},{3,2},{4,5},{5,4},{6,7},{7,6},{8,9},{9,8},{10,11... | collective-permute-start | bytes 196616 | tf_op jit(solution)/shard_map/ppermute | solution.py:17
  184.8 2.4 %collective-permute-done.2 = bf16[2,1,1,64,256]{4,3,0,2,1:T(8,128)(2,1)S(1)} collective-permute-done((bf16[2,1,1,64,256]{4,3,0,2,1:T(8,128)(2,1)S(1)}, bf16[2,1,1,64,256]{4,3,0,2,1:T(8,128)(2,1)S(1)}, u32[]{:S(2)}, u32[]{:S(2)}) %collective-permute-start.2) | collective-permute-done | bytes 65568 | tf_op jit(solution)/shard_map/ppermute | solution.py:17
  187.3 4.6 %collective-permute-start.3 = (bf16[1,2,1,64,256]{4,3,1,2,0:T(8,128)(2,1)S(1)}, bf16[1,2,1,64,256]{4,3,1,2,0:T(8,128)(2,1)S(1)}, u32[]{:S(2)}, u32[]{:S(2)}) collective-permute-start(bf16[1,2,1,64,256]{4,3,1,2,0:T(8,128)(2,1)S(1)} %fusion.41), channel_id=1, source_target_pairs={{0,2},{2,0},{1,3},{3,1},{4,6},{6,4},{5,7},{7,5},{8,10},{10,8},{9,1... | collective-permute-start | bytes 196616 | tf_op jit(solution)/shard_map/ppermute | solution.py:17
  191.9 3.8 %fusion.15 = f32[1,64,1024]{2,1,0:T(8,128)} fusion(bf16[64,1024]{1,0:T(8,128)(2,1)S(1)} %convolution_convert_fusion.6, bf16[2,1024,1024]{2,1,0:T(8,128)(2,1)} %all-gather.5.cloned.1.call-done, f32[1,64,1024]{2,1,0:T(8,128)S(1)} %copy-done.3), kind=kOutput, calls=%fused_computation.21 | convolution fusion | flops 268697600 | bytes 4849664 | tf_op jit(solution)/shard_map/brk,bkc->brc/dot_general | solution.py:55
  (49 shorter events, 8.0 us)
Async XLA Ops:
  7.2 2.8 %copy-start = (bf16[128,4096]{1,0:T(8,128)(2,1)S(1)}, bf16[128,4096]{1,0:T(8,128)(2,1)}, u32[]{:S(2)}) copy-start(bf16[128,4096]{1,0:T(8,128)(2,1)} %param.10) | copy-start | bytes 3145732
  7.2 98.3 %all-gather.5.cloned.1.call-start = ((), (), s32[]{:S(2)}) async-start(), calls=%async_computation.3 | async-start | bytes 4456448 | tf_op jit(solution)/shard_map/all_gather | solution.py:23
  13.1 77.1 %all-to-all-start = ((bf16[16,4,64,256]{3,2,1,0:T(8,128)(2,1)}), bf16[16,4,64,256]{3,2,1,0:T(8,128)(2,1)S(1)}, u32[]{:S(2)}, u32[]{:S(2)}) async-start(bf16[16,4,64,256]{3,2,1,0:T(8,128)(2,1)} %bitcast.152), calls=%async_computation | async-start | bytes 4194304 | tf_op jit(solution)/shard_map/all_to_all | solution.py:35
  24.9 125.3 %all-gather.3.cloned.1.call-start = ((), (), s32[]{:S(2)}) async-start(), calls=%async_computation.2 | async-start | bytes 2228224 | tf_op jit(solution)/shard_map/all_gather | solution.py:118
  91.2 5.5 %collective-permute-start = (bf16[2,1,1,64,256]{4,3,0,2,1:T(8,128)(2,1)S(1)}, bf16[2,1,1,64,256]{4,3,0,2,1:T(8,128)(2,1)S(1)}, u32[]{:S(2)}, u32[]{:S(2)}) collective-permute-start(bf16[2,1,1,64,256]{4,3,0,2,1:T(8,128)(2,1)S(1)} %get-tuple-element.12), channel_id=1, source_target_pairs={{0,1},{1,0},{2,3},{3,2},{4,5},{5,4},{6,7},{7,6},{8,9},{9,8},{10,11... | collective-permute-start | bytes 196616 | tf_op jit(solution)/shard_map/ppermute | solution.py:17
  96.8 6.5 %collective-permute-start.1 = (bf16[1,2,1,64,256]{4,3,1,2,0:T(8,128)(2,1)S(1)}, bf16[1,2,1,64,256]{4,3,1,2,0:T(8,128)(2,1)S(1)}, u32[]{:S(2)}, u32[]{:S(2)}) collective-permute-start(bf16[1,2,1,64,256]{4,3,1,2,0:T(8,128)(2,1)S(1)} %get-tuple-element.10), channel_id=1, source_target_pairs={{0,2},{2,0},{1,3},{3,1},{4,6},{6,4},{5,7},{7,5},{8,10},{10,8},{9,1... | collective-permute-start | bytes 196616 | tf_op jit(solution)/shard_map/ppermute | solution.py:17
  150.2 9.5 %copy-start.1 = (bf16[1,1024,1024]{2,1,0:T(8,128)(2,1)S(1)}, bf16[1,1024,1024]{2,1,0:T(8,128)(2,1)}, u32[]{:S(2)}) copy-start(bf16[1,1024,1024]{2,1,0:T(8,128)(2,1)} %all-gather.3.cloned.1.call-done) | copy-start | bytes 6291460
  155.3 24.1 %all-to-all-start.1 = ((f32[16,1,1]{2,1,0:T(1,128)}), f32[16,1,1]{2,1,0:T(1,128)S(1)}, u32[]{:S(2)}, u32[]{:S(2)}) async-start(f32[16,1,1]{2,1,0:T(1,128)} %broadcast_in_dim.22), calls=%async_computation.1 | async-start | bytes 16384 | tf_op jit(solution)/shard_map/all_to_all | solution.py:41
  167.9 3.9 %copy-start.2 = (bf16[8,8,4,256]{3,1,2,0:T(8,128)(2,1)S(1)}, bf16[8,8,4,256]{3,1,2,0:T(8,128)(2,1)}, u32[]{:S(2)}) copy-start(bf16[8,8,4,256]{3,1,2,0:T(8,128)(2,1)} %copy.70) | copy-start | bytes 393220
  179.4 12.5 %copy-start.3 = (f32[1,64,1024]{2,1,0:T(8,128)S(1)}, f32[1,64,1024]{2,1,0:T(8,128)}, u32[]{:S(2)}) copy-start(f32[1,64,1024]{2,1,0:T(8,128)} %param.14) | copy-start | bytes 786436
  181.7 5.6 %collective-permute-start.2 = (bf16[2,1,1,64,256]{4,3,0,2,1:T(8,128)(2,1)S(1)}, bf16[2,1,1,64,256]{4,3,0,2,1:T(8,128)(2,1)S(1)}, u32[]{:S(2)}, u32[]{:S(2)}) collective-permute-start(bf16[2,1,1,64,256]{4,3,0,2,1:T(8,128)(2,1)S(1)} %fusion.42), channel_id=1, source_target_pairs={{0,1},{1,0},{2,3},{3,2},{4,5},{5,4},{6,7},{7,6},{8,9},{9,8},{10,11... | collective-permute-start | bytes 196616 | tf_op jit(solution)/shard_map/ppermute | solution.py:17
  187.3 8.4 %collective-permute-start.3 = (bf16[1,2,1,64,256]{4,3,1,2,0:T(8,128)(2,1)S(1)}, bf16[1,2,1,64,256]{4,3,1,2,0:T(8,128)(2,1)S(1)}, u32[]{:S(2)}, u32[]{:S(2)}) collective-permute-start(bf16[1,2,1,64,256]{4,3,1,2,0:T(8,128)(2,1)S(1)} %fusion.41), channel_id=1, source_target_pairs={{0,2},{2,0},{1,3},{3,1},{4,6},{6,4},{5,7},{7,5},{8,10},{10,8},{9,1... | collective-permute-start | bytes 196616 | tf_op jit(solution)/shard_map/ppermute | solution.py:17
Sparse Core Ops, SparseCore 0:
  10.7 85.3 all-gather.4
  104.8 45.3 all-gather.2
where the time goes:
time: 205 us; the launch traced here: 204 us
  waiting for transfers between devices  117 us (57%)
  starting transfers between devices  31.8 us (16%)
  matrix products  28.9 us (14%)
  between operations  15.1 us (7%)
  local copies, waits for them, and re-layouts  6.68 us (3%)
  other arithmetic  4.93 us (2%)
    all_to_all x1, waiting for transfers between devices, sent_and_summed(): parts = lax.all_to_all(split_up(value, dim, length), axis, 0, 0, tiled=True)  65.2 us
    all_gather x1, waiting for transfers between devices, on_device(): lax.all_gather(own_rows, 'tok', axis=1, tiled=True)  44.8 us
    dot_general x6, matrix products, newton_rows(): jnp.einsum('brk,bkc->brc', product, root_full, preferred_element_type=jnp...  18.7 us
    ppermute x4, starting transfers between devices, partner(): return lax.ppermute(block, axis, route)  15.5 us
    all_to_all x1, starting transfers between devices, sent_and_summed(): parts = lax.all_to_all(split_up(value, dim, length), axis, 0, 0, tiled=True)  11.8 us
    ppermute x4, waiting for transfers between devices, partner(): return lax.ppermute(block, axis, route)  6.65 us
    all_to_all x1, starting transfers between devices, sent_to_all(): return lax.all_to_all(copies, axis, split_axis=0, concat_axis=0, tiled=True)  4.42 us
  transfers between devices with their start and end apart: 8, of which 5 were waited for; matrix products, arithmetic and copies ran while one was open for 15% of the time, Pallas kernels for 0%

commit v1 on v0

v1 whole, which is shorter than its diff:
```python
import functools

import jax
import jax.numpy as jnp
from jax import lax
from jax.experimental import pallas as pl
from jax.experimental.pallas import tpu as pltpu
from jax.sharding import Mesh
from jax.sharding import PartitionSpec as P

BETA = 0.95
EPS = 1e-06
F32 = jnp.float32
BF16 = jnp.bfloat16
NZ, NC, NY, NX = 8, 2, 8, 4
BS = 1024
HALF = BS // NC
ROWS = BS // (NZ * NC)
WIDTH = BS // NX
TOK = ("z", "core")
HID = ("y", "x")
SWAP = [(0, 1), (1, 0)]
VMEM = pl.BlockSpec(memory_space=pltpu.VMEM)
SMEM = pl.BlockSpec(memory_space=pltpu.SMEM)
PARAMS = pltpu.CompilerParams(vmem_limit_bytes=48 * 1024 * 1024)


def dot(a, b, dims=((1,), (0,))):
    return lax.dot_general(a, b, (dims, ((), ())), preferred_element_type=F32)


def call(body, outs, specs, scratch=(), flops=0, moved=0):
    return pl.pallas_call(
        body,
        out_shape=outs,
        in_specs=specs,
        out_specs=jax.tree.map(lambda _: VMEM, outs),
        scratch_shapes=list(scratch),
        compiler_params=PARAMS,
        cost_estimate=pl.CostEstimate(flops=flops, bytes_accessed=moved, transcendentals=0),
    )


def partial_kernel(where, act, cot, more_act, more_cot, out):
    core = where[1]
    for r in range(NX):
        own = act[:, pl.ds(pl.multiple_of(r * BS + core * HALF, 128), HALF)]
        total = dot(own, cot[...], ((0,), (0,)))
        total += dot(more_act[:, r * HALF : (r + 1) * HALF], more_cot[...], ((0,), (0,)))
        out[r] = total.astype(BF16).reshape(NZ, ROWS, WIDTH)


def sum_kernel(parts, out):
    for x in range(NX):
        total = parts[x, 0].astype(F32)
        for z in range(1, NZ):
            total += parts[x, z].astype(F32)
        low = total.astype(BF16)
        for z in range(NZ):
            out[z, :, x * WIDTH : (x + 1) * WIDTH] = low


def precond_kernel(where, mine, other, left_root, right_low, out, squares):
    core = where[1]
    low = left_root[...].astype(BF16)
    first, second = low[:, :HALF], low[:, HALF:]
    own = jnp.where(core == 0, first.astype(F32), second.astype(F32)).astype(BF16)
    far = jnp.where(core == 0, second.astype(F32), first.astype(F32)).astype(BF16)
    applied = dot(own, mine[...]) + dot(far, other[...])
    precond = dot(applied.astype(BF16), right_low[...])
    for x in range(NX):
        out[x] = precond[:, x * WIDTH : (x + 1) * WIDTH].astype(BF16)
    squares[...] = jnp.full(squares.shape, jnp.sum(precond * precond), F32)


def factor_kernel(
    where, mine, other, left_gram, right_gram, left_root, right_root, left_power, right_power,
    left_next, right_next, left_refined, right_refined, whole, columns,
):
    z, core = where[0], where[1]
    whole[pl.ds(pl.multiple_of(core * HALF, HALF), HALF)] = mine[...]
    whole[pl.ds(pl.multiple_of((1 - core) * HALF, HALF), HALF)] = other[...]
    rows = whole[pl.ds(pl.multiple_of((z * NC + core) * ROWS, ROWS), ROWS)]
    left = BETA * left_gram[...] + dot(rows, whole[...], ((1,), (1,)))
    left_next[...] = left
    slab = whole[:, pl.ds(pl.multiple_of(z * NC * ROWS, 128), NC * ROWS)]
    columns[...] = slab.astype(F32).T
    turned = columns[pl.ds(pl.multiple_of(core * ROWS, ROWS), ROWS)].astype(BF16)
    right = BETA * right_gram[...] + dot(turned, whole[...])
    right_next[...] = right
    left_refined[...] = (5.0 * left_root[...] - dot(left.astype(BF16), left_power[...])) / 4.0
    right_refined[...] = (5.0 * right_root[...] - dot(right.astype(BF16), right_power[...])) / 4.0


def update_kernel(arrived, squares, out):
    for x in range(NX):
        total = jnp.sum(squares[x * NZ * NC : (x + 1) * NZ * NC], axis=0)
        scale = 1.0 / jnp.sqrt(total / (BS * BS) + EPS)
        for part in range(WIDTH // 128):
            cols = slice(part * 128, (part + 1) * 128)
            out[x, :, cols] = arrived[x, :, cols].astype(F32) * scale


def on_device(activations, cotangent, left_gram, right_gram, left_root, right_root):
    left_gram, right_gram = left_gram[0], right_gram[0]
    left_root, right_root = left_root[0], right_root[0]
    z, core = lax.axis_index("z"), lax.axis_index("core")
    where = jnp.stack([z, core]).astype(jnp.int32)
    even = core == 0

    left_low, right_low = left_root.astype(BF16), right_root.astype(BF16)
    sent = jnp.where(even, right_low, left_low)
    kept = jnp.where(even, left_low, right_low)
    got = lax.ppermute(sent, "core", SWAP)
    shard = jnp.concatenate([jnp.where(even, kept, got), jnp.where(even, got, kept)], axis=0)
    root = lax.all_gather(shard, "z", axis=0, tiled=True)

    halves = [
        (activations[:, r * BS : r * BS + HALF], activations[:, r * BS + HALF : (r + 1) * BS])
        for r in range(NX)
    ]
    lent = jnp.concatenate([jnp.where(even, b, a) for a, b in halves], axis=1)
    more_act = lax.ppermute(lent, "core", SWAP)
    more_cot = lax.ppermute(cotangent, "core", SWAP)
    partial = call(
        partial_kernel, jax.ShapeDtypeStruct((NX, NZ, ROWS, WIDTH), BF16),
        [SMEM, VMEM, VMEM, VMEM, VMEM], flops=2 * 256 * 2048 * 256, moved=3_000_000,
    )(where, activations, cotangent, more_act, more_cot)
    parts = lax.all_to_all(
        partial.reshape(NX * NZ, ROWS, WIDTH), ("x", "z"), 0, 0, tiled=True
    ).reshape(NX, NZ, ROWS, WIDTH)
    copies = call(
        sum_kernel, jax.ShapeDtypeStruct((NZ, ROWS, BS), BF16), [VMEM], flops=1_000_000, moved=2_000_000
    )(parts)
    mine = lax.all_to_all(copies, "z", 0, 0, tiled=True).reshape(HALF, BS)
    other = lax.ppermute(mine, "core", SWAP)

    squared = dot(root, root).astype(BF16)
    fourth = dot(squared, squared).astype(BF16)
    fifth = dot(fourth, root).astype(BF16)
    far_root = lax.ppermute(root, "core", SWAP)
    far_fifth = lax.ppermute(fifth, "core", SWAP)
    right_whole = jnp.where(even, far_root, root)
    left_power = jnp.where(even, fifth, far_fifth)
    right_power = jnp.where(even, far_fifth, fifth)

    precond, squares = call(
        precond_kernel,
        (
            jax.ShapeDtypeStruct((NX, ROWS, WIDTH), BF16),
            jax.ShapeDtypeStruct((NX * NZ * NC, 1, 128), F32),
        ),
        [SMEM] + [VMEM] * 4, flops=4 * 64 * 1024 * 1024, moved=5_000_000,
    )(where, mine, other, left_root, right_whole)
    arrived = lax.all_to_all(precond, "x", 0, 0, tiled=True)
    sums = lax.all_to_all(squares, ("x", "z", "core"), 0, 0, tiled=True)
    shape = jax.ShapeDtypeStruct((ROWS, BS), F32)
    outs = call(
        factor_kernel, (shape,) * 4, [SMEM] + [VMEM] * 8,
        scratch=[pltpu.VMEM((BS, BS), BF16), pltpu.VMEM((NC * ROWS, BS), F32)],
        flops=8 * 64 * 1024 * 1024, moved=8_000_000,
    )(where, mine, other, left_gram, right_gram, left_root, right_root, left_power, right_power)
    update = call(
        update_kernel, jax.ShapeDtypeStruct((NX, ROWS, WIDTH), F32), [VMEM, VMEM],
        flops=100_000, moved=500_000,
    )(arrived, sums)
    return (*(o[None] for o in outs), update)


def solution(mesh):
    split = Mesh(mesh.devices.reshape(NZ, NC, NY, NX), (*TOK, *HID))
    factor = P(HID, TOK, None)
    return jax.shard_map(
        on_device,
        mesh=split,
        in_specs=(P(TOK, None), P(TOK, HID), factor, factor, factor, factor),
        out_specs=(factor, factor, factor, factor, P(None, TOK, HID)),
        check_vma=False,
    )
```

time: 205 us -> 148 us (0.72)
  waiting for transfers between devices: 117 us -> 9.13 us
  blocking collectives: 0 us -> 59.1 us
  matrix products: 28.9 us -> 14 us
  Pallas kernels: 0 us -> 9.64 us
  local copies, waits for them, and re-layouts: 6.68 us -> 0.04 us
  other arithmetic: 4.93 us -> 8.85 us
    all_to_all x2, waiting for transfers between devices: 65.2 us -> 2.62 us  [the longest x1 2.61 us: on_device(): mine = lax.all_to_all(copies, 'z', 0, 0, tiled=True).reshape(HALF, BS)]
    all_to_all x0 -> x2, blocking collectives: none -> 59.1 us  [the longest x1 43.1 us: on_device(): lax.all_to_all(partial.reshape(NX * NZ, ROWS, WIDTH), ('x', 'z'), 0, 0, t...]
    all_gather x2 -> x1, waiting for transfers between devices: 44.8 us -> 4.09 us  [on_device(): root = lax.all_gather(shard, 'z', axis=0, tiled=True)]
    dot_general x10 -> x2, matrix products: 28.9 us -> 14 us  [dot(): return lax.dot_general(a, b, (dims, ((), ())), preferred_element_type=F32)]
    pallas_call x0 -> x5, Pallas kernels: none -> 9.64 us  [the longest x1 4.32 us: on_device(): call(factor_kernel, (shape,) * 4, [SMEM] + [VMEM] * 8, scratch=[pltpu.VME...]
    ppermute x4 -> x6, starting transfers between devices: 15.5 us -> 23.5 us  [the longest x1 8.79 us: on_device(): got = lax.ppermute(sent, 'core', SWAP)]
    select_n x3 -> x6, other arithmetic: 0.18 us -> 8 us  [the longest x1 3.9 us: on_device(): right_power = jnp.where(even, far_fifth, fifth)]
    all_to_all x2, starting transfers between devices: 16.3 us -> 9.34 us  [the longest x1 6.01 us: on_device(): mine = lax.all_to_all(copies, 'z', 0, 0, tiled=True).reshape(HALF, BS)]
  transfers between devices with their start and end apart: 8 -> 9, of which waited for: 5 -> 5; matrix products, arithmetic and copies ran while one was open for 15% -> 13% of each run, Pallas kernels for 0% -> 6%
where the time goes in v1:
time: 148 us
  blocking collectives  59.1 us (40%)
  starting transfers between devices  32.9 us (22%)
  between operations  14.2 us (10%)
  matrix products  14 us (9%)
  Pallas kernels  9.64 us (7%)
  waiting for transfers between devices  9.13 us (6%)
  other arithmetic  8.85 us (6%)
    all_to_all x1, blocking collectives, on_device(): lax.all_to_all(partial.reshape(NX * NZ, ROWS, WIDTH), ('x', 'z'), 0, 0, t...  43.1 us
    all_to_all x1, blocking collectives, on_device(): sums = lax.all_to_all(squares, ('x', 'z', 'core'), 0, 0, tiled=True)  15.9 us
    dot_general x2, matrix products, dot(): return lax.dot_general(a, b, (dims, ((), ())), preferred_element_type=F32)  14 us
    ppermute x1, starting transfers between devices, on_device(): got = lax.ppermute(sent, 'core', SWAP)  8.79 us
    all_to_all x1, starting transfers between devices, on_device(): mine = lax.all_to_all(copies, 'z', 0, 0, tiled=True).reshape(HALF, BS)  6.01 us
    ppermute x1, starting transfers between devices, on_device(): far_root = lax.ppermute(root, 'core', SWAP)  5.06 us
    pallas_call x1, Pallas kernels, on_device(): call(factor_kernel, (shape,) * 4, [SMEM] + [VMEM] * 8, scratch=[pltpu.VME...  4.32 us
    all_gather x1, waiting for transfers between devices, on_device(): root = lax.all_gather(shard, 'z', axis=0, tiled=True)  4.09 us
  transfers between devices with their start and end apart: 9, of which 5 were waited for; matrix products, arithmetic and copies ran while one was open for 13% of the time, Pallas kernels for 6%

profile of v1, /device:TPU:1, one launch (start us, length us, event | category | flops | bytes accessed | tf_op | source)
XLA Modules:
  0.0 147.8 jit_solution(1948412435412303451)
XLA Ops:
  7.2 1.1 broadcast_select_fusion.5
  8.4 8.8 %collective-permute-start.3 = (bf16[64,1024]{1,0:T(8,128)(2,1)S(1)}, bf16[64,1024]{1,0:T(8,128)(2,1)S(1)}, u32[]{:S(2)}, u32[]{:S(2)}) collective-permute-start(bf16[64,1024]{1,0:T(8,128)(2,1)S(1)} %broadcast_select_fusion.5), channel_id=1, source_target_pairs={{0,32},{32,0},{1,33},{33,1},{2,34},{34,2},{3,35},{35,3},{4,36},{36... | collective-permute-start | bytes 393224 | tf_op jit(solution)/shard_map/ppermute | solution.py:114
  17.2 1.0 collective-permute-done.3
  18.1 1.1 broadcast_select_fusion.4
  20.1 2.3 %collective-permute-start = (bf16[128,2048]{1,0:T(8,128)(2,1)S(1)}, bf16[128,2048]{1,0:T(8,128)(2,1)S(1)}, u32[]{:S(2)}, u32[]{:S(2)}) collective-permute-start(bf16[128,2048]{1,0:T(8,128)(2,1)S(1)} %pad_maximum_fusion), channel_id=1, source_target_pairs={{0,32},{32,0},{1,33},{33,1},{2,34},{34,2},{3,35},{35,3},{4,36},{36... | collective-permute-start | bytes 1572872 | tf_op jit(solution)/shard_map/ppermute | solution.py:123
  22.4 2.1 %collective-permute-start.1 = (bf16[128,256]{1,0:T(8,128)(2,1)S(1)}, bf16[128,256]{1,0:T(8,128)(2,1)S(1)}, u32[]{:S(2)}, u32[]{:S(2)}) collective-permute-start(bf16[128,256]{1,0:T(8,128)(2,1)S(1)} %copy-done.5), channel_id=1, source_target_pairs={{0,32},{32,0},{1,33},{33,1},{2,34},{34,2},{3,35},{35,3},{4,36},{36... | collective-permute-start | bytes 196616 | tf_op jit(solution)/shard_map/ppermute | solution.py:124
  24.5 1.0 collective-permute-done.1.more_cot
  25.6 1.3 shard_map.101
  26.8 43.1 %all_to_all.20 = bf16[32,64,256]{2,1,0:T(8,128)(2,1)S(1)} all-to-all(bf16[32,64,256]{2,1,0:T(8,128)(2,1)S(1)} %bitcast.27), channel_id=1, replica_groups=mesh['z'=8,'core'=2,'y'=8,'x'=4] {'x','z'}, dimensions={0} | all-to-all | bytes 2097152 | tf_op jit(solution)/shard_map/all_to_all | solution.py:129
  70.0 1.2 shard_map.102
  71.2 6.0 %all-to-all-start.1 = ((bf16[8,64,1024]{2,1,0:T(8,128)(2,1)}), bf16[8,64,1024]{2,1,0:T(8,128)(2,1)S(1)}, u32[]{:S(2)}, u32[]{:S(2)}) async-start(bf16[8,64,1024]{2,1,0:T(8,128)(2,1)} %shard_map.102), calls=%async_computation.1 | async-start | bytes 2097152 | tf_op jit(solution)/shard_map/all_to_all | solution.py:135
  77.2 4.1 %all-gather.2.cloned.1.call-done = bf16[1024,1024]{1,0:T(8,128)(2,1)} async-done(((bf16[128,1024]{1,0:T(8,128)(2,1)}), bf16[1024,1024]{1,0:T(8,128)(2,1)}) %all-gather.2.cloned.1.call-update) | async-done | bytes 2097168 | tf_op jit(solution)/shard_map/all_gather | solution.py:116
  81.3 5.1 %collective-permute-start.5 = (bf16[1024,1024]{1,0:T(8,128)(2,1)}, bf16[1024,1024]{1,0:T(8,128)(2,1)}, u32[]{:S(2)}, u32[]{:S(2)}) collective-permute-start(bf16[1024,1024]{1,0:T(8,128)(2,1)} %all-gather.2.cloned.1.call-done), channel_id=1, source_target_pairs={{0,32},{32,0},{1,33},{33,1},{2,34},{34,2},{3,35},{35,3},{4,36},{36... | collective-permute-start | bytes 6291464 | tf_op jit(solution)/shard_map/ppermute | solution.py:141
  86.4 5.9 %fusion.11 = bf16[1024,1024]{1,0:T(8,128)(2,1)} fusion(bf16[1024,1024]{1,0:T(8,128)(2,1)} %all-gather.2.cloned.1.call-done), kind=kOutput, calls=%fused_computation.19 | convolution fusion | flops 2147483648 | bytes 4194304 | tf_op jit(solution)/shard_map/dot_general | solution.py:29
  92.3 8.1 %fusion.4 = bf16[1024,1024]{1,0:T(8,128)(2,1)} fusion(bf16[1024,1024]{1,0:T(8,128)(2,1)S(1)} %copy-done.6, bf16[1024,1024]{1,0:T(8,128)(2,1)} %fusion.11), kind=kOutput, calls=%fused_computation.7 | convolution fusion | flops 4297064448 | bytes 6291456 | tf_op jit(solution)/shard_map/dot_general | solution.py:29
  100.4 1.9 %collective-permute-start.4 = (bf16[1024,1024]{1,0:T(8,128)(2,1)}, bf16[1024,1024]{1,0:T(8,128)(2,1)}, u32[]{:S(2)}, u32[]{:S(2)}) collective-permute-start(bf16[1024,1024]{1,0:T(8,128)(2,1)} %fusion.4), channel_id=1, source_target_pairs={{0,32},{32,0},{1,33},{33,1},{2,34},{34,2},{3,35},{35,3},{4,36},{36... | collective-permute-start | bytes 6291464 | tf_op jit(solution)/shard_map/ppermute | solution.py:142
  102.3 2.6 %all-to-all-done.1 = bf16[8,64,1024]{2,1,0:T(8,128)(2,1)S(1)} async-done(((bf16[8,64,1024]{2,1,0:T(8,128)(2,1)}), bf16[8,64,1024]{2,1,0:T(8,128)(2,1)S(1)}, u32[]{:S(2)}, u32[]{:S(2)}) %all-to-all-start.1) | async-done | bytes 1048608 | tf_op jit(solution)/shard_map/all_to_all | solution.py:135
  104.9 3.4 %collective-permute-start.2 = (bf16[512,1024]{1,0:T(8,128)(2,1)S(1)}, bf16[512,1024]{1,0:T(8,128)(2,1)S(1)}, u32[]{:S(2)}, u32[]{:S(2)}) collective-permute-start(bf16[512,1024]{1,0:T(8,128)(2,1)S(1)} %bitcast.24), channel_id=1, source_target_pairs={{0,32},{32,0},{1,33},{33,1},{2,34},{34,2},{3,35},{35,3},{4,36},{36... | collective-permute-start | bytes 3145736 | tf_op jit(solution)/shard_map/ppermute | solution.py:136
  108.4 1.8 %broadcast_select_fusion.right_low = bf16[1024,1024]{1,0:T(8,128)(2,1)S(1)} fusion(bf16[1024,1024]{1,0:T(8,128)(2,1)} %collective-permute-done.5, bf16[1024,1024]{1,0:T(8,128)(2,1)} %all-gather.2.cloned.1.call-done, pred[]{:T(512)S(6)} %eq.3), kind=kLoop, calls=%fused_computation.4 | loop fusion | flops 1048576 | bytes 6291457 | tf_op jit(solution)/shard_map/jit(_where)/select_n | solution.py:143
  110.6 2.1 %shard_map.104 = (bf16[4,64,256]{2,1,0:T(8,128)(2,1)}, f32[64,1,128]{2,1,0:T(1,128)S(1)}) custom-call(s32[2]{0:T(128)S(1)} %pad_add_fusion.where, bf16[512,1024]{1,0:T(8,128)(2,1)S(1)} %bitcast.25, bf16[512,1024]{1,0:T(8,128)(2,1)S(1)} %collective-permute-done.2.other, f32[64,1024]{1,0:T(8,128)S(1)} %bitcast.29, ...), custom_call_target="tpu_custom_call" | custom-call | flops 268435456 | bytes 5000000 | tf_op jit(solution)/shard_map/pallas_call | solution.py:147
  112.7 15.9 %all_to_all.21.squares = f32[64,1,128]{2,1,0:T(1,128)S(1)} all-to-all(f32[64,1,128]{2,1,0:T(1,128)S(1)} %get-tuple-element.16), channel_id=1, replica_groups=mesh['z'=8,'core'=2,'y'=8,'x'=4] {'x','z','core'}, dimensions={0} | all-to-all | bytes 65536 | tf_op jit(solution)/shard_map/all_to_all | solution.py:156
  128.6 3.3 %all-to-all-start.2 = ((bf16[4,64,256]{2,1,0:T(8,128)(2,1)}), bf16[4,64,256]{2,1,0:T(8,128)(2,1)S(1)}, u32[]{:S(2)}, u32[]{:S(2)}) async-start(bf16[4,64,256]{2,1,0:T(8,128)(2,1)} %get-tuple-element.15), calls=%async_computation.2 | async-start | bytes 262144 | tf_op jit(solution)/shard_map/all_to_all | solution.py:155
  132.0 3.9 %broadcast_select_fusion.1 = (bf16[1024,1024]{1,0:T(8,128)(2,1)}, bf16[1024,1024]{1,0:T(8,128)(2,1)S(1)}) fusion(bf16[1024,1024]{1,0:T(8,128)(2,1)} %collective-permute-done.4, bf16[1024,1024]{1,0:T(8,128)(2,1)} %fusion.4, pred[]{:T(512)S(6)} %eq.3), kind=kLoop, calls=%fused_computation.5 | loop fusion | flops 2097152 | bytes 8388609 | tf_op jit(solution)/shard_map/jit(_where)/select_n | solution.py:145
  135.9 4.3 %shard_map.103 = (f32[64,1024]{1,0:T(8,128)}, f32[64,1024]{1,0:T(8,128)}, f32[64,1024]{1,0:T(8,128)}, f32[64,1024]{1,0:T(8,128)}) custom-call(s32[2]{0:T(128)S(1)} %pad_add_fusion.where, bf16[512,1024]{1,0:T(8,128)(2,1)S(1)} %bitcast.26, bf16[512,1024]{1,0:T(8,128)(2,1)S(1)} %collective-permute-done.2.other, f32[64,1024]{1,0:T(8,128)S(1)} %bitcast.32, ...), custom_call_target="tpu_custom_call" | custom-call | flops 536870912 | bytes 8000000 | tf_op jit(solution)/shard_map/pallas_call | solution.py:158
  (27 shorter events, 2.2 us)
Async XLA Ops:
  7.2 12.8 %copy-start = (bf16[128,4096]{1,0:T(8,128)(2,1)S(1)}, bf16[128,4096]{1,0:T(8,128)(2,1)}, u32[]{:S(2)}) copy-start(bf16[128,4096]{1,0:T(8,128)(2,1)} %act.1) | copy-start | bytes 3145732
  7.2 74.1 %all-gather.2.cloned.1.call-start = ((), (), s32[]{:S(2)}) async-start(), calls=%async_computation.4 | async-start | bytes 2359296 | tf_op jit(solution)/shard_map/all_gather | solution.py:116
  8.4 9.8 %collective-permute-start.3 = (bf16[64,1024]{1,0:T(8,128)(2,1)S(1)}, bf16[64,1024]{1,0:T(8,128)(2,1)S(1)}, u32[]{:S(2)}, u32[]{:S(2)}) collective-permute-start(bf16[64,1024]{1,0:T(8,128)(2,1)S(1)} %broadcast_select_fusion.5), channel_id=1, source_target_pairs={{0,32},{32,0},{1,33},{33,1},{2,34},{34,2},{3,35},{35,3},{4,36},{36... | collective-permute-start | bytes 393224 | tf_op jit(solution)/shard_map/ppermute | solution.py:114
  19.2 3.2 %copy-start.5 = (bf16[128,256]{1,0:T(8,128)(2,1)S(1)}, bf16[128,256]{1,0:T(8,128)(2,1)}, u32[]{:S(2)}) copy-start(bf16[128,256]{1,0:T(8,128)(2,1)} %cot.1) | copy-start | bytes 196612
  20.1 5.4 %collective-permute-start = (bf16[128,2048]{1,0:T(8,128)(2,1)S(1)}, bf16[128,2048]{1,0:T(8,128)(2,1)S(1)}, u32[]{:S(2)}, u32[]{:S(2)}) collective-permute-start(bf16[128,2048]{1,0:T(8,128)(2,1)S(1)} %pad_maximum_fusion), channel_id=1, source_target_pairs={{0,32},{32,0},{1,33},{33,1},{2,34},{34,2},{3,35},{35,3},{4,36},{36... | collective-permute-start | bytes 1572872 | tf_op jit(solution)/shard_map/ppermute | solution.py:123
  22.4 3.1 %collective-permute-start.1 = (bf16[128,256]{1,0:T(8,128)(2,1)S(1)}, bf16[128,256]{1,0:T(8,128)(2,1)S(1)}, u32[]{:S(2)}, u32[]{:S(2)}) collective-permute-start(bf16[128,256]{1,0:T(8,128)(2,1)S(1)} %copy-done.5), channel_id=1, source_target_pairs={{0,32},{32,0},{1,33},{33,1},{2,34},{34,2},{3,35},{35,3},{4,36},{36... | collective-permute-start | bytes 196616 | tf_op jit(solution)/shard_map/ppermute | solution.py:124
  71.2 33.7 %all-to-all-start.1 = ((bf16[8,64,1024]{2,1,0:T(8,128)(2,1)}), bf16[8,64,1024]{2,1,0:T(8,128)(2,1)S(1)}, u32[]{:S(2)}, u32[]{:S(2)}) async-start(bf16[8,64,1024]{2,1,0:T(8,128)(2,1)} %shard_map.102), calls=%async_computation.1 | async-start | bytes 2097152 | tf_op jit(solution)/shard_map/all_to_all | solution.py:135
  81.3 11.0 %copy-start.6 = (bf16[1024,1024]{1,0:T(8,128)(2,1)S(1)}, bf16[1024,1024]{1,0:T(8,128)(2,1)}, u32[]{:S(2)}) copy-start(bf16[1024,1024]{1,0:T(8,128)(2,1)} %all-gather.2.cloned.1.call-done) | copy-start | bytes 6291460
  81.3 27.0 %collective-permute-start.5 = (bf16[1024,1024]{1,0:T(8,128)(2,1)}, bf16[1024,1024]{1,0:T(8,128)(2,1)}, u32[]{:S(2)}, u32[]{:S(2)}) collective-permute-start(bf16[1024,1024]{1,0:T(8,128)(2,1)} %all-gather.2.cloned.1.call-done), channel_id=1, source_target_pairs={{0,32},{32,0},{1,33},{33,1},{2,34},{34,2},{3,35},{35,3},{4,36},{36... | collective-permute-start | bytes 6291464 | tf_op jit(solution)/shard_map/ppermute | solution.py:141
  100.4 31.6 %collective-permute-start.4 = (bf16[1024,1024]{1,0:T(8,128)(2,1)}, bf16[1024,1024]{1,0:T(8,128)(2,1)}, u32[]{:S(2)}, u32[]{:S(2)}) collective-permute-start(bf16[1024,1024]{1,0:T(8,128)(2,1)} %fusion.4), channel_id=1, source_target_pairs={{0,32},{32,0},{1,33},{33,1},{2,34},{34,2},{3,35},{35,3},{4,36},{36... | collective-permute-start | bytes 6291464 | tf_op jit(solution)/shard_map/ppermute | solution.py:142
  104.9 5.7 %copy-start.1 = (f32[1,64,1024]{2,1,0:T(8,128)S(1)}, f32[1,64,1024]{2,1,0:T(8,128)}, u32[]{:S(2)}) copy-start(f32[1,64,1024]{2,1,0:T(8,128)} %param.10) | copy-start | bytes 786436
  104.9 5.7 %collective-permute-start.2 = (bf16[512,1024]{1,0:T(8,128)(2,1)S(1)}, bf16[512,1024]{1,0:T(8,128)(2,1)S(1)}, u32[]{:S(2)}, u32[]{:S(2)}) collective-permute-start(bf16[512,1024]{1,0:T(8,128)(2,1)S(1)} %bitcast.24), channel_id=1, source_target_pairs={{0,32},{32,0},{1,33},{33,1},{2,34},{34,2},{3,35},{35,3},{4,36},{36... | collective-permute-start | bytes 3145736 | tf_op jit(solution)/shard_map/ppermute | solution.py:136
  128.6 11.6 %all-to-all-start.2 = ((bf16[4,64,256]{2,1,0:T(8,128)(2,1)}), bf16[4,64,256]{2,1,0:T(8,128)(2,1)S(1)}, u32[]{:S(2)}, u32[]{:S(2)}) async-start(bf16[4,64,256]{2,1,0:T(8,128)(2,1)} %get-tuple-element.15), calls=%async_computation.2 | async-start | bytes 262144 | tf_op jit(solution)/shard_map/all_to_all | solution.py:155
  131.9 3.9 %copy-start.2 = (f32[1,64,1024]{2,1,0:T(8,128)S(1)}, f32[1,64,1024]{2,1,0:T(8,128)}, u32[]{:S(2)}) copy-start(f32[1,64,1024]{2,1,0:T(8,128)} %param.11) | copy-start | bytes 786436
  132.0 3.9 %copy-start.3 = (f32[1,64,1024]{2,1,0:T(8,128)S(1)}, f32[1,64,1024]{2,1,0:T(8,128)}, u32[]{:S(2)}) copy-start(f32[1,64,1024]{2,1,0:T(8,128)} %param.8) | copy-start | bytes 786436
  132.0 3.9 %copy-start.4 = (f32[1,64,1024]{2,1,0:T(8,128)S(1)}, f32[1,64,1024]{2,1,0:T(8,128)}, u32[]{:S(2)}) copy-start(f32[1,64,1024]{2,1,0:T(8,128)} %param.9) | copy-start | bytes 786436
Sparse Core Ops, SparseCore 0:
  20.1 61.1 all-gather.1

commit v2 on v1

v2 whole, which is shorter than its diff:
```python
import functools

import jax
import jax.numpy as jnp
from jax import lax
from jax.experimental import pallas as pl
from jax.experimental.pallas import tpu as pltpu
from jax.sharding import Mesh
from jax.sharding import PartitionSpec as P

BETA = 0.95
EPS = 1e-06
F32 = jnp.float32
BF16 = jnp.bfloat16
NZ, NC, NY, NX = 8, 2, 8, 4
BS = 1024
HALF = BS // NC
TOKENS = 128
ROWS = BS // (NZ * NC)
WIDTH = BS // NX
COT = NX * HALF
ROOT = COT + WIDTH
TILE = 256
TOK = ("z", "core")
HID = ("y", "x")
SWAP = [(0, 1), (1, 0)]
VMEM = pl.BlockSpec(memory_space=pltpu.VMEM)
SMEM = pl.BlockSpec(memory_space=pltpu.SMEM)
PARAMS = pltpu.CompilerParams(vmem_limit_bytes=48 * 1024 * 1024)


def dot(a, b, dims=((1,), (0,))):
    return lax.dot_general(a, b, (dims, ((), ())), preferred_element_type=F32)


def call(body, outs, specs, scratch=(), flops=0, moved=0):
    return pl.pallas_call(
        body,
        out_shape=outs,
        in_specs=specs,
        out_specs=jax.tree.map(lambda _: VMEM, outs),
        scratch_shapes=list(scratch),
        compiler_params=PARAMS,
        cost_estimate=pl.CostEstimate(flops=flops, bytes_accessed=moved, transcendentals=0),
    )


def pack_kernel(where, act, cot, left_root, right_root, out):
    core = where[1]
    for r in range(NX):
        far = act[:, pl.ds(pl.multiple_of(r * BS + (1 - core) * HALF, 128), HALF)]
        out[:, r * HALF : (r + 1) * HALF] = far
    out[:, COT : COT + WIDTH] = cot[...]
    lent = jnp.where(core == 0, right_root[...], left_root[...]).astype(BF16)
    out[:ROWS, ROOT:] = lent[:, :HALF]
    out[ROWS:, ROOT:] = lent[:, HALF:]


def partial_kernel(where, act, cot, left_root, right_root, more, out, shard):
    core = where[1]
    kept = jnp.where(core == 0, left_root[...], right_root[...]).astype(BF16)
    shard[pl.ds(pl.multiple_of(core * ROWS, ROWS), ROWS)] = kept
    far = pl.ds(pl.multiple_of((1 - core) * ROWS, ROWS), ROWS)
    shard[far, :HALF] = more[:ROWS, ROOT:]
    shard[far, HALF:] = more[ROWS:, ROOT:]
    more_cot = more[:, COT : COT + WIDTH]
    for r in range(NX):
        own = act[:, pl.ds(pl.multiple_of(r * BS + core * HALF, 128), HALF)]
        total = dot(own, cot[...], ((0,), (0,)))
        total += dot(more[:, r * HALF : (r + 1) * HALF], more_cot, ((0,), (0,)))
        out[r] = total.astype(BF16).reshape(NZ, ROWS, WIDTH)


def sum_kernel(parts, out):
    for x in range(NX):
        total = parts[x, 0].astype(F32)
        for z in range(1, NZ):
            total += parts[x, z].astype(F32)
        low = total.astype(BF16)
        for z in range(NZ):
            out[z, :, x * WIDTH : (x + 1) * WIDTH] = low


def power_kernel(root, fifth, squared, fourth):
    def times(a, b, out):
        def tile(i, carry):
            rows = pl.ds(pl.multiple_of(i * TILE, TILE), TILE)
            out[rows] = dot(a[rows], b[...]).astype(BF16)
            return carry

        lax.fori_loop(0, BS // TILE, tile, 0)

    times(root, root, squared)
    times(squared, squared, fourth)
    times(fourth, root, fifth)


def precond_kernel(where, mine, other, root, far_root, out, kept):
    z, core = where[0], where[1]
    place = (z * NC + core) * ROWS

    def run(left, right, upper, lower):
        def tile(i, total):
            rows = pl.ds(pl.multiple_of(i * TILE, TILE), TILE)
            applied = dot(left[rows, :HALF], upper[...]) + dot(left[rows, HALF:], lower[...])
            precond = dot(applied.astype(BF16), right[...])

            @pl.when(i == place // TILE)
            def _():
                kept[...] = precond

            return total + jnp.sum(precond * precond, axis=0, keepdims=True)

        total = lax.fori_loop(0, BS // TILE, tile, jnp.zeros((1, BS), F32))
        scale = 1.0 / jnp.sqrt(jnp.sum(total) / (BS * BS) + EPS)
        scaled = kept[pl.ds(pl.multiple_of(place % TILE, ROWS), ROWS)] * scale
        for x in range(NX):
            out[x] = scaled[:, x * WIDTH : (x + 1) * WIDTH].astype(BF16)

    @pl.when(core == 0)
    def _():
        run(root, far_root, mine, other)

    @pl.when(core == 1)
    def _():
        run(far_root, root, other, mine)


def factor_kernel(
    where, mine, other, left_gram, right_gram, left_root, right_root, fifth, far_fifth,
    left_next, right_next, left_refined, right_refined, whole, columns,
):
    z, core = where[0], where[1]
    even = core == 0
    whole[pl.ds(pl.multiple_of(core * HALF, HALF), HALF)] = mine[...]
    whole[pl.ds(pl.multiple_of((1 - core) * HALF, HALF), HALF)] = other[...]
    rows = whole[pl.ds(pl.multiple_of((z * NC + core) * ROWS, ROWS), ROWS)]
    left = BETA * left_gram[...] + dot(rows, whole[...], ((1,), (1,)))
    left_next[...] = left
    slab = whole[:, pl.ds(pl.multiple_of(z * NC * ROWS, 128), NC * ROWS)]
    columns[...] = slab.astype(F32).T
    turned = columns[pl.ds(pl.multiple_of(core * ROWS, ROWS), ROWS)].astype(BF16)
    right = BETA * right_gram[...] + dot(turned, whole[...])
    right_next[...] = right
    own = dot(jnp.where(even, left, right).astype(BF16), fifth[...])
    far = dot(jnp.where(even, right, left).astype(BF16), far_fifth[...])
    left_refined[...] = (5.0 * left_root[...] - jnp.where(even, own, far)) / 4.0
    right_refined[...] = (5.0 * right_root[...] - jnp.where(even, far, own)) / 4.0


def on_device(activations, cotangent, left_gram, right_gram, left_root, right_root):
    left_gram, right_gram = left_gram[0], right_gram[0]
    left_root, right_root = left_root[0], right_root[0]
    z, core = lax.axis_index("z"), lax.axis_index("core")
    where = jnp.stack([z, core]).astype(jnp.int32)
    even = core == 0

    packed = call(
        pack_kernel, jax.ShapeDtypeStruct((TOKENS, ROOT + HALF), BF16), [SMEM] + [VMEM] * 4,
        flops=100_000, moved=1_500_000,
    )(where, activations, cotangent, left_root, right_root)
    more = lax.ppermute(packed, "core", SWAP)
    partial, shard = call(
        partial_kernel,
        (
            jax.ShapeDtypeStruct((NX, NZ, ROWS, WIDTH), BF16),
            jax.ShapeDtypeStruct((NC * ROWS, BS), BF16),
        ),
        [SMEM] + [VMEM] * 5, flops=2 * 256 * 2048 * 256, moved=3_000_000,
    )(where, activations, cotangent, left_root, right_root, more)
    root = lax.all_gather(shard, "z", axis=0, tiled=True)
    parts = lax.all_to_all(
        partial.reshape(NX * NZ, ROWS, WIDTH), ("x", "z"), 0, 0, tiled=True
    ).reshape(NX, NZ, ROWS, WIDTH)
    copies = call(
        sum_kernel, jax.ShapeDtypeStruct((NZ, ROWS, BS), BF16), [VMEM], flops=1_000_000, moved=2_000_000
    )(parts)
    mine = lax.all_to_all(copies, "z", 0, 0, tiled=True).reshape(HALF, BS)
    other = lax.ppermute(mine, "core", SWAP)

    far_root = lax.ppermute(root, "core", SWAP)
    square = jax.ShapeDtypeStruct((BS, BS), BF16)
    fifth = call(
        power_kernel, square, [VMEM], scratch=[pltpu.VMEM((BS, BS), BF16)] * 2,
        flops=6 * BS**3, moved=4_000_000,
    )(root)
    far_fifth = lax.ppermute(fifth, "core", SWAP)

    precond = call(
        precond_kernel, jax.ShapeDtypeStruct((NX, ROWS, WIDTH), BF16), [SMEM] + [VMEM] * 4,
        scratch=[pltpu.VMEM((TILE, BS), F32)], flops=4 * BS**3, moved=6_000_000,
    )(where, mine, other, root, far_root)
    arrived = lax.all_to_all(precond, "x", 0, 0, tiled=True)
    shape = jax.ShapeDtypeStruct((ROWS, BS), F32)
    outs = call(
        factor_kernel, (shape,) * 4, [SMEM] + [VMEM] * 8,
        scratch=[pltpu.VMEM((BS, BS), BF16), pltpu.VMEM((NC * ROWS, BS), F32)],
        flops=8 * 64 * 1024 * 1024, moved=8_000_000,
    )(where, mine, other, left_gram, right_gram, left_root, right_root, fifth, far_fifth)
    return (*(o[None] for o in outs), arrived.astype(F32))


def solution(mesh):
    split = Mesh(mesh.devices.reshape(NZ, NC, NY, NX), (*TOK, *HID))
    factor = P(HID, TOK, None)
    return jax.shard_map(
        on_device,
        mesh=split,
        in_specs=(P(TOK, None), P(TOK, HID), factor, factor, factor, factor),
        out_specs=(factor, factor, factor, factor, P(None, TOK, HID)),
        check_vma=False,
    )
```

time: 148 us -> 138 us (0.932); the launches traced: 148 us -> 136 us
  blocking collectives: 59.1 us -> 38.1 us
  Pallas kernels: 9.64 us -> 26.8 us
  matrix products: 14 us -> 0 us
  waiting for transfers between devices: 9.13 us -> 17.5 us
  other arithmetic: 8.85 us -> 0.8 us
  local copies, waits for them, and re-layouts: 0.04 us -> 7.16 us
    pallas_call x3 -> x4, Pallas kernels: 4.09 us -> 20.5 us  [the longest x1 9.91 us: on_device(): call(power_kernel, square, [VMEM], scratch=[pltpu.VMEM((BS, BS), BF16)] *...]
    all_to_all x1 -> x0, blocking collectives: 15.9 us -> none  [on_device(): sums = lax.all_to_all(squares, ('x', 'z', 'core'), 0, 0, tiled=True)]
    dot_general x2 -> x0, matrix products: 14 us -> none  [dot(): return lax.dot_general(a, b, (dims, ((), ())), preferred_element_type=F32)]
    all_gather x1, waiting for transfers between devices: 4.09 us -> 12.6 us  [on_device(): root = lax.all_gather(shard, 'z', axis=0, tiled=True)]
    select_n x6 -> x0, other arithmetic: 8 us -> none  [the longest x1 3.9 us: on_device(): right_power = jnp.where(even, far_fifth, fifth)]
    unnamed x14 -> x20, local copies, waits for them, and re-layouts: 0.04 us -> 7.16 us
    all_to_all x1, blocking collectives: 43.1 us -> 38.1 us  [on_device(): lax.all_to_all(partial.reshape(NX * NZ, ROWS, WIDTH), ('x', 'z'), 0, 0, t...]
    ppermute x3 -> x1, starting transfers between devices: 13.1 us -> 8.79 us  [on_device(): more = lax.ppermute(packed, 'core', SWAP)]
  transfers between devices with their start and end apart: 9 -> 7, of which waited for: 5 -> 3; matrix products, arithmetic and copies ran while one was open for 13% -> 0% of each run, Pallas kernels for 6% -> 18%
where the time goes in v2:
time: 138 us; the launch traced here: 136 us
  blocking collectives  38.1 us (28%)
  starting transfers between devices  31.8 us (23%)
  Pallas kernels  26.8 us (19%)
  waiting for transfers between devices  17.5 us (13%)
  between operations  14.2 us (10%)
  local copies, waits for them, and re-layouts  7.16 us (5%)
    all_to_all x1, blocking collectives, on_device(): lax.all_to_all(partial.reshape(NX * NZ, ROWS, WIDTH), ('x', 'z'), 0, 0, t...  38.1 us
    all_gather x1, waiting for transfers between devices, on_device(): root = lax.all_gather(shard, 'z', axis=0, tiled=True)  12.6 us
    pallas_call x1, Pallas kernels, on_device(): call(power_kernel, square, [VMEM], scratch=[pltpu.VMEM((BS, BS), BF16)] *...  9.91 us
    ppermute x1, starting transfers between devices, on_device(): more = lax.ppermute(packed, 'core', SWAP)  8.79 us
    all_to_all x1, starting transfers between devices, on_device(): mine = lax.all_to_all(copies, 'z', 0, 0, tiled=True).reshape(HALF, BS)  8.63 us
    pallas_call x1, Pallas kernels, on_device(): call(precond_kernel, jax.ShapeDtypeStruct((NX, ROWS, WIDTH), BF16), [SMEM...  8.01 us
    unnamed x20, local copies, waits for them, and re-layouts  7.16 us
    ppermute x1, starting transfers between devices, on_device(): far_root = lax.ppermute(root, 'core', SWAP)  6.38 us
  transfers between devices with their start and end apart: 7, of which 3 were waited for; matrix products, arithmetic and copies ran while one was open for 0% of the time, Pallas kernels for 18%

profile of v2, /device:TPU:1, one launch (start us, length us, event | category | flops | bytes accessed | tf_op | source)
XLA Modules:
  0.0 136.3 jit_solution(9638165379162169313)
XLA Ops:
  7.2 0.1 pad_add_fusion.where
  7.3 1.2 copy-done
  8.5 0.9 copy-done.1
  9.5 0.9 copy-done.3
  10.4 0.8 copy-done.5
  11.3 0.6 shard_map.101
  11.9 8.8 %collective-permute-start = (bf16[128,2816]{1,0:T(8,128)(2,1)S(1)}, bf16[128,2816]{1,0:T(8,128)(2,1)S(1)}, u32[]{:S(2)}, u32[]{:S(2)}) collective-permute-start(bf16[128,2816]{1,0:T(8,128)(2,1)S(1)} %shard_map.101), channel_id=1, source_target_pairs={{0,32},{32,0},{1,33},{33,1},{2,34},{34,2},{3,35},{35,3},{4,36},{36... | collective-permute-start | bytes 2162696 | tf_op jit(solution)/shard_map/ppermute | solution.py:162
  20.7 1.8 %collective-permute-done.more = bf16[128,2816]{1,0:T(8,128)(2,1)S(1)} collective-permute-done((bf16[128,2816]{1,0:T(8,128)(2,1)S(1)}, bf16[128,2816]{1,0:T(8,128)(2,1)S(1)}, u32[]{:S(2)}, u32[]{:S(2)}) %collective-permute-start) | collective-permute-done | bytes 720928 | tf_op jit(solution)/shard_map/ppermute | solution.py:162
  22.5 2.0 %shard_map.102 = (bf16[4,8,64,256]{3,2,1,0:T(8,128)(2,1)S(1)}, bf16[128,1024]{1,0:T(8,128)(2,1)}) custom-call(s32[2]{0:T(128)S(1)} %pad_add_fusion.where, bf16[128,4096]{1,0:T(8,128)(2,1)S(1)} %copy-done, bf16[128,256]{1,0:T(8,128)(2,1)S(1)} %copy-done.5, f32[64,1024]{1,0:T(8,128)S(1)} %bitcast.18, f32[64,1024]{1,0:T(8,128)S(1)} %bitcast.21, ...), custom_call_target="tpu_custom_call" | custom-call | flops 268435456 | bytes 3000000 | tf_op jit(solution)/shard_map/pallas_call | solution.py:163
  24.4 38.1 %all_to_all.15 = bf16[32,64,256]{2,1,0:T(8,128)(2,1)S(1)} all-to-all(bf16[32,64,256]{2,1,0:T(8,128)(2,1)S(1)} %bitcast.23), channel_id=1, replica_groups=mesh['z'=8,'core'=2,'y'=8,'x'=4] {'x','z'}, dimensions={0} | all-to-all | bytes 2097152 | tf_op jit(solution)/shard_map/all_to_all | solution.py:172
  62.5 1.2 shard_map.103
  63.7 8.6 %all-to-all-start.1 = ((bf16[8,64,1024]{2,1,0:T(8,128)(2,1)}), bf16[8,64,1024]{2,1,0:T(8,128)(2,1)S(1)}, u32[]{:S(2)}, u32[]{:S(2)}) async-start(bf16[8,64,1024]{2,1,0:T(8,128)(2,1)} %shard_map.103), calls=%async_computation.1 | async-start | bytes 2097152 | tf_op jit(solution)/shard_map/all_to_all | solution.py:178
  72.4 12.6 %all-gather.2.cloned.1.call-done.root = bf16[1024,1024]{1,0:T(8,128)(2,1)} async-done(((bf16[128,1024]{1,0:T(8,128)(2,1)}), bf16[1024,1024]{1,0:T(8,128)(2,1)}) %all-gather.2.cloned.1.call-update) | async-done | bytes 2097168 | tf_op jit(solution)/shard_map/all_gather | solution.py:171
  85.0 6.4 %collective-permute-start.3 = (bf16[1024,1024]{1,0:T(8,128)(2,1)}, bf16[1024,1024]{1,0:T(8,128)(2,1)}, u32[]{:S(2)}, u32[]{:S(2)}) collective-permute-start(bf16[1024,1024]{1,0:T(8,128)(2,1)} %all-gather.2.cloned.1.call-done.root), channel_id=1, source_target_pairs={{0,32},{32,0},{1,33},{33,1},{2,34},{34,2},{3,35},{35,3},{4,36},{36... | collective-permute-start | bytes 6291464 | tf_op jit(solution)/shard_map/ppermute | solution.py:181
  91.4 1.6 %copy-done.8 = bf16[1024,1024]{1,0:T(8,128)(2,1)S(1)} copy-done((bf16[1024,1024]{1,0:T(8,128)(2,1)S(1)}, bf16[1024,1024]{1,0:T(8,128)(2,1)}, u32[]{:S(2)}) %copy-start.8) | copy-done | bytes 2097176
  93.0 9.9 %shard_map.104.fifth = bf16[1024,1024]{1,0:T(8,128)(2,1)} custom-call(bf16[1024,1024]{1,0:T(8,128)(2,1)S(1)} %copy-done.8), custom_call_target="tpu_custom_call" | custom-call | flops 6442450944 | bytes 4000000 | tf_op jit(solution)/shard_map/pallas_call | solution.py:183
  102.9 1.9 %collective-permute-start.2 = (bf16[1024,1024]{1,0:T(8,128)(2,1)}, bf16[1024,1024]{1,0:T(8,128)(2,1)}, u32[]{:S(2)}, u32[]{:S(2)}) collective-permute-start(bf16[1024,1024]{1,0:T(8,128)(2,1)} %shard_map.104.fifth), channel_id=1, source_target_pairs={{0,32},{32,0},{1,33},{33,1},{2,34},{34,2},{3,35},{35,3},{4,36},{36... | collective-permute-start | bytes 6291464 | tf_op jit(solution)/shard_map/ppermute | solution.py:187
  104.9 2.5 %collective-permute-start.1 = (bf16[512,1024]{1,0:T(8,128)(2,1)S(1)}, bf16[512,1024]{1,0:T(8,128)(2,1)S(1)}, u32[]{:S(2)}, u32[]{:S(2)}) collective-permute-start(bf16[512,1024]{1,0:T(8,128)(2,1)S(1)} %bitcast.14), channel_id=1, source_target_pairs={{0,32},{32,0},{1,33},{33,1},{2,34},{34,2},{3,35},{35,3},{4,36},{36... | collective-permute-start | bytes 3145736 | tf_op jit(solution)/shard_map/ppermute | solution.py:179
  107.4 3.0 %collective-permute-done.1.other = bf16[512,1024]{1,0:T(8,128)(2,1)S(1)} collective-permute-done((bf16[512,1024]{1,0:T(8,128)(2,1)S(1)}, bf16[512,1024]{1,0:T(8,128)(2,1)S(1)}, u32[]{:S(2)}, u32[]{:S(2)}) %collective-permute-start.1) | collective-permute-done | bytes 1048608 | tf_op jit(solution)/shard_map/ppermute | solution.py:179
  110.5 1.6 %copy-done.9 = bf16[1024,1024]{1,0:T(8,128)(2,1)S(1)} copy-done((bf16[1024,1024]{1,0:T(8,128)(2,1)S(1)}, bf16[1024,1024]{1,0:T(8,128)(2,1)}, u32[]{:S(2)}) %copy-start.9) | copy-done | bytes 2097176
  112.1 8.0 %shard_map.106 = bf16[4,64,256]{2,1,0:T(8,128)(2,1)} custom-call(s32[2]{0:T(128)S(1)} %pad_add_fusion.where, bf16[512,1024]{1,0:T(8,128)(2,1)S(1)} %bitcast.15, bf16[512,1024]{1,0:T(8,128)(2,1)S(1)} %collective-permute-done.1.other, bf16[1024,1024]{1,0:T(8,128)(2,1)S(1)} %copy-done.9, bf16[1024,1024]{1,0:T(8,128)(2,1)} %collective-permute-done.3.far_root), custom_call_target="tpu_custom_call" | custom-call | flops 4294967296 | bytes 6000000 | tf_op jit(solution)/shard_map/pallas_call | solution.py:189
  120.1 3.5 %all-to-all-start.2 = ((bf16[4,64,256]{2,1,0:T(8,128)(2,1)}), bf16[4,64,256]{2,1,0:T(8,128)(2,1)S(1)}, u32[]{:S(2)}, u32[]{:S(2)}) async-start(bf16[4,64,256]{2,1,0:T(8,128)(2,1)} %shard_map.106), calls=%async_computation.2 | async-start | bytes 262144 | tf_op jit(solution)/shard_map/all_to_all | solution.py:193
  123.6 5.1 %shard_map.105 = (f32[64,1024]{1,0:T(8,128)}, f32[64,1024]{1,0:T(8,128)}, f32[64,1024]{1,0:T(8,128)}, f32[64,1024]{1,0:T(8,128)}) custom-call(s32[2]{0:T(128)S(1)} %pad_add_fusion.where, bf16[512,1024]{1,0:T(8,128)(2,1)S(1)} %bitcast.16, bf16[512,1024]{1,0:T(8,128)(2,1)S(1)} %collective-permute-done.1.other, f32[64,1024]{1,0:T(8,128)S(1)} %bitcast.24, ...), custom_call_target="tpu_custom_call" | custom-call | flops 536870912 | bytes 8000000 | tf_op jit(solution)/shard_map/pallas_call | solution.py:195
  128.7 0.7 convert_element_type.3
  (20 shorter events, 0.1 us)
Async XLA Ops:
  7.2 77.9 %all-gather.2.cloned.1.call-start = ((), (), s32[]{:S(2)}) async-start(), calls=%async_computation.3 | async-start | bytes 2359296 | tf_op jit(solution)/shard_map/all_gather | solution.py:171
  7.3 1.2 copy-start
  8.5 0.9 copy-start.1
  9.5 0.9 copy-start.3
  10.4 0.8 copy-start.5
  11.9 10.6 %collective-permute-start = (bf16[128,2816]{1,0:T(8,128)(2,1)S(1)}, bf16[128,2816]{1,0:T(8,128)(2,1)S(1)}, u32[]{:S(2)}, u32[]{:S(2)}) collective-permute-start(bf16[128,2816]{1,0:T(8,128)(2,1)S(1)} %shard_map.101), channel_id=1, source_target_pairs={{0,32},{32,0},{1,33},{33,1},{2,34},{34,2},{3,35},{35,3},{4,36},{36... | collective-permute-start | bytes 2162696 | tf_op jit(solution)/shard_map/ppermute | solution.py:162
  63.7 41.1 %all-to-all-start.1 = ((bf16[8,64,1024]{2,1,0:T(8,128)(2,1)}), bf16[8,64,1024]{2,1,0:T(8,128)(2,1)S(1)}, u32[]{:S(2)}, u32[]{:S(2)}) async-start(bf16[8,64,1024]{2,1,0:T(8,128)(2,1)} %shard_map.103), calls=%async_computation.1 | async-start | bytes 2097152 | tf_op jit(solution)/shard_map/all_to_all | solution.py:178
  85.0 25.4 %collective-permute-start.3 = (bf16[1024,1024]{1,0:T(8,128)(2,1)}, bf16[1024,1024]{1,0:T(8,128)(2,1)}, u32[]{:S(2)}, u32[]{:S(2)}) collective-permute-start(bf16[1024,1024]{1,0:T(8,128)(2,1)} %all-gather.2.cloned.1.call-done.root), channel_id=1, source_target_pairs={{0,32},{32,0},{1,33},{33,1},{2,34},{34,2},{3,35},{35,3},{4,36},{36... | collective-permute-start | bytes 6291464 | tf_op jit(solution)/shard_map/ppermute | solution.py:181
  91.4 1.6 %copy-start.8 = (bf16[1024,1024]{1,0:T(8,128)(2,1)S(1)}, bf16[1024,1024]{1,0:T(8,128)(2,1)}, u32[]{:S(2)}) copy-start(bf16[1024,1024]{1,0:T(8,128)(2,1)} %all-gather.2.cloned.1.call-done.root) | copy-start | bytes 6291460
  102.9 20.6 %collective-permute-start.2 = (bf16[1024,1024]{1,0:T(8,128)(2,1)}, bf16[1024,1024]{1,0:T(8,128)(2,1)}, u32[]{:S(2)}, u32[]{:S(2)}) collective-permute-start(bf16[1024,1024]{1,0:T(8,128)(2,1)} %shard_map.104.fifth), channel_id=1, source_target_pairs={{0,32},{32,0},{1,33},{33,1},{2,34},{34,2},{3,35},{35,3},{4,36},{36... | collective-permute-start | bytes 6291464 | tf_op jit(solution)/shard_map/ppermute | solution.py:187
  104.8 18.7 %copy-start.2 = (f32[1,64,1024]{2,1,0:T(8,128)S(1)}, f32[1,64,1024]{2,1,0:T(8,128)}, u32[]{:S(2)}) copy-start(f32[1,64,1024]{2,1,0:T(8,128)} %param.10) | copy-start | bytes 786436
  104.9 18.7 %copy-start.4 = (f32[1,64,1024]{2,1,0:T(8,128)S(1)}, f32[1,64,1024]{2,1,0:T(8,128)}, u32[]{:S(2)}) copy-start(f32[1,64,1024]{2,1,0:T(8,128)} %param.11) | copy-start | bytes 786436
  104.9 18.7 %copy-start.6 = (f32[1,64,1024]{2,1,0:T(8,128)S(1)}, f32[1,64,1024]{2,1,0:T(8,128)}, u32[]{:S(2)}) copy-start(f32[1,64,1024]{2,1,0:T(8,128)} %param.8) | copy-start | bytes 786436
  104.9 18.7 %copy-start.7 = (f32[1,64,1024]{2,1,0:T(8,128)S(1)}, f32[1,64,1024]{2,1,0:T(8,128)}, u32[]{:S(2)}) copy-start(f32[1,64,1024]{2,1,0:T(8,128)} %param.9) | copy-start | bytes 786436
  104.9 5.6 %collective-permute-start.1 = (bf16[512,1024]{1,0:T(8,128)(2,1)S(1)}, bf16[512,1024]{1,0:T(8,128)(2,1)S(1)}, u32[]{:S(2)}, u32[]{:S(2)}) collective-permute-start(bf16[512,1024]{1,0:T(8,128)(2,1)S(1)} %bitcast.14), channel_id=1, source_target_pairs={{0,32},{32,0},{1,33},{33,1},{2,34},{34,2},{3,35},{35,3},{4,36},{36... | collective-permute-start | bytes 3145736 | tf_op jit(solution)/shard_map/ppermute | solution.py:179
  110.5 1.6 %copy-start.9 = (bf16[1024,1024]{1,0:T(8,128)(2,1)S(1)}, bf16[1024,1024]{1,0:T(8,128)(2,1)}, u32[]{:S(2)}) copy-start(bf16[1024,1024]{1,0:T(8,128)(2,1)} %all-gather.2.cloned.1.call-done.root) | copy-start | bytes 6291460
  120.1 8.6 %all-to-all-start.2 = ((bf16[4,64,256]{2,1,0:T(8,128)(2,1)}), bf16[4,64,256]{2,1,0:T(8,128)(2,1)S(1)}, u32[]{:S(2)}, u32[]{:S(2)}) async-start(bf16[4,64,256]{2,1,0:T(8,128)(2,1)} %shard_map.106), calls=%async_computation.2 | async-start | bytes 262144 | tf_op jit(solution)/shard_map/all_to_all | solution.py:193
Sparse Core Ops, SparseCore 0:
  24.6 60.4 all-gather.1

commit v3 on v2

v3 whole, which is shorter than its diff:
```python
import jax
import jax.numpy as jnp
from jax import lax
from jax.experimental import pallas as pl
from jax.experimental.pallas import tpu as pltpu
from jax.sharding import Mesh
from jax.sharding import PartitionSpec as P

BETA = 0.95
EPS = 1e-06
F32 = jnp.float32
BF16 = jnp.bfloat16
NZ, NC, NY, NX = 8, 2, 8, 4
BS = 1024
HALF = BS // NC
TOKENS = 128
ROWS = BS // (NZ * NC)
WIDTH = BS // NX
COT = NX * HALF
ROOT = COT + WIDTH
TILE = 512
SIDE = NC * ROWS
OFF = 3
STRIP = OFF * 2 * SIDE + SIDE
SLABS = NX * ROWS
CHUNK = SLABS + ROWS + ROWS // 2
TOK = ("z", "core")
HID = ("y", "x")
SWAP = [(0, 1), (1, 0)]
VMEM = pl.BlockSpec(memory_space=pltpu.VMEM)
SMEM = pl.BlockSpec(memory_space=pltpu.SMEM)
HBM = pl.BlockSpec(memory_space=pltpu.HBM)
PARAMS = pltpu.CompilerParams(vmem_limit_bytes=48 * 1024 * 1024)


def dot(a, b, dims=((1,), (0,))):
    return lax.dot_general(a, b, (dims, ((), ())), preferred_element_type=F32)


def call(body, outs, specs, scratch=(), flops=0, moved=0):
    return pl.pallas_call(
        body,
        out_shape=outs,
        in_specs=specs,
        out_specs=jax.tree.map(lambda _: VMEM, outs),
        scratch_shapes=list(scratch),
        compiler_params=PARAMS,
        cost_estimate=pl.CostEstimate(flops=flops, bytes_accessed=moved, transcendentals=0),
    )


def at(start, size, unit):
    return pl.ds(pl.multiple_of(start, unit), size)


def pack_kernel(where, act, cot, left_root, right_root, own, far, roots, sems):
    core = where[1]
    copies = []
    for k, (out, side) in enumerate(((far, 1 - core), (own, core))):
        for r in range(NX):
            source = act.at[:, at(r * BS + side * HALF, HALF, 128)]
            target = out.at[:, pl.ds(r * HALF, HALF)]
            copies.append(pltpu.make_async_copy(source, target, sems.at[k, r]))
        copies.append(pltpu.make_async_copy(cot, out.at[:, pl.ds(COT, WIDTH)], sems.at[k, NX]))
    copies.append(pltpu.make_async_copy(left_root, roots.at[0], sems.at[0, NX + 1]))
    copies.append(pltpu.make_async_copy(right_root, roots.at[1], sems.at[1, NX + 1]))
    for copy in copies:
        copy.start()
    for copy in copies:
        copy.wait()
    for out, side in ((far, 1 - core), (own, core)):
        low = roots[side].astype(BF16)
        out[:ROWS, ROOT:] = low[:, :HALF]
        out[ROWS:, ROOT:] = low[:, HALF:]


def partial_kernel(where, own, more, out, strip, shard):
    z, core = where[0], where[1]
    for r in range(NX):
        cols = slice(r * HALF, (r + 1) * HALF)
        total = dot(own[:, cols], own[:, COT : COT + WIDTH], ((0,), (0,)))
        total += dot(more[:, cols], more[:, COT : COT + WIDTH], ((0,), (0,)))
        low = total.astype(BF16)
        for to in range(NZ):
            out[to, r * ROWS : (r + 1) * ROWS] = low[to * ROWS : (to + 1) * ROWS]
    for given, side in ((own, core), (more, 1 - core)):
        rows = at(side * ROWS, ROWS, ROWS)
        shard[rows, :HALF] = given[:ROWS, ROOT:]
        shard[rows, HALF:] = given[ROWS:, ROOT:]

    def block(k):
        return shard[:, at(lax.rem(z + k, NZ) * SIDE, SIDE, SIDE)]

    for k in range(1, OFF + 1):
        piece, first = block(k), (k - 1) * 2 * SIDE
        strip[:, first : first + SIDE] = piece[:ROWS]
        strip[:, first + SIDE : first + 2 * SIDE] = piece[ROWS:]
    middle, across = block(0), block(OFF + 1)
    strip[:, OFF * 2 * SIDE :] = across[:ROWS]
    for to in range(NZ):
        out[to, SLABS : SLABS + ROWS, :SIDE] = middle[:ROWS]
        out[to, SLABS : SLABS + ROWS, SIDE:] = middle[ROWS:]
        out[to, SLABS + ROWS :, :SIDE] = across[ROWS : ROWS + ROWS // 2]
        out[to, SLABS + ROWS :, SIDE:] = across[ROWS + ROWS // 2 :]


def sum_kernel(parts, out):
    for x in range(NX):
        rows = slice(x * ROWS, (x + 1) * ROWS)
        total = parts[0, rows].astype(F32)
        for z in range(1, NZ):
            total += parts[z, rows].astype(F32)
        low = total.astype(BF16)
        for z in range(NZ):
            out[x, z] = low


def root_kernel(strips, parts, root):
    for z in range(NZ):
        top, low = slice(z * SIDE, z * SIDE + ROWS), slice(z * SIDE + ROWS, (z + 1) * SIDE)
        own = slice(z * SIDE, (z + 1) * SIDE)
        root[top, own] = parts[z, SLABS : SLABS + ROWS, :SIDE]
        root[low, own] = parts[z, SLABS : SLABS + ROWS, SIDE:]
        for k in range(1, OFF + 1):
            j, first = (z + k) % NZ, (k - 1) * 2 * SIDE
            piece = jnp.concatenate(
                [strips[z, :, first : first + SIDE], strips[z, :, first + SIDE : first + 2 * SIDE]],
                axis=0,
            )
            there = slice(j * SIDE, (j + 1) * SIDE)
            root[own, there] = piece
            root[there, own] = piece.T
        j = (z + OFF + 1) % NZ
        there = slice(j * SIDE, (j + 1) * SIDE)
        half = z * SIDE + ROWS + ROWS // 2
        root[top, there] = strips[z, :, OFF * 2 * SIDE :]
        root[z * SIDE + ROWS : half, there] = parts[z, SLABS + ROWS :, :SIDE]
        root[half : (z + 1) * SIDE, there] = parts[z, SLABS + ROWS :, SIDE:]


def precond_kernel(where, mine, other, root, far_root, out, kept):
    z, core = where[0], where[1]
    place = (z * NC + core) * ROWS

    def run(left, right, upper, lower):
        def tile(i, total):
            rows = at(i * TILE, TILE, TILE)
            first, second = left[rows, :HALF], left[rows, HALF:]
            applied = jnp.concatenate(
                [(dot(first, upper[x]) + dot(second, lower[x])).astype(BF16) for x in range(NX)],
                axis=1,
            )
            precond = dot(applied, right[...])

            @pl.when(i == place // TILE)
            def _():
                kept[...] = precond

            return total + jnp.sum(precond * precond, axis=0, keepdims=True)

        total = lax.fori_loop(0, BS // TILE, tile, jnp.zeros((1, BS), F32))
        scale = 1.0 / jnp.sqrt(jnp.sum(total) / (BS * BS) + EPS)
        scaled = kept[at(place % TILE, ROWS, ROWS)] * scale
        for x in range(NX):
            out[x] = scaled[:, x * WIDTH : (x + 1) * WIDTH].astype(BF16)

    @pl.when(core == 0)
    def _():
        run(root, far_root, mine, other)

    @pl.when(core == 1)
    def _():
        run(far_root, root, other, mine)


def power_kernel(root, fifth, squared, fourth):
    def times(a, b, out):
        def tile(i, carry):
            rows = at(i * TILE, TILE, TILE)
            out[rows] = dot(a[rows], b[...]).astype(BF16)
            return carry

        lax.fori_loop(0, BS // TILE, tile, 0)

    times(root, root, squared)
    times(squared, squared, fourth)
    times(fourth, root, fifth)


def factor_kernel(
    where, mine, other, left_gram, right_gram, left_root, right_root, fifth, far_fifth,
    left_next, right_next, left_refined, right_refined, whole, columns, old, sems,
):
    z, core = where[0], where[1]
    even = core == 0
    copies = [
        pltpu.make_async_copy(source, old.at[k], sems.at[k])
        for k, source in enumerate((left_gram, right_gram, left_root, right_root))
    ]
    for copy in copies:
        copy.start()
    for x in range(NX):
        whole[at(core * HALF, HALF, HALF), x * WIDTH : (x + 1) * WIDTH] = mine[x]
        whole[at((1 - core) * HALF, HALF, HALF), x * WIDTH : (x + 1) * WIDTH] = other[x]
    slab = whole[:, at(z * SIDE, SIDE, SIDE)]
    columns[...] = slab.astype(F32).T
    rows = whole[at((z * NC + core) * ROWS, ROWS, ROWS)]
    left = dot(rows, whole[...], ((1,), (1,)))
    turned = columns[at(core * ROWS, ROWS, ROWS)].astype(BF16)
    right = dot(turned, whole[...])
    for copy in copies:
        copy.wait()
    left = BETA * old[0] + left
    left_next[...] = left
    right = BETA * old[1] + right
    right_next[...] = right
    own = dot(jnp.where(even, left, right).astype(BF16), fifth[...])
    far = dot(jnp.where(even, right, left).astype(BF16), far_fifth[...])
    left_refined[...] = (5.0 * old[2] - jnp.where(even, own, far)) / 4.0
    right_refined[...] = (5.0 * old[3] - jnp.where(even, far, own)) / 4.0


def on_device(activations, cotangent, left_gram, right_gram, left_root, right_root):
    left_gram, right_gram = left_gram[0], right_gram[0]
    left_root, right_root = left_root[0], right_root[0]
    where = jnp.stack([lax.axis_index("z"), lax.axis_index("core")]).astype(jnp.int32)

    half = jax.ShapeDtypeStruct((TOKENS, ROOT + HALF), BF16)
    own, far = call(
        pack_kernel, (half, half), [SMEM] + [HBM] * 4,
        scratch=[pltpu.VMEM((2, ROWS, BS), F32), pltpu.SemaphoreType.DMA((2, NX + 2))],
        flops=100_000, moved=1_500_000,
    )(where, activations, cotangent, left_root, right_root)
    more = lax.ppermute(far, "core", SWAP)
    partial, strip = call(
        partial_kernel,
        (
            jax.ShapeDtypeStruct((NZ, CHUNK, WIDTH), BF16),
            jax.ShapeDtypeStruct((ROWS, STRIP), BF16),
        ),
        [SMEM, VMEM, VMEM], scratch=[pltpu.VMEM((SIDE, BS), BF16)],
        flops=2 * 256 * 2048 * 256, moved=3_000_000,
    )(where, own, more)
    parts = lax.all_to_all(partial, "z", 0, 0, tiled=True)
    strips = lax.all_gather(strip, "z", axis=0)
    parts, strips = lax.optimization_barrier((parts, strips))
    copies = call(
        sum_kernel, jax.ShapeDtypeStruct((NX, NZ, ROWS, WIDTH), BF16), [VMEM],
        flops=1_000_000, moved=2_000_000,
    )(parts)
    root = call(
        root_kernel, jax.ShapeDtypeStruct((BS, BS), BF16), [VMEM, VMEM], flops=1_000_000, moved=4_000_000
    )(strips, parts)
    far_root = lax.ppermute(root, "core", SWAP)
    fifth = call(
        power_kernel, jax.ShapeDtypeStruct((BS, BS), BF16), [VMEM],
        scratch=[pltpu.VMEM((BS, BS), BF16)] * 2, flops=6 * BS**3, moved=4_000_000,
    )(root)
    far_fifth = lax.ppermute(fifth, "core", SWAP)
    mine = lax.all_to_all(
        copies.reshape(NX * NZ, ROWS, WIDTH), ("x", "z"), 0, 0, tiled=True
    ).reshape(NX, HALF, WIDTH)
    other = lax.ppermute(mine, "core", SWAP)

    precond = call(
        precond_kernel, jax.ShapeDtypeStruct((NX, ROWS, WIDTH), BF16), [SMEM] + [VMEM] * 4,
        scratch=[pltpu.VMEM((TILE, BS), F32)], flops=4 * BS**3, moved=6_000_000,
    )(where, mine, other, root, far_root)
    arrived = lax.all_to_all(precond, "x", 0, 0, tiled=True)
    shape = jax.ShapeDtypeStruct((ROWS, BS), F32)
    outs = call(
        factor_kernel, (shape,) * 4, [SMEM, VMEM, VMEM] + [HBM] * 4 + [VMEM] * 2,
        scratch=[
            pltpu.VMEM((BS, BS), BF16),
            pltpu.VMEM((SIDE, BS), F32),
            pltpu.VMEM((4, ROWS, BS), F32),
            pltpu.SemaphoreType.DMA((4,)),
        ],
        flops=8 * 64 * 1024 * 1024, moved=8_000_000,
    )(where, mine, other, left_gram, right_gram, left_root, right_root, fifth, far_fifth)
    return (*(o[None] for o in outs), arrived.astype(F32))


def solution(mesh):
    split = Mesh(mesh.devices.reshape(NZ, NC, NY, NX), (*TOK, *HID))
    factor = P(HID, TOK, None)
    return jax.shard_map(
        on_device,
        mesh=split,
        in_specs=(P(TOK, None), P(TOK, HID), factor, factor, factor, factor),
        out_specs=(factor, factor, factor, factor, P(None, TOK, HID)),
        check_vma=False,
    )
```

time: 138 us -> 134 us (0.971)
  waiting for transfers between devices: 17.5 us -> 4.06 us
  between operations: 14.2 us -> 0.8 us
  starting transfers between devices: 31.8 us -> 43.8 us
  blocking collectives: 38.1 us -> 49.7 us
  Pallas kernels: 26.8 us -> 30.5 us
  local copies, waits for them, and re-layouts: 7.16 us -> 3.99 us
    all_gather x0 -> x1, blocking collectives: none -> 49.7 us  [on_device(): strips = lax.all_gather(strip, 'z', axis=0)]
    all_to_all x1 -> x0, blocking collectives: 38.1 us -> none  [on_device(): lax.all_to_all(partial.reshape(NX * NZ, ROWS, WIDTH), ('x', 'z'), 0, 0, t...]
    all_gather x1 -> x0, waiting for transfers between devices: 12.6 us -> none  [on_device(): root = lax.all_gather(shard, 'z', axis=0, tiled=True)]
    ppermute x1, starting transfers between devices: 2.53 us -> 8.21 us  [on_device(): other = lax.ppermute(mine, 'core', SWAP)]
    all_to_all x1 -> x2, starting transfers between devices: 8.63 us -> 13.2 us  [the longest x1 8.54 us: on_device(): lax.all_to_all(copies.reshape(NX * NZ, ROWS, WIDTH), ('x', 'z'), 0, 0, ti...]
    pallas_call x5 -> x6, Pallas kernels: 18.8 us -> 22.2 us  [the longest x1 10.4 us: on_device(): call(power_kernel, jax.ShapeDtypeStruct((BS, BS), BF16), [VMEM], scratch=...]
    unnamed x20 -> x16, local copies, waits for them, and re-layouts: 7.16 us -> 3.99 us
    ppermute x1, starting transfers between devices: 6.38 us -> 8.33 us  [on_device(): far_root = lax.ppermute(root, 'core', SWAP)]
  transfers between devices with their start and end apart: 7 -> 7, of which waited for: 3 -> 2; matrix products, arithmetic and copies ran while one was open for 0% -> 0% of each run, Pallas kernels for 18% -> 19%
where the time goes in v3:
time: 134 us
  blocking collectives  49.7 us (37%)
  starting transfers between devices  43.8 us (33%)
  Pallas kernels  30.5 us (23%)
  waiting for transfers between devices  4.06 us (3%)
  local copies, waits for them, and re-layouts  3.99 us (3%)
    all_gather x1, blocking collectives, on_device(): strips = lax.all_gather(strip, 'z', axis=0)  49.7 us
    pallas_call x1, Pallas kernels, on_device(): call(power_kernel, jax.ShapeDtypeStruct((BS, BS), BF16), [VMEM], scratch=...  10.4 us
    ppermute x1, starting transfers between devices, on_device(): more = lax.ppermute(far, 'core', SWAP)  8.79 us
    all_to_all x1, starting transfers between devices, on_device(): lax.all_to_all(copies.reshape(NX * NZ, ROWS, WIDTH), ('x', 'z'), 0, 0, ti...  8.54 us
    pallas_call x1, Pallas kernels, on_device(): call(precond_kernel, jax.ShapeDtypeStruct((NX, ROWS, WIDTH), BF16), [SMEM...  8.35 us
    ppermute x1, starting transfers between devices, on_device(): far_root = lax.ppermute(root, 'core', SWAP)  8.33 us
    ppermute x1, starting transfers between devices, on_device(): other = lax.ppermute(mine, 'core', SWAP)  8.21 us
    pallas_call x1, Pallas kernels, on_device(): call(factor_kernel, (shape,) * 4, [SMEM, VMEM, VMEM] + [HBM] * 4 + [VMEM]...  5.46 us
  transfers between devices with their start and end apart: 7, of which 2 were waited for; matrix products, arithmetic and copies ran while one was open for 0% of the time, Pallas kernels for 19%

profile of v3, /device:TPU:1, one launch (start us, length us, event | category | flops | bytes accessed | tf_op | source)
XLA Modules:
  0.0 133.6 jit_solution(3743898240949031303)
XLA Ops:
  0.6 0.1 pad_add_fusion.where
  0.7 1.2 copy-done
  1.9 0.9 copy-done.1
  2.9 0.9 copy-done.3
  3.8 0.8 copy-done.7
  4.7 0.9 shard_map.101
  5.6 8.8 %collective-permute-start = (bf16[128,2816]{1,0:T(8,128)(2,1)S(1)}, bf16[128,2816]{1,0:T(8,128)(2,1)S(1)}, u32[]{:S(2)}, u32[]{:S(2)}) collective-permute-start(bf16[128,2816]{1,0:T(8,128)(2,1)S(1)} %get-tuple-element.16), channel_id=1, source_target_pairs={{0,32},{32,0},{1,33},{33,1},{2,34},{34,2},{3,35},{35,3},{4,36},{36... | collective-permute-start | bytes 2162696 | tf_op jit(solution)/shard_map/ppermute | solution.py:234
  14.4 1.8 %collective-permute-done.more = bf16[128,2816]{1,0:T(8,128)(2,1)S(1)} collective-permute-done((bf16[128,2816]{1,0:T(8,128)(2,1)S(1)}, bf16[128,2816]{1,0:T(8,128)(2,1)S(1)}, u32[]{:S(2)}, u32[]{:S(2)}) %collective-permute-start) | collective-permute-done | bytes 720928 | tf_op jit(solution)/shard_map/ppermute | solution.py:234
  16.2 2.4 %shard_map.102 = (bf16[8,352,256]{2,1,0:T(8,128)(2,1)}, bf16[64,896]{1,0:T(8,128)(2,1)S(1)}) custom-call(s32[2]{0:T(128)S(1)} %pad_add_fusion.where, bf16[128,2816]{1,0:T(8,128)(2,1)S(1)} %get-tuple-element.15.own, bf16[128,2816]{1,0:T(8,128)(2,1)S(1)} %collective-permute-done.more), custom_call_target="tpu_custom_call" | custom-call | flops 268435456 | bytes 3000000 | tf_op jit(solution)/shard_map/pallas_call | solution.py:235
  18.6 4.7 %all-to-all-start = ((bf16[8,352,256]{2,1,0:T(8,128)(2,1)}), bf16[8,352,256]{2,1,0:T(8,128)(2,1)S(1)}, u32[]{:S(2)}, u32[]{:S(2)}) async-start(bf16[8,352,256]{2,1,0:T(8,128)(2,1)} %get-tuple-element.17), calls=%async_computation | async-start | bytes 2883584 | tf_op jit(solution)/shard_map/all_to_all | solution.py:244
  23.3 49.7 %all-gather = bf16[512,896]{1,0:T(8,128)(2,1)S(1)} all-gather(bf16[64,896]{1,0:T(8,128)(2,1)S(1)} %get-tuple-element.18), channel_id=2, replica_groups=mesh['z'=8,'core'=2,'y'=8,'x'=4] {'z'}, dimensions={0}, use_global_device_ids=true | all-gather | bytes 1032192 | tf_op jit(solution)/shard_map/all_gather | solution.py:245
  73.0 1.2 shard_map.103
  74.2 8.5 %all-to-all-start.1 = ((bf16[32,64,256]{2,1,0:T(8,128)(2,1)}), bf16[32,64,256]{2,1,0:T(8,128)(2,1)S(1)}, u32[]{:S(2)}, u32[]{:S(2)}) async-start(bf16[32,64,256]{2,1,0:T(8,128)(2,1)} %bitcast.5), calls=%async_computation.1 | async-start | bytes 2097152 | tf_op jit(solution)/shard_map/all_to_all | solution.py:260
  82.7 1.8 %shard_map.104.root = bf16[1024,1024]{1,0:T(8,128)(2,1)} custom-call(bf16[8,64,896]{2,1,0:T(8,128)(2,1)S(1)} %bitcast.16, bf16[8,352,256]{2,1,0:T(8,128)(2,1)S(1)} %all-to-all-done.parts), custom_call_target="tpu_custom_call" | custom-call | flops 1000000 | bytes 4000000 | tf_op jit(solution)/shard_map/pallas_call | solution.py:251
  84.5 8.3 %collective-permute-start.3 = (bf16[1024,1024]{1,0:T(8,128)(2,1)}, bf16[1024,1024]{1,0:T(8,128)(2,1)}, u32[]{:S(2)}, u32[]{:S(2)}) collective-permute-start(bf16[1024,1024]{1,0:T(8,128)(2,1)} %shard_map.104.root), channel_id=1, source_target_pairs={{0,32},{32,0},{1,33},{33,1},{2,34},{34,2},{3,35},{35,3},{4,36},{36... | collective-permute-start | bytes 6291464 | tf_op jit(solution)/shard_map/ppermute | solution.py:254
  92.8 10.4 %shard_map.105.fifth = bf16[1024,1024]{1,0:T(8,128)(2,1)} custom-call(bf16[1024,1024]{1,0:T(8,128)(2,1)} %shard_map.104.root), custom_call_target="tpu_custom_call" | custom-call | flops 6442450944 | bytes 4000000 | tf_op jit(solution)/shard_map/pallas_call | solution.py:255
  103.2 1.9 %collective-permute-start.2 = (bf16[1024,1024]{1,0:T(8,128)(2,1)}, bf16[1024,1024]{1,0:T(8,128)(2,1)}, u32[]{:S(2)}, u32[]{:S(2)}) collective-permute-start(bf16[1024,1024]{1,0:T(8,128)(2,1)} %shard_map.105.fifth), channel_id=1, source_target_pairs={{0,32},{32,0},{1,33},{33,1},{2,34},{34,2},{3,35},{35,3},{4,36},{36... | collective-permute-start | bytes 6291464 | tf_op jit(solution)/shard_map/ppermute | solution.py:259
  105.2 0.0 copy-start.4
  105.2 8.2 %collective-permute-start.1 = (bf16[4,512,256]{2,1,0:T(8,128)(2,1)S(1)}, bf16[4,512,256]{2,1,0:T(8,128)(2,1)S(1)}, u32[]{:S(2)}, u32[]{:S(2)}) collective-permute-start(bf16[4,512,256]{2,1,0:T(8,128)(2,1)S(1)} %bitcast.13), channel_id=1, source_target_pairs={{0,32},{32,0},{1,33},{33,1},{2,34},{34,2},{3,35},{35,3},{4,36},{36... | collective-permute-start | bytes 3145736 | tf_op jit(solution)/shard_map/ppermute | solution.py:263
  113.5 2.3 %collective-permute-done.1.other = bf16[4,512,256]{2,1,0:T(8,128)(2,1)S(1)} collective-permute-done((bf16[4,512,256]{2,1,0:T(8,128)(2,1)S(1)}, bf16[4,512,256]{2,1,0:T(8,128)(2,1)S(1)}, u32[]{:S(2)}, u32[]{:S(2)}) %collective-permute-start.1) | collective-permute-done | bytes 1048608 | tf_op jit(solution)/shard_map/ppermute | solution.py:263
  115.7 8.4 %shard_map.107 = bf16[4,64,256]{2,1,0:T(8,128)(2,1)} custom-call(s32[2]{0:T(128)S(1)} %pad_add_fusion.where, bf16[4,512,256]{2,1,0:T(8,128)(2,1)S(1)} %bitcast.14, bf16[4,512,256]{2,1,0:T(8,128)(2,1)S(1)} %collective-permute-done.1.other, bf16[1024,1024]{1,0:T(8,128)(2,1)} %shard_map.104.root, bf16[1024,1024]{1,0:T(8,128)(2,1)} %collective-permute-done.3.far_root), custom_call_target="tpu_custom_call" | custom-call | flops 4294967296 | bytes 6000000 | tf_op jit(solution)/shard_map/pallas_call | solution.py:265
  124.1 3.3 %all-to-all-start.2 = ((bf16[4,64,256]{2,1,0:T(8,128)(2,1)}), bf16[4,64,256]{2,1,0:T(8,128)(2,1)S(1)}, u32[]{:S(2)}, u32[]{:S(2)}) async-start(bf16[4,64,256]{2,1,0:T(8,128)(2,1)} %shard_map.107), calls=%async_computation.2 | async-start | bytes 262144 | tf_op jit(solution)/shard_map/all_to_all | solution.py:269
  127.4 5.5 %shard_map.106 = (f32[64,1024]{1,0:T(8,128)}, f32[64,1024]{1,0:T(8,128)}, f32[64,1024]{1,0:T(8,128)}, f32[64,1024]{1,0:T(8,128)}) custom-call(s32[2]{0:T(128)S(1)} %pad_add_fusion.where, bf16[4,512,256]{2,1,0:T(8,128)(2,1)S(1)} %bitcast.15, bf16[4,512,256]{2,1,0:T(8,128)(2,1)S(1)} %collective-permute-done.1.other, f32[64,1024]{1,0:T(8,128)S(1)} %bitcast.21, ...), custom_call_target="tpu_custom_call" | custom-call | flops 536870912 | bytes 8000000 | tf_op jit(solution)/shard_map/pallas_call | solution.py:271
  132.9 0.7 convert_element_type.3
  (16 shorter events, 0.0 us)
Async XLA Ops:
  0.7 1.2 copy-start
  1.9 0.9 copy-start.1
  2.9 0.9 copy-start.3
  3.8 0.8 copy-start.7
  5.6 10.6 %collective-permute-start = (bf16[128,2816]{1,0:T(8,128)(2,1)S(1)}, bf16[128,2816]{1,0:T(8,128)(2,1)S(1)}, u32[]{:S(2)}, u32[]{:S(2)}) collective-permute-start(bf16[128,2816]{1,0:T(8,128)(2,1)S(1)} %get-tuple-element.16), channel_id=1, source_target_pairs={{0,32},{32,0},{1,33},{33,1},{2,34},{34,2},{3,35},{35,3},{4,36},{36... | collective-permute-start | bytes 2162696 | tf_op jit(solution)/shard_map/ppermute | solution.py:234
  18.6 54.4 %all-to-all-start = ((bf16[8,352,256]{2,1,0:T(8,128)(2,1)}), bf16[8,352,256]{2,1,0:T(8,128)(2,1)S(1)}, u32[]{:S(2)}, u32[]{:S(2)}) async-start(bf16[8,352,256]{2,1,0:T(8,128)(2,1)} %get-tuple-element.17), calls=%async_computation | async-start | bytes 2883584 | tf_op jit(solution)/shard_map/all_to_all | solution.py:244
  74.2 31.0 %all-to-all-start.1 = ((bf16[32,64,256]{2,1,0:T(8,128)(2,1)}), bf16[32,64,256]{2,1,0:T(8,128)(2,1)S(1)}, u32[]{:S(2)}, u32[]{:S(2)}) async-start(bf16[32,64,256]{2,1,0:T(8,128)(2,1)} %bitcast.5), calls=%async_computation.1 | async-start | bytes 2097152 | tf_op jit(solution)/shard_map/all_to_all | solution.py:260
  84.5 29.0 %collective-permute-start.3 = (bf16[1024,1024]{1,0:T(8,128)(2,1)}, bf16[1024,1024]{1,0:T(8,128)(2,1)}, u32[]{:S(2)}, u32[]{:S(2)}) collective-permute-start(bf16[1024,1024]{1,0:T(8,128)(2,1)} %shard_map.104.root), channel_id=1, source_target_pairs={{0,32},{32,0},{1,33},{33,1},{2,34},{34,2},{3,35},{35,3},{4,36},{36... | collective-permute-start | bytes 6291464 | tf_op jit(solution)/shard_map/ppermute | solution.py:254
  103.2 24.1 %collective-permute-start.2 = (bf16[1024,1024]{1,0:T(8,128)(2,1)}, bf16[1024,1024]{1,0:T(8,128)(2,1)}, u32[]{:S(2)}, u32[]{:S(2)}) collective-permute-start(bf16[1024,1024]{1,0:T(8,128)(2,1)} %shard_map.105.fifth), channel_id=1, source_target_pairs={{0,32},{32,0},{1,33},{33,1},{2,34},{34,2},{3,35},{35,3},{4,36},{36... | collective-permute-start | bytes 6291464 | tf_op jit(solution)/shard_map/ppermute | solution.py:259
  105.2 22.2 %copy-start.2 = (f32[1,64,1024]{2,1,0:T(8,128)S(1)}, f32[1,64,1024]{2,1,0:T(8,128)}, u32[]{:S(2)}) copy-start(f32[1,64,1024]{2,1,0:T(8,128)} %param.10) | copy-start | bytes 786436
  105.2 22.2 %copy-start.4 = (f32[1,64,1024]{2,1,0:T(8,128)S(1)}, f32[1,64,1024]{2,1,0:T(8,128)}, u32[]{:S(2)}) copy-start(f32[1,64,1024]{2,1,0:T(8,128)} %param.11) | copy-start | bytes 786436
  105.2 22.2 %copy-start.5 = (f32[1,64,1024]{2,1,0:T(8,128)S(1)}, f32[1,64,1024]{2,1,0:T(8,128)}, u32[]{:S(2)}) copy-start(f32[1,64,1024]{2,1,0:T(8,128)} %param.8) | copy-start | bytes 786436
  105.2 22.2 %copy-start.6 = (f32[1,64,1024]{2,1,0:T(8,128)S(1)}, f32[1,64,1024]{2,1,0:T(8,128)}, u32[]{:S(2)}) copy-start(f32[1,64,1024]{2,1,0:T(8,128)} %param.9) | copy-start | bytes 786436
  105.2 10.5 %collective-permute-start.1 = (bf16[4,512,256]{2,1,0:T(8,128)(2,1)S(1)}, bf16[4,512,256]{2,1,0:T(8,128)(2,1)S(1)}, u32[]{:S(2)}, u32[]{:S(2)}) collective-permute-start(bf16[4,512,256]{2,1,0:T(8,128)(2,1)S(1)} %bitcast.13), channel_id=1, source_target_pairs={{0,32},{32,0},{1,33},{33,1},{2,34},{34,2},{3,35},{35,3},{4,36},{36... | collective-permute-start | bytes 3145736 | tf_op jit(solution)/shard_map/ppermute | solution.py:263
  124.1 8.9 %all-to-all-start.2 = ((bf16[4,64,256]{2,1,0:T(8,128)(2,1)}), bf16[4,64,256]{2,1,0:T(8,128)(2,1)S(1)}, u32[]{:S(2)}, u32[]{:S(2)}) async-start(bf16[4,64,256]{2,1,0:T(8,128)(2,1)} %shard_map.107), calls=%async_computation.2 | async-start | bytes 262144 | tf_op jit(solution)/shard_map/all_to_all | solution.py:269

commit v4 on v3

--- a/solution.py
+++ b/solution.py
@@ -21,16 +21,15 @@
 TILE = 512
 SIDE = NC * ROWS
 OFF = 3
-STRIP = OFF * 2 * SIDE + SIDE
 SLABS = NX * ROWS
-CHUNK = SLABS + ROWS + ROWS // 2
+CHUNK = SLABS + (OFF + 1) * ROWS + ROWS
 TOK = ("z", "core")
 HID = ("y", "x")
 SWAP = [(0, 1), (1, 0)]
 VMEM = pl.BlockSpec(memory_space=pltpu.VMEM)
-SMEM = pl.BlockSpec(memory_space=pltpu.SMEM)
+ANY = pl.BlockSpec(memory_space=pl.ANY)
 HBM = pl.BlockSpec(memory_space=pltpu.HBM)
-PARAMS = pltpu.CompilerParams(vmem_limit_bytes=48 * 1024 * 1024)
+PARAMS = pltpu.CompilerParams(vmem_limit_bytes=28 * 1024 * 1024)
 
 
 def dot(a, b, dims=((1,), (0,))):
@@ -49,12 +48,16 @@
     )
 
 
+def in_hbm(value):
+    return pltpu.with_memory_space_constraint(value, pltpu.HBM)
+
+
 def at(start, size, unit):
     return pl.ds(pl.multiple_of(start, unit), size)
 
 
-def pack_kernel(where, act, cot, left_root, right_root, own, far, roots, sems):
-    core = where[1]
+def pack_kernel(act, cot, left_root, right_root, own, far, roots, sems):
+    core = lax.axis_index("core")
     copies = []
     for k, (out, side) in enumerate(((far, 1 - core), (own, core))):
         for r in range(NX):
@@ -74,8 +77,8 @@
         out[ROWS:, ROOT:] = low[:, HALF:]
 
 
-def partial_kernel(where, own, more, out, strip, shard):
-    z, core = where[0], where[1]
+def partial_kernel(own, more, out, shard):
+    z, core = lax.axis_index("z"), lax.axis_index("core")
     for r in range(NX):
         cols = slice(r * HALF, (r + 1) * HALF)
         total = dot(own[:, cols], own[:, COT : COT + WIDTH], ((0,), (0,)))
@@ -91,17 +94,11 @@
     def block(k):
         return shard[:, at(lax.rem(z + k, NZ) * SIDE, SIDE, SIDE)]
 
-    for k in range(1, OFF + 1):
-        piece, first = block(k), (k - 1) * 2 * SIDE
-        strip[:, first : first + SIDE] = piece[:ROWS]
-        strip[:, first + SIDE : first + 2 * SIDE] = piece[ROWS:]
-    middle, across = block(0), block(OFF + 1)
-    strip[:, OFF * 2 * SIDE :] = across[:ROWS]
-    for to in range(NZ):
-        out[to, SLABS : SLABS + ROWS, :SIDE] = middle[:ROWS]
-        out[to, SLABS : SLABS + ROWS, SIDE:] = middle[ROWS:]
-        out[to, SLABS + ROWS :, :SIDE] = across[ROWS : ROWS + ROWS // 2]
-        out[to, SLABS + ROWS :, SIDE:] = across[ROWS + ROWS // 2 :]
+    for k in range(OFF + 2):
+        piece, first = block(k), SLABS + k * ROWS
+        for to in range(NZ):
+            out[to, first : first + ROWS, :SIDE] = piece[:ROWS]
+            out[to, first : first + ROWS, SIDE:] = piece[ROWS:]
 
 
 def sum_kernel(parts, out):
@@ -115,31 +112,22 @@
             out[x, z] = low
 
 
-def root_kernel(strips, parts, root):
+def root_kernel(parts, root):
     for z in range(NZ):
-        top, low = slice(z * SIDE, z * SIDE + ROWS), slice(z * SIDE + ROWS, (z + 1) * SIDE)
         own = slice(z * SIDE, (z + 1) * SIDE)
-        root[top, own] = parts[z, SLABS : SLABS + ROWS, :SIDE]
-        root[low, own] = parts[z, SLABS : SLABS + ROWS, SIDE:]
-        for k in range(1, OFF + 1):
-            j, first = (z + k) % NZ, (k - 1) * 2 * SIDE
+        for k in range(OFF + 2):
+            j, first = (z + k) % NZ, SLABS + k * ROWS
+            there = slice(j * SIDE, (j + 1) * SIDE)
             piece = jnp.concatenate(
-                [strips[z, :, first : first + SIDE], strips[z, :, first + SIDE : first + 2 * SIDE]],
-                axis=0,
+                [parts[z, first : first + ROWS, :SIDE], parts[z, first : first + ROWS, SIDE:]], axis=0
             )
-            there = slice(j * SIDE, (j + 1) * SIDE)
             root[own, there] = piece
-            root[there, own] = piece.T
-        j = (z + OFF + 1) % NZ
-        there = slice(j * SIDE, (j + 1) * SIDE)
-        half = z * SIDE + ROWS + ROWS // 2
-        root[top, there] = strips[z, :, OFF * 2 * SIDE :]
-        root[z * SIDE + ROWS : half, there] = parts[z, SLABS + ROWS :, :SIDE]
-        root[half : (z + 1) * SIDE, there] = parts[z, SLABS + ROWS :, SIDE:]
-
-
-def precond_kernel(where, mine, other, root, far_root, out, kept):
-    z, core = where[0], where[1]
+            if 0 < k <= OFF:
+                root[there, own] = piece.T
+
+
+def precond_kernel(mine, other, root, far_root, out, kept):
+    z, core = lax.axis_index("z"), lax.axis_index("core")
     place = (z * NC + core) * ROWS
 
     def run(left, right, upper, lower):
@@ -188,34 +176,42 @@
 
 
 def factor_kernel(
-    where, mine, other, left_gram, right_gram, left_root, right_root, fifth, far_fifth,
-    left_next, right_next, left_refined, right_refined, whole, columns, old, sems,
+    mine, other, left_gram, right_gram, left_root, right_root, fifth, far_fifth,
+    left_next, right_next, left_refined, right_refined, whole, columns, old, powers, sems,
 ):
-    z, core = where[0], where[1]
+    z, core = lax.axis_index("z"), lax.axis_index("core")
     even = core == 0
-    copies = [
-        pltpu.make_async_copy(source, old.at[k], sems.at[k])
+    pieces = []
+    for k, (half, side) in enumerate(((mine, core), (other, 1 - core))):
+        for x in range(NX):
+            target = whole.at[at(side * HALF, HALF, HALF), pl.ds(x * WIDTH, WIDTH)]
+            pieces.append(pltpu.make_async_copy(half.at[x], target, sems.at[k, x]))
+    olds = [
+        pltpu.make_async_copy(source, old.at[k], sems.at[2, k])
         for k, source in enumerate((left_gram, right_gram, left_root, right_root))
     ]
-    for copy in copies:
+    both = [
+        pltpu.make_async_copy(source, powers.at[k], sems.at[3, k])
+        for k, source in enumerate((fifth, far_fifth))
+    ]
+    for copy in pieces + olds + both:
         copy.start()
-    for x in range(NX):
-        whole[at(core * HALF, HALF, HALF), x * WIDTH : (x + 1) * WIDTH] = mine[x]
-        whole[at((1 - core) * HALF, HALF, HALF), x * WIDTH : (x + 1) * WIDTH] = other[x]
+    for copy in pieces:
+        copy.wait()
     slab = whole[:, at(z * SIDE, SIDE, SIDE)]
     columns[...] = slab.astype(F32).T
     rows = whole[at((z * NC + core) * ROWS, ROWS, ROWS)]
     left = dot(rows, whole[...], ((1,), (1,)))
     turned = columns[at(core * ROWS, ROWS, ROWS)].astype(BF16)
     right = dot(turned, whole[...])
-    for copy in copies:
+    for copy in olds + both:
         copy.wait()
     left = BETA * old[0] + left
     left_next[...] = left
     right = BETA * old[1] + right
     right_next[...] = right
-    own = dot(jnp.where(even, left, right).astype(BF16), fifth[...])
-    far = dot(jnp.where(even, right, left).astype(BF16), far_fifth[...])
+    own = dot(jnp.where(even, left, right).astype(BF16), powers[0])
+    far = dot(jnp.where(even, right, left).astype(BF16), powers[1])
     left_refined[...] = (5.0 * old[2] - jnp.where(even, own, far)) / 4.0
     right_refined[...] = (5.0 * old[3] - jnp.where(even, far, own)) / 4.0
 
@@ -223,34 +219,27 @@
 def on_device(activations, cotangent, left_gram, right_gram, left_root, right_root):
     left_gram, right_gram = left_gram[0], right_gram[0]
     left_root, right_root = left_root[0], right_root[0]
-    where = jnp.stack([lax.axis_index("z"), lax.axis_index("core")]).astype(jnp.int32)
 
     half = jax.ShapeDtypeStruct((TOKENS, ROOT + HALF), BF16)
     own, far = call(
-        pack_kernel, (half, half), [SMEM] + [HBM] * 4,
+        pack_kernel, (half, half), [HBM] * 4,
         scratch=[pltpu.VMEM((2, ROWS, BS), F32), pltpu.SemaphoreType.DMA((2, NX + 2))],
         flops=100_000, moved=1_500_000,
-    )(where, activations, cotangent, left_root, right_root)
+    )(*map(in_hbm, (activations, cotangent, left_root, right_root)))
     more = lax.ppermute(far, "core", SWAP)
-    partial, strip = call(
-        partial_kernel,
-        (
-            jax.ShapeDtypeStruct((NZ, CHUNK, WIDTH), BF16),
-            jax.ShapeDtypeStruct((ROWS, STRIP), BF16),
-        ),
-        [SMEM, VMEM, VMEM], scratch=[pltpu.VMEM((SIDE, BS), BF16)],
+    partial = call(
+        partial_kernel, jax.ShapeDtypeStruct((NZ, CHUNK, WIDTH), BF16),
+        [VMEM, VMEM], scratch=[pltpu.VMEM((SIDE, BS), BF16)],
         flops=2 * 256 * 2048 * 256, moved=3_000_000,
-    )(where, own, more)
+    )(own, more)
     parts = lax.all_to_all(partial, "z", 0, 0, tiled=True)
-    strips = lax.all_gather(strip, "z", axis=0)
-    parts, strips = lax.optimization_barrier((parts, strips))
     copies = call(
         sum_kernel, jax.ShapeDtypeStruct((NX, NZ, ROWS, WIDTH), BF16), [VMEM],
         flops=1_000_000, moved=2_000_000,
     )(parts)
     root = call(
-        root_kernel, jax.ShapeDtypeStruct((BS, BS), BF16), [VMEM, VMEM], flops=1_000_000, moved=4_000_000
-    )(strips, parts)
+        root_kernel, jax.ShapeDtypeStruct((BS, BS), BF16), [VMEM], flops=1_000_000, moved=4_000_000
+    )(parts)
     far_root = lax.ppermute(root, "core", SWAP)
     fifth = call(
         power_kernel, jax.ShapeDtypeStruct((BS, BS), BF16), [VMEM],
@@ -263,21 +252,22 @@
     other = lax.ppermute(mine, "core", SWAP)
 
     precond = call(
-        precond_kernel, jax.ShapeDtypeStruct((NX, ROWS, WIDTH), BF16), [SMEM] + [VMEM] * 4,
+        precond_kernel, jax.ShapeDtypeStruct((NX, ROWS, WIDTH), BF16), [VMEM] * 4,
         scratch=[pltpu.VMEM((TILE, BS), F32)], flops=4 * BS**3, moved=6_000_000,
-    )(where, mine, other, root, far_root)
+    )(in_hbm(mine), in_hbm(other), root, far_root)
     arrived = lax.all_to_all(precond, "x", 0, 0, tiled=True)
     shape = jax.ShapeDtypeStruct((ROWS, BS), F32)
     outs = call(
-        factor_kernel, (shape,) * 4, [SMEM, VMEM, VMEM] + [HBM] * 4 + [VMEM] * 2,
+        factor_kernel, (shape,) * 4, [ANY] * 2 + [HBM] * 4 + [ANY] * 2,
         scratch=[
             pltpu.VMEM((BS, BS), BF16),
             pltpu.VMEM((SIDE, BS), F32),
             pltpu.VMEM((4, ROWS, BS), F32),
-            pltpu.SemaphoreType.DMA((4,)),
+            pltpu.VMEM((2, BS, BS), BF16),
+            pltpu.SemaphoreType.DMA((4, 4)),
         ],
         flops=8 * 64 * 1024 * 1024, moved=8_000_000,
-    )(where, mine, other, left_gram, right_gram, left_root, right_root, fifth, far_fifth)
+    )(in_hbm(mine), in_hbm(other), *map(in_hbm, (left_gram, right_gram, left_root, right_root)), fifth, far_fifth)
     return (*(o[None] for o in outs), arrived.astype(F32))
 
 

time: 134 us -> 134 us (level)
  starting transfers between devices: 43.8 us -> 29.4 us
  blocking collectives: 49.7 us -> 60.5 us
  waiting for transfers between devices: 4.06 us -> 12.7 us
  local copies, waits for them, and re-layouts: 3.99 us -> 1.02 us
  Pallas kernels: 30.5 us -> 27.9 us
    all_to_all x0 -> x1, blocking collectives: none -> 60.5 us  [on_device(): parts = lax.all_to_all(partial, 'z', 0, 0, tiled=True)]
    all_gather x1 -> x0, blocking collectives: 49.7 us -> none  [on_device(): strips = lax.all_gather(strip, 'z', axis=0)]
    all_to_all x1, waiting for transfers between devices: 0.01 us -> 8.35 us  [on_device(): lax.all_to_all(copies.reshape(NX * NZ, ROWS, WIDTH), ('x', 'z'), 0, 0, ti...]
    ppermute x1, starting transfers between devices: 8.33 us -> 3.51 us  [on_device(): far_root = lax.ppermute(root, 'core', SWAP)]
    all_to_all x1 -> x0, starting transfers between devices: 4.66 us -> none  [on_device(): parts = lax.all_to_all(partial, 'z', 0, 0, tiled=True)]
    all_to_all x1, starting transfers between devices: 8.54 us -> 4.81 us  [on_device(): lax.all_to_all(copies.reshape(NX * NZ, ROWS, WIDTH), ('x', 'z'), 0, 0, ti...]
    unnamed x16 -> x4, local copies, waits for them, and re-layouts: 3.99 us -> 1.02 us
  transfers between devices with their start and end apart: 7 -> 6, of which waited for: 2 -> 4; matrix products, arithmetic and copies ran while one was open for 0% -> 0% of each run, Pallas kernels for 19% -> 18%
where the time goes in v4:
time: 134 us; the launch traced here: 133 us
  blocking collectives  60.5 us (45%)
  starting transfers between devices  29.4 us (22%)
  Pallas kernels  27.9 us (21%)
  waiting for transfers between devices  12.7 us (9%)
    all_to_all x1, blocking collectives, on_device(): parts = lax.all_to_all(partial, 'z', 0, 0, tiled=True)  60.5 us
    pallas_call x1, Pallas kernels, on_device(): call(power_kernel, jax.ShapeDtypeStruct((BS, BS), BF16), [VMEM], scratch=...  9.1 us
    pallas_call x1, Pallas kernels, on_device(): call(precond_kernel, jax.ShapeDtypeStruct((NX, ROWS, WIDTH), BF16), [VMEM...  8.98 us
    ppermute x1, starting transfers between devices, on_device(): more = lax.ppermute(far, 'core', SWAP)  8.79 us
    all_to_all x1, waiting for transfers between devices, on_device(): lax.all_to_all(copies.reshape(NX * NZ, ROWS, WIDTH), ('x', 'z'), 0, 0, ti...  8.35 us
    ppermute x1, starting transfers between devices, on_device(): other = lax.ppermute(mine, 'core', SWAP)  7.01 us
    all_to_all x1, starting transfers between devices, on_device(): lax.all_to_all(copies.reshape(NX * NZ, ROWS, WIDTH), ('x', 'z'), 0, 0, ti...  4.81 us
    pallas_call x1, Pallas kernels, on_device(): call(factor_kernel, (shape,) * 4, [ANY] * 2 + [HBM] * 4 + [ANY] * 2, scra...  4.44 us
  transfers between devices with their start and end apart: 6, of which 4 were waited for; matrix products, arithmetic and copies ran while one was open for 0% of the time, Pallas kernels for 18%

profile of v4, /device:TPU:1, one launch (start us, length us, event | category | flops | bytes accessed | tf_op | source)
XLA Modules:
  0.0 133.0 jit_solution(12582404529332128019)
XLA Ops:
  0.6 1.6 %shard_map.101 = (bf16[128,2816]{1,0:T(8,128)(2,1)S(1)}, bf16[128,2816]{1,0:T(8,128)(2,1)S(1)}) custom-call(bf16[128,4096]{1,0:T(8,128)(2,1)} %act.1, bf16[128,256]{1,0:T(8,128)(2,1)} %cot.1, f32[64,1024]{1,0:T(8,128)} %bitcast.13, f32[64,1024]{1,0:T(8,128)} %bitcast.15), custom_call_target="tpu_custom_call" | custom-call | flops 100000 | bytes 1500000 | tf_op jit(solution)/shard_map/pallas_call | solution.py:224
  2.3 8.8 %collective-permute-start = (bf16[128,2816]{1,0:T(8,128)(2,1)S(1)}, bf16[128,2816]{1,0:T(8,128)(2,1)S(1)}, u32[]{:S(2)}, u32[]{:S(2)}) collective-permute-start(bf16[128,2816]{1,0:T(8,128)(2,1)S(1)} %get-tuple-element.12), channel_id=1, source_target_pairs={{0,32},{32,0},{1,33},{33,1},{2,34},{34,2},{3,35},{35,3},{4,36},{36... | collective-permute-start | bytes 2162696 | tf_op jit(solution)/shard_map/ppermute | solution.py:229
  11.1 1.8 %collective-permute-done.more = bf16[128,2816]{1,0:T(8,128)(2,1)S(1)} collective-permute-done((bf16[128,2816]{1,0:T(8,128)(2,1)S(1)}, bf16[128,2816]{1,0:T(8,128)(2,1)S(1)}, u32[]{:S(2)}, u32[]{:S(2)}) %collective-permute-start) | collective-permute-done | bytes 720928 | tf_op jit(solution)/shard_map/ppermute | solution.py:229
  12.9 0.9 shard_map.102
  13.7 60.5 %all_to_all.15.parts = bf16[8,576,256]{2,1,0:T(8,128)(2,1)S(1)} all-to-all(bf16[8,576,256]{2,1,0:T(8,128)(2,1)S(1)} %shard_map.102), channel_id=1, replica_groups=mesh['z'=8,'core'=2,'y'=8,'x'=4] {'z'}, dimensions={0} | all-to-all | bytes 4718592 | tf_op jit(solution)/shard_map/all_to_all | solution.py:235
  74.2 1.1 shard_map.103
  75.4 4.8 %all-to-all-start.1 = ((bf16[32,64,256]{2,1,0:T(8,128)(2,1)}), bf16[32,64,256]{2,1,0:T(8,128)(2,1)S(1)}, u32[]{:S(2)}, u32[]{:S(2)}) async-start(bf16[32,64,256]{2,1,0:T(8,128)(2,1)} %bitcast.2), calls=%async_computation.1 | async-start | bytes 2097152 | tf_op jit(solution)/shard_map/all_to_all | solution.py:249
  80.2 1.8 %shard_map.104.root = bf16[1024,1024]{1,0:T(8,128)(2,1)} custom-call(bf16[8,576,256]{2,1,0:T(8,128)(2,1)S(1)} %all_to_all.15.parts), custom_call_target="tpu_custom_call" | custom-call | flops 1000000 | bytes 4000000 | tf_op jit(solution)/shard_map/pallas_call | solution.py:240
  82.0 3.5 %collective-permute-start.3 = (bf16[1024,1024]{1,0:T(8,128)(2,1)}, bf16[1024,1024]{1,0:T(8,128)(2,1)}, u32[]{:S(2)}, u32[]{:S(2)}) collective-permute-start(bf16[1024,1024]{1,0:T(8,128)(2,1)} %shard_map.104.root), channel_id=1, source_target_pairs={{0,32},{32,0},{1,33},{33,1},{2,34},{34,2},{3,35},{35,3},{4,36},{36... | collective-permute-start | bytes 6291464 | tf_op jit(solution)/shard_map/ppermute | solution.py:243
  85.5 9.1 %shard_map.105.fifth = bf16[1024,1024]{1,0:T(8,128)(2,1)S(1)} custom-call(bf16[1024,1024]{1,0:T(8,128)(2,1)} %shard_map.104.root), custom_call_target="tpu_custom_call" | custom-call | flops 6442450944 | bytes 4000000 | tf_op jit(solution)/shard_map/pallas_call | solution.py:244
  94.6 1.9 %collective-permute-start.2 = (bf16[1024,1024]{1,0:T(8,128)(2,1)S(1)}, bf16[1024,1024]{1,0:T(8,128)(2,1)}, u32[]{:S(2)}, u32[]{:S(2)}) collective-permute-start(bf16[1024,1024]{1,0:T(8,128)(2,1)S(1)} %shard_map.105.fifth), channel_id=1, source_target_pairs={{0,32},{32,0},{1,33},{33,1},{2,34},{34,2},{3,35},{35,3},{4,36},{36... | collective-permute-start | bytes 6291464 | tf_op jit(solution)/shard_map/ppermute | solution.py:248
  96.5 8.3 %all-to-all-done.1 = bf16[32,64,256]{2,1,0:T(8,128)(2,1)S(1)} async-done(((bf16[32,64,256]{2,1,0:T(8,128)(2,1)}), bf16[32,64,256]{2,1,0:T(8,128)(2,1)S(1)}, u32[]{:S(2)}, u32[]{:S(2)}) %all-to-all-start.1) | async-done | bytes 1048608 | tf_op jit(solution)/shard_map/all_to_all | solution.py:249
  104.9 0.0 copy-start
  104.9 7.0 %collective-permute-start.1 = (bf16[4,512,256]{2,1,0:T(8,128)(2,1)S(1)}, bf16[4,512,256]{2,1,0:T(8,128)(2,1)S(1)}, u32[]{:S(2)}, u32[]{:S(2)}) collective-permute-start(bf16[4,512,256]{2,1,0:T(8,128)(2,1)S(1)} %bitcast.10), channel_id=1, source_target_pairs={{0,32},{32,0},{1,33},{33,1},{2,34},{34,2},{3,35},{35,3},{4,36},{36... | collective-permute-start | bytes 3145736 | tf_op jit(solution)/shard_map/ppermute | solution.py:252
  111.9 0.0 collective-permute-done.3.far_root
  111.9 2.3 %collective-permute-done.1.other = bf16[4,512,256]{2,1,0:T(8,128)(2,1)S(1)} collective-permute-done((bf16[4,512,256]{2,1,0:T(8,128)(2,1)S(1)}, bf16[4,512,256]{2,1,0:T(8,128)(2,1)S(1)}, u32[]{:S(2)}, u32[]{:S(2)}) %collective-permute-start.1) | collective-permute-done | bytes 1048608 | tf_op jit(solution)/shard_map/ppermute | solution.py:252
  114.1 0.0 copy-done
  114.1 1.0 copy-done.1
  115.2 9.0 %shard_map.107 = bf16[4,64,256]{2,1,0:T(8,128)(2,1)} custom-call(bf16[4,512,256]{2,1,0:T(8,128)(2,1)} %bitcast.11, bf16[4,512,256]{2,1,0:T(8,128)(2,1)} %copy-done.1, bf16[1024,1024]{1,0:T(8,128)(2,1)} %shard_map.104.root, bf16[1024,1024]{1,0:T(8,128)(2,1)} %collective-permute-done.3.far_root), custom_call_target="tpu_custom_call" | custom-call | flops 4294967296 | bytes 6000000 | tf_op jit(solution)/shard_map/pallas_call | solution.py:254
  124.1 3.3 %all-to-all-start.2 = ((bf16[4,64,256]{2,1,0:T(8,128)(2,1)}), bf16[4,64,256]{2,1,0:T(8,128)(2,1)S(1)}, u32[]{:S(2)}, u32[]{:S(2)}) async-start(bf16[4,64,256]{2,1,0:T(8,128)(2,1)} %shard_map.107), calls=%async_computation.2 | async-start | bytes 262144 | tf_op jit(solution)/shard_map/all_to_all | solution.py:258
  127.5 0.0 collective-permute-done.2.far_fifth
  127.5 4.4 %shard_map.106 = (f32[64,1024]{1,0:T(8,128)}, f32[64,1024]{1,0:T(8,128)}, f32[64,1024]{1,0:T(8,128)}, f32[64,1024]{1,0:T(8,128)}) custom-call(bf16[4,512,256]{2,1,0:T(8,128)(2,1)} %bitcast.12, bf16[4,512,256]{2,1,0:T(8,128)(2,1)} %copy-done.1, f32[64,1024]{1,0:T(8,128)} %bitcast.17, f32[64,1024]{1,0:T(8,128)} %bitcast.18, f32[64,1024]{1,0:T(8,128)} %bitcast.14, ...), custom_call_target="tpu_custom_call" | custom-call | flops 536870912 | bytes 8000000 | tf_op jit(solution)/shard_map/pallas_call | solution.py:260
  131.9 0.3 all-to-all-done.2
  132.3 0.7 convert_element_type.3
  (1 shorter events, 0.0 us)
Async XLA Ops:
  2.3 10.6 %collective-permute-start = (bf16[128,2816]{1,0:T(8,128)(2,1)S(1)}, bf16[128,2816]{1,0:T(8,128)(2,1)S(1)}, u32[]{:S(2)}, u32[]{:S(2)}) collective-permute-start(bf16[128,2816]{1,0:T(8,128)(2,1)S(1)} %get-tuple-element.12), channel_id=1, source_target_pairs={{0,32},{32,0},{1,33},{33,1},{2,34},{34,2},{3,35},{35,3},{4,36},{36... | collective-permute-start | bytes 2162696 | tf_op jit(solution)/shard_map/ppermute | solution.py:229
  75.4 29.5 %all-to-all-start.1 = ((bf16[32,64,256]{2,1,0:T(8,128)(2,1)}), bf16[32,64,256]{2,1,0:T(8,128)(2,1)S(1)}, u32[]{:S(2)}, u32[]{:S(2)}) async-start(bf16[32,64,256]{2,1,0:T(8,128)(2,1)} %bitcast.2), calls=%async_computation.1 | async-start | bytes 2097152 | tf_op jit(solution)/shard_map/all_to_all | solution.py:249
  82.0 29.9 %collective-permute-start.3 = (bf16[1024,1024]{1,0:T(8,128)(2,1)}, bf16[1024,1024]{1,0:T(8,128)(2,1)}, u32[]{:S(2)}, u32[]{:S(2)}) collective-permute-start(bf16[1024,1024]{1,0:T(8,128)(2,1)} %shard_map.104.root), channel_id=1, source_target_pairs={{0,32},{32,0},{1,33},{33,1},{2,34},{34,2},{3,35},{35,3},{4,36},{36... | collective-permute-start | bytes 6291464 | tf_op jit(solution)/shard_map/ppermute | solution.py:243
  94.6 32.9 %collective-permute-start.2 = (bf16[1024,1024]{1,0:T(8,128)(2,1)S(1)}, bf16[1024,1024]{1,0:T(8,128)(2,1)}, u32[]{:S(2)}, u32[]{:S(2)}) collective-permute-start(bf16[1024,1024]{1,0:T(8,128)(2,1)S(1)} %shard_map.105.fifth), channel_id=1, source_target_pairs={{0,32},{32,0},{1,33},{33,1},{2,34},{34,2},{3,35},{35,3},{4,36},{36... | collective-permute-start | bytes 6291464 | tf_op jit(solution)/shard_map/ppermute | solution.py:248
  104.9 9.3 %copy-start = (bf16[32,64,256]{2,1,0:T(8,128)(2,1)}, bf16[32,64,256]{2,1,0:T(8,128)(2,1)S(1)}, u32[]{:S(2)}) copy-start(bf16[32,64,256]{2,1,0:T(8,128)(2,1)S(1)} %all-to-all-done.1) | copy-start | bytes 3145732
  104.9 9.3 %collective-permute-start.1 = (bf16[4,512,256]{2,1,0:T(8,128)(2,1)S(1)}, bf16[4,512,256]{2,1,0:T(8,128)(2,1)S(1)}, u32[]{:S(2)}, u32[]{:S(2)}) collective-permute-start(bf16[4,512,256]{2,1,0:T(8,128)(2,1)S(1)} %bitcast.10), channel_id=1, source_target_pairs={{0,32},{32,0},{1,33},{33,1},{2,34},{34,2},{3,35},{35,3},{4,36},{36... | collective-permute-start | bytes 3145736 | tf_op jit(solution)/shard_map/ppermute | solution.py:252
  114.1 1.0 copy-start.1
  124.1 8.1 %all-to-all-start.2 = ((bf16[4,64,256]{2,1,0:T(8,128)(2,1)}), bf16[4,64,256]{2,1,0:T(8,128)(2,1)S(1)}, u32[]{:S(2)}, u32[]{:S(2)}) async-start(bf16[4,64,256]{2,1,0:T(8,128)(2,1)} %shard_map.107), calls=%async_computation.2 | async-start | bytes 262144 | tf_op jit(solution)/shard_map/all_to_all | solution.py:258

commit v5 on v4

v5 whole, which is shorter than its diff:
```python
import jax
import jax.numpy as jnp
from jax import lax
from jax.experimental import pallas as pl
from jax.experimental.pallas import tpu as pltpu
from jax.sharding import Mesh
from jax.sharding import PartitionSpec as P

BETA = 0.95
EPS = 1e-06
F32 = jnp.float32
BF16 = jnp.bfloat16
NZ, NC, NY, NX = 8, 2, 8, 4
BS = 1024
HALF = BS // NC
TOKENS = 128
ROWS = BS // (NZ * NC)
WIDTH = BS // NX
COT = NX * HALF
ROOT = COT + WIDTH
TILE = 512
SIDE = NC * ROWS
OFF = 3
SLABS = NX * ROWS
STRIP = (OFF + 2) * SIDE
TOK = ("z", "core")
HID = ("y", "x")
SWAP = [(0, 1), (1, 0)]
VMEM = pl.BlockSpec(memory_space=pltpu.VMEM)
ANY = pl.BlockSpec(memory_space=pl.ANY)
HBM = pl.BlockSpec(memory_space=pltpu.HBM)
PARAMS = pltpu.CompilerParams(vmem_limit_bytes=28 * 1024 * 1024)


def dot(a, b, dims=((1,), (0,))):
    return lax.dot_general(a, b, (dims, ((), ())), preferred_element_type=F32)


def call(body, outs, specs, scratch=(), flops=0, moved=0, places=None):
    return pl.pallas_call(
        body,
        out_shape=outs,
        in_specs=specs,
        out_specs=places or jax.tree.map(lambda _: VMEM, outs),
        scratch_shapes=list(scratch),
        compiler_params=PARAMS,
        cost_estimate=pl.CostEstimate(flops=flops, bytes_accessed=moved, transcendentals=0),
    )


def in_hbm(value):
    return pltpu.with_memory_space_constraint(value, pltpu.HBM)


def at(start, size, unit):
    return pl.ds(pl.multiple_of(start, unit), size)


def pack_kernel(act, cot, left_root, right_root, own, far, roots, sems):
    core = lax.axis_index("core")
    copies = []
    for k, (out, side) in enumerate(((far, 1 - core), (own, core))):
        for r in range(NX):
            source = act.at[:, at(r * BS + side * HALF, HALF, 128)]
            target = out.at[:, pl.ds(r * HALF, HALF)]
            copies.append(pltpu.make_async_copy(source, target, sems.at[k, r]))
        copies.append(pltpu.make_async_copy(cot, out.at[:, pl.ds(COT, WIDTH)], sems.at[k, NX]))
    copies.append(pltpu.make_async_copy(left_root, roots.at[0], sems.at[0, NX + 1]))
    copies.append(pltpu.make_async_copy(right_root, roots.at[1], sems.at[1, NX + 1]))
    for copy in copies:
        copy.start()
    for copy in copies:
        copy.wait()
    for out, side in ((far, 1 - core), (own, core)):
        low = roots[side].astype(BF16)
        out[:ROWS, ROOT:] = low[:, :HALF]
        out[ROWS:, ROOT:] = low[:, HALF:]


def strip_kernel(own, more, strip, shard):
    z, core = lax.axis_index("z"), lax.axis_index("core")
    for given, side in ((own, core), (more, 1 - core)):
        rows = at(side * ROWS, ROWS, ROWS)
        shard[rows, :HALF] = given[:ROWS, ROOT:]
        shard[rows, HALF:] = given[ROWS:, ROOT:]
    for k in range(OFF + 2):
        strip[:, k * SIDE : (k + 1) * SIDE] = shard[:, at(lax.rem(z + k, NZ) * SIDE, SIDE, SIDE)]


def partial_kernel(own, more, out):
    for r in range(NX):
        cols = slice(r * HALF, (r + 1) * HALF)
        total = dot(own[:, cols], own[:, COT : COT + WIDTH], ((0,), (0,)))
        total += dot(more[:, cols], more[:, COT : COT + WIDTH], ((0,), (0,)))
        low = total.astype(BF16)
        for to in range(NZ):
            out[to, r * ROWS : (r + 1) * ROWS] = low[to * ROWS : (to + 1) * ROWS]


def sum_kernel(parts, out):
    for x in range(NX):
        rows = slice(x * ROWS, (x + 1) * ROWS)
        total = parts[0, rows].astype(F32)
        for z in range(1, NZ):
            total += parts[z, rows].astype(F32)
        low = total.astype(BF16)
        for z in range(NZ):
            out[x, z] = low


def root_kernel(strips, root):
    for z in range(NZ):
        own = slice(z * SIDE, (z + 1) * SIDE)
        for k in range(OFF + 2):
            j = (z + k) % NZ
            there = slice(j * SIDE, (j + 1) * SIDE)
            piece = strips[own, k * SIDE : (k + 1) * SIDE]
            root[own, there] = piece
            if 0 < k <= OFF:
                root[there, own] = piece.T


def precond_kernel(mine, other, root, far_root, out, stored, whole, left, right, kept, sems):
    z, core = lax.axis_index("z"), lax.axis_index("core")
    place = (z * NC + core) * ROWS

    def bring(first, second):
        return [
            pltpu.make_async_copy(first, left, sems.at[2, 0]),
            pltpu.make_async_copy(second, right, sems.at[2, 1]),
        ]

    pieces = []
    for k, (half, side) in enumerate(((mine, core), (other, 1 - core))):
        for x in range(NX):
            target = whole.at[at(side * HALF, HALF, HALF), pl.ds(x * WIDTH, WIDTH)]
            pieces.append(pltpu.make_async_copy(half.at[x], target, sems.at[k, x]))
    for copy in pieces:
        copy.start()

    @pl.when(core == 0)
    def _():
        for copy in bring(root, far_root):
            copy.start()

    @pl.when(core == 1)
    def _():
        for copy in bring(far_root, root):
            copy.start()

    for copy in pieces + bring(root, far_root):
        copy.wait()
    store = pltpu.make_async_copy(whole, stored, sems.at[2, 2])
    store.start()

    def tile(i, total):
        rows = at(i * TILE, TILE, TILE)
        precond = dot(dot(left[rows], whole[...]).astype(BF16), right[...])

        @pl.when(i == place // TILE)
        def _():
            kept[...] = precond

        return total + jnp.sum(precond * precond, axis=0, keepdims=True)

    total = lax.fori_loop(0, BS // TILE, tile, jnp.zeros((1, BS), F32))
    scale = 1.0 / jnp.sqrt(jnp.sum(total) / (BS * BS) + EPS)
    scaled = kept[at(place % TILE, ROWS, ROWS)] * scale
    for x in range(NX):
        out[x] = scaled[:, x * WIDTH : (x + 1) * WIDTH].astype(BF16)
    store.wait()


def factor_kernel(
    stored, left_gram, right_gram, left_root, right_root, root, far_root,
    left_next, right_next, left_refined, right_refined, whole, columns, old, powers, sems,
):
    z, core = lax.axis_index("z"), lax.axis_index("core")
    even = core == 0
    olds = [
        pltpu.make_async_copy(source, old.at[k], sems.at[0, k])
        for k, source in enumerate((left_gram, right_gram, left_root, right_root))
    ]
    both = [
        pltpu.make_async_copy(source, powers.at[k], sems.at[1, k])
        for k, source in enumerate((root, far_root))
    ]
    load = pltpu.make_async_copy(stored, whole, sems.at[2, 0])
    for copy in [load] + olds + both:
        copy.start()
    load.wait()
    slab = whole[:, at(z * SIDE, SIDE, SIDE)]
    columns[...] = slab.astype(F32).T
    rows = whole[at((z * NC + core) * ROWS, ROWS, ROWS)]
    left = dot(rows, whole[...], ((1,), (1,)))
    turned = columns[at(core * ROWS, ROWS, ROWS)].astype(BF16)
    right = dot(turned, whole[...])
    for copy in olds + both:
        copy.wait()
    left = BETA * old[0] + left
    left_next[...] = left
    right = BETA * old[1] + right
    right_next[...] = right
    own, far = jnp.where(even, left, right), jnp.where(even, right, left)
    for _ in range(5):
        own, far = dot(own.astype(BF16), powers[0]), dot(far.astype(BF16), powers[1])
    left_refined[...] = (5.0 * old[2] - jnp.where(even, own, far)) / 4.0
    right_refined[...] = (5.0 * old[3] - jnp.where(even, far, own)) / 4.0


def on_device(activations, cotangent, left_gram, right_gram, left_root, right_root):
    left_gram, right_gram = left_gram[0], right_gram[0]
    left_root, right_root = left_root[0], right_root[0]

    half = jax.ShapeDtypeStruct((TOKENS, ROOT + HALF), BF16)
    own, far = call(
        pack_kernel, (half, half), [HBM] * 4,
        scratch=[pltpu.VMEM((2, ROWS, BS), F32), pltpu.SemaphoreType.DMA((2, NX + 2))],
        flops=100_000, moved=1_500_000,
    )(*map(in_hbm, (activations, cotangent, left_root, right_root)))
    more = lax.ppermute(far, "core", SWAP)
    strip = call(
        strip_kernel, jax.ShapeDtypeStruct((SIDE, STRIP), BF16), [VMEM, VMEM],
        scratch=[pltpu.VMEM((SIDE, BS), BF16)], moved=500_000,
    )(own, more)
    strip, more = lax.optimization_barrier((strip, more))
    strips = lax.all_gather(strip, "z", axis=0, tiled=True)
    partial = call(
        partial_kernel, jax.ShapeDtypeStruct((NZ, SLABS, WIDTH), BF16), [VMEM, VMEM],
        flops=2 * 256 * 2048 * 256, moved=3_000_000,
    )(own, more)
    parts = lax.all_to_all(partial, "z", 0, 0, tiled=True)
    copies = call(
        sum_kernel, jax.ShapeDtypeStruct((NX, NZ, ROWS, WIDTH), BF16), [VMEM],
        flops=1_000_000, moved=2_000_000,
    )(parts)
    root = call(
        root_kernel, jax.ShapeDtypeStruct((BS, BS), BF16), [VMEM], flops=1_000_000, moved=4_000_000
    )(strips)
    far_root = lax.ppermute(root, "core", SWAP)
    mine = lax.all_to_all(
        copies.reshape(NX * NZ, ROWS, WIDTH), ("x", "z"), 0, 0, tiled=True
    ).reshape(NX, HALF, WIDTH)
    other = lax.ppermute(mine, "core", SWAP)

    square = jax.ShapeDtypeStruct((BS, BS), BF16)
    precond, whole = call(
        precond_kernel, (jax.ShapeDtypeStruct((NX, ROWS, WIDTH), BF16), square), [ANY] * 4,
        places=(VMEM, HBM),
        scratch=[
            pltpu.VMEM((BS, BS), BF16),
            pltpu.VMEM((BS, BS), BF16),
            pltpu.VMEM((BS, BS), BF16),
            pltpu.VMEM((TILE, BS), F32),
            pltpu.SemaphoreType.DMA((3, 4)),
        ],
        flops=4 * BS**3, moved=6_000_000,
    )(mine, other, root, far_root)
    arrived = lax.all_to_all(precond, "x", 0, 0, tiled=True)
    shape = jax.ShapeDtypeStruct((ROWS, BS), F32)
    outs = call(
        factor_kernel, (shape,) * 4, [HBM] * 5 + [ANY] * 2,
        scratch=[
            pltpu.VMEM((BS, BS), BF16),
            pltpu.VMEM((SIDE, BS), F32),
            pltpu.VMEM((4, ROWS, BS), F32),
            pltpu.VMEM((2, BS, BS), BF16),
            pltpu.SemaphoreType.DMA((3, 4)),
        ],
        flops=8 * 64 * 1024 * 1024, moved=8_000_000,
    )(*map(in_hbm, (whole, left_gram, right_gram, left_root, right_root)), root, far_root)
    return (*(o[None] for o in outs), arrived.astype(F32))


def solution(mesh):
    split = Mesh(mesh.devices.reshape(NZ, NC, NY, NX), (*TOK, *HID))
    factor = P(HID, TOK, None)
    return jax.shard_map(
        on_device,
        mesh=split,
        in_specs=(P(TOK, None), P(TOK, HID), factor, factor, factor, factor),
        out_specs=(factor, factor, factor, factor, P(None, TOK, HID)),
        check_vma=False,
    )
```

time: 134 us -> 129 us (0.963)
  blocking collectives: 60.5 us -> 0 us
  waiting for transfers between devices: 12.7 us -> 56.4 us
  between operations: 0.73 us -> 14.1 us
  Pallas kernels: 27.9 us -> 21.3 us
  starting transfers between devices: 29.4 us -> 33.6 us
  local copies, waits for them, and re-layouts: 1.02 us -> 2.64 us
    all_to_all x1 -> x0, blocking collectives: 60.5 us -> none  [on_device(): parts = lax.all_to_all(partial, 'z', 0, 0, tiled=True)]
    all_to_all x0 -> x1, waiting for transfers between devices: none -> 28.4 us  [on_device(): parts = lax.all_to_all(partial, 'z', 0, 0, tiled=True)]
    all_gather x0 -> x1, waiting for transfers between devices: none -> 16.7 us  [on_device(): strips = lax.all_gather(strip, 'z', axis=0, tiled=True)]
    pallas_call x4, Pallas kernels: 23.4 us -> 18.1 us  [the longest x1 8.24 us: on_device(): call(precond_kernel, (jax.ShapeDtypeStruct((NX, ROWS, WIDTH), BF16), squa...]
    all_to_all x0 -> x1, starting transfers between devices: none -> 4.66 us  [on_device(): parts = lax.all_to_all(partial, 'z', 0, 0, tiled=True)]
    ppermute x1, starting transfers between devices: 7.01 us -> 3.23 us  [on_device(): other = lax.ppermute(mine, 'core', SWAP)]
    ppermute x1, starting transfers between devices: 3.51 us -> 6.97 us  [on_device(): far_root = lax.ppermute(root, 'core', SWAP)]
    ppermute x1 -> x0, starting transfers between devices: 1.92 us -> none  [on_device(): far_fifth = lax.ppermute(fifth, 'core', SWAP)]
  transfers between devices with their start and end apart: 6 -> 7, of which waited for: 4 -> 5; matrix products, arithmetic and copies ran while one was open for 0% -> 0% of each run, Pallas kernels for 18% -> 7%
where the time goes in v5:
time: 129 us
  waiting for transfers between devices  56.4 us (44%)
  starting transfers between devices  33.6 us (26%)
  Pallas kernels  21.3 us (17%)
  between operations  14.1 us (11%)
  local copies, waits for them, and re-layouts  2.64 us (2%)
    all_to_all x1, waiting for transfers between devices, on_device(): parts = lax.all_to_all(partial, 'z', 0, 0, tiled=True)  28.4 us
    all_gather x1, waiting for transfers between devices, on_device(): strips = lax.all_gather(strip, 'z', axis=0, tiled=True)  16.7 us
    ppermute x1, starting transfers between devices, on_device(): more = lax.ppermute(far, 'core', SWAP)  8.79 us
    pallas_call x1, Pallas kernels, on_device(): call(precond_kernel, (jax.ShapeDtypeStruct((NX, ROWS, WIDTH), BF16), squa...  8.24 us
    pallas_call x1, Pallas kernels, on_device(): call(factor_kernel, (shape,) * 4, [HBM] * 5 + [ANY] * 2, scratch=[pltpu.V...  7.43 us
    ppermute x1, starting transfers between devices, on_device(): far_root = lax.ppermute(root, 'core', SWAP)  6.97 us
    all_to_all x1, starting transfers between devices, on_device(): lax.all_to_all(copies.reshape(NX * NZ, ROWS, WIDTH), ('x', 'z'), 0, 0, ti...  6.58 us
    all_to_all x1, waiting for transfers between devices, on_device(): lax.all_to_all(copies.reshape(NX * NZ, ROWS, WIDTH), ('x', 'z'), 0, 0, ti...  6.57 us
  transfers between devices with their start and end apart: 7, of which 5 were waited for; matrix products, arithmetic and copies ran while one was open for 0% of the time, Pallas kernels for 7%

profile of v5, /device:TPU:1, one launch (start us, length us, event | category | flops | bytes accessed | tf_op | source)
XLA Modules:
  0.0 128.7 jit_solution(16338867331579532854)
XLA Ops:
  7.2 1.6 %shard_map.101 = (bf16[128,2816]{1,0:T(8,128)(2,1)S(1)}, bf16[128,2816]{1,0:T(8,128)(2,1)S(1)}) custom-call(bf16[128,4096]{1,0:T(8,128)(2,1)} %act.1, bf16[128,256]{1,0:T(8,128)(2,1)} %cot.1, f32[64,1024]{1,0:T(8,128)} %bitcast.12, f32[64,1024]{1,0:T(8,128)} %bitcast.14), custom_call_target="tpu_custom_call" | custom-call | flops 100000 | bytes 1500000 | tf_op jit(solution)/shard_map/pallas_call | solution.py:216
  8.8 8.8 %collective-permute-start = (bf16[128,2816]{1,0:T(8,128)(2,1)S(1)}, bf16[128,2816]{1,0:T(8,128)(2,1)S(1)}, u32[]{:S(2)}, u32[]{:S(2)}) collective-permute-start(bf16[128,2816]{1,0:T(8,128)(2,1)S(1)} %get-tuple-element.16), channel_id=1, source_target_pairs={{0,32},{32,0},{1,33},{33,1},{2,34},{34,2},{3,35},{35,3},{4,36},{36... | collective-permute-start | bytes 2162696 | tf_op jit(solution)/shard_map/ppermute | solution.py:221
  17.6 1.8 %collective-permute-done.more = bf16[128,2816]{1,0:T(8,128)(2,1)S(1)} collective-permute-done((bf16[128,2816]{1,0:T(8,128)(2,1)S(1)}, bf16[128,2816]{1,0:T(8,128)(2,1)S(1)}, u32[]{:S(2)}, u32[]{:S(2)}) %collective-permute-start) | collective-permute-done | bytes 720928 | tf_op jit(solution)/shard_map/ppermute | solution.py:221
  19.4 0.7 shard_map.102
  20.1 1.7 %shard_map.103 = bf16[8,256,256]{2,1,0:T(8,128)(2,1)} custom-call(bf16[128,2816]{1,0:T(8,128)(2,1)S(1)} %get-tuple-element.15.own, bf16[128,2816]{1,0:T(8,128)(2,1)S(1)} %collective-permute-done.more), custom_call_target="tpu_custom_call" | custom-call | flops 268435456 | bytes 3000000 | tf_op jit(solution)/shard_map/pallas_call | solution.py:228
  21.9 4.7 %all-to-all-start = ((bf16[8,256,256]{2,1,0:T(8,128)(2,1)}), bf16[8,256,256]{2,1,0:T(8,128)(2,1)S(1)}, u32[]{:S(2)}, u32[]{:S(2)}) async-start(bf16[8,256,256]{2,1,0:T(8,128)(2,1)} %shard_map.103), calls=%async_computation | async-start | bytes 2097152 | tf_op jit(solution)/shard_map/all_to_all | solution.py:232
  26.5 0.0 all-gather.2.cloned.1.call-start
  26.6 0.7 all-gather.2.cloned.1.call-update
  27.2 28.4 %all-to-all-done.parts = bf16[8,256,256]{2,1,0:T(8,128)(2,1)S(1)} async-done(((bf16[8,256,256]{2,1,0:T(8,128)(2,1)}), bf16[8,256,256]{2,1,0:T(8,128)(2,1)S(1)}, u32[]{:S(2)}, u32[]{:S(2)}) %all-to-all-start) | async-done | bytes 1048608 | tf_op jit(solution)/shard_map/all_to_all | solution.py:232
  55.6 1.1 shard_map.104
  56.7 6.6 %all-to-all-start.1 = ((bf16[32,64,256]{2,1,0:T(8,128)(2,1)}), bf16[32,64,256]{2,1,0:T(8,128)(2,1)S(1)}, u32[]{:S(2)}, u32[]{:S(2)}) async-start(bf16[32,64,256]{2,1,0:T(8,128)(2,1)} %bitcast.2), calls=%async_computation.1 | async-start | bytes 2097152 | tf_op jit(solution)/shard_map/all_to_all | solution.py:241
  63.3 16.7 %all-gather.2.cloned.1.call-done.strips = bf16[1024,640]{1,0:T(8,128)(2,1)} async-done(((bf16[128,640]{1,0:T(8,128)(2,1)}), bf16[1024,640]{1,0:T(8,128)(2,1)}) %all-gather.2.cloned.1.call-update) | async-done | bytes 1310736 | tf_op jit(solution)/shard_map/all_gather | solution.py:227
  80.0 1.3 %copy-done.1 = bf16[1024,640]{1,0:T(8,128)(2,1)S(1)} copy-done((bf16[1024,640]{1,0:T(8,128)(2,1)S(1)}, bf16[1024,640]{1,0:T(8,128)(2,1)}, u32[]{:S(2)}) %copy-start.1) | copy-done | bytes 1310744
  81.3 0.4 shard_map.105.root
  81.7 7.0 %collective-permute-start.2 = (bf16[1024,1024]{1,0:T(8,128)(2,1)S(1)}, bf16[1024,1024]{1,0:T(8,128)(2,1)}, u32[]{:S(2)}, u32[]{:S(2)}) collective-permute-start(bf16[1024,1024]{1,0:T(8,128)(2,1)S(1)} %shard_map.105.root), channel_id=1, source_target_pairs={{0,32},{32,0},{1,33},{33,1},{2,34},{34,2},{3,35},{35,3},{4,36},{36... | collective-permute-start | bytes 6291464 | tf_op jit(solution)/shard_map/ppermute | solution.py:240
  88.7 6.6 %all-to-all-done.1 = bf16[32,64,256]{2,1,0:T(8,128)(2,1)S(1)} async-done(((bf16[32,64,256]{2,1,0:T(8,128)(2,1)}), bf16[32,64,256]{2,1,0:T(8,128)(2,1)S(1)}, u32[]{:S(2)}, u32[]{:S(2)}) %all-to-all-start.1) | async-done | bytes 1048608 | tf_op jit(solution)/shard_map/all_to_all | solution.py:241
  95.3 3.2 %collective-permute-start.1 = (bf16[4,512,256]{2,1,0:T(8,128)(2,1)S(1)}, bf16[4,512,256]{2,1,0:T(8,128)(2,1)S(1)}, u32[]{:S(2)}, u32[]{:S(2)}) collective-permute-start(bf16[4,512,256]{2,1,0:T(8,128)(2,1)S(1)} %bitcast.10), channel_id=1, source_target_pairs={{0,32},{32,0},{1,33},{33,1},{2,34},{34,2},{3,35},{35,3},{4,36},{36... | collective-permute-start | bytes 3145736 | tf_op jit(solution)/shard_map/ppermute | solution.py:244
  98.5 0.0 collective-permute-done.2.far_root
  98.5 2.3 %collective-permute-done.1.other = bf16[4,512,256]{2,1,0:T(8,128)(2,1)S(1)} collective-permute-done((bf16[4,512,256]{2,1,0:T(8,128)(2,1)S(1)}, bf16[4,512,256]{2,1,0:T(8,128)(2,1)S(1)}, u32[]{:S(2)}, u32[]{:S(2)}) %collective-permute-start.1) | collective-permute-done | bytes 1048608 | tf_op jit(solution)/shard_map/ppermute | solution.py:244
  100.8 8.2 %shard_map.106 = (bf16[4,64,256]{2,1,0:T(8,128)(2,1)}, bf16[1024,1024]{1,0:T(8,128)(2,1)S(1)}) custom-call(bf16[4,512,256]{2,1,0:T(8,128)(2,1)S(1)} %bitcast.11, bf16[4,512,256]{2,1,0:T(8,128)(2,1)S(1)} %collective-permute-done.1.other, bf16[1024,1024]{1,0:T(8,128)(2,1)S(1)} %shard_map.105.root, bf16[1024,1024]{1,0:T(8,128)(2,1)} %collective-permute-done.2.far_root), custom_call_target="tpu_custom_call" | custom-call | flops 4294967296 | bytes 6000000 | tf_op jit(solution)/shard_map/pallas_call | solution.py:247
  109.1 1.3 %copy-done = bf16[1024,1024]{1,0:T(8,128)(2,1)} copy-done((bf16[1024,1024]{1,0:T(8,128)(2,1)}, bf16[1024,1024]{1,0:T(8,128)(2,1)S(1)}, u32[]{:S(2)}) %copy-start) | copy-done | bytes 2097176
  110.4 3.3 %all-to-all-start.2 = ((bf16[4,64,256]{2,1,0:T(8,128)(2,1)}), bf16[4,64,256]{2,1,0:T(8,128)(2,1)S(1)}, u32[]{:S(2)}, u32[]{:S(2)}) async-start(bf16[4,64,256]{2,1,0:T(8,128)(2,1)} %get-tuple-element.24), calls=%async_computation.2 | async-start | bytes 262144 | tf_op jit(solution)/shard_map/all_to_all | solution.py:259
  113.7 7.4 %shard_map.107 = (f32[64,1024]{1,0:T(8,128)}, f32[64,1024]{1,0:T(8,128)}, f32[64,1024]{1,0:T(8,128)}, f32[64,1024]{1,0:T(8,128)}) custom-call(bf16[1024,1024]{1,0:T(8,128)(2,1)} %copy-done, f32[64,1024]{1,0:T(8,128)} %bitcast.16, f32[64,1024]{1,0:T(8,128)} %bitcast.17, f32[64,1024]{1,0:T(8,128)} %bitcast.13, f32[64,1024]{1,0:T(8,128)} %bitcast.15, ...), custom_call_target="tpu_custom_call" | custom-call | flops 536870912 | bytes 8000000 | tf_op jit(solution)/shard_map/pallas_call | solution.py:261
  121.2 0.7 convert_element_type.3
  (3 shorter events, 0.0 us)
Async XLA Ops:
  8.8 10.6 %collective-permute-start = (bf16[128,2816]{1,0:T(8,128)(2,1)S(1)}, bf16[128,2816]{1,0:T(8,128)(2,1)S(1)}, u32[]{:S(2)}, u32[]{:S(2)}) collective-permute-start(bf16[128,2816]{1,0:T(8,128)(2,1)S(1)} %get-tuple-element.16), channel_id=1, source_target_pairs={{0,32},{32,0},{1,33},{33,1},{2,34},{34,2},{3,35},{35,3},{4,36},{36... | collective-permute-start | bytes 2162696 | tf_op jit(solution)/shard_map/ppermute | solution.py:221
  21.9 33.8 %all-to-all-start = ((bf16[8,256,256]{2,1,0:T(8,128)(2,1)}), bf16[8,256,256]{2,1,0:T(8,128)(2,1)S(1)}, u32[]{:S(2)}, u32[]{:S(2)}) async-start(bf16[8,256,256]{2,1,0:T(8,128)(2,1)} %shard_map.103), calls=%async_computation | async-start | bytes 2097152 | tf_op jit(solution)/shard_map/all_to_all | solution.py:232
  26.5 53.5 %all-gather.2.cloned.1.call-start = ((), (), s32[]{:S(2)}) async-start(), calls=%async_computation.3 | async-start | bytes 1474560 | tf_op jit(solution)/shard_map/all_gather | solution.py:227
  56.7 38.6 %all-to-all-start.1 = ((bf16[32,64,256]{2,1,0:T(8,128)(2,1)}), bf16[32,64,256]{2,1,0:T(8,128)(2,1)S(1)}, u32[]{:S(2)}, u32[]{:S(2)}) async-start(bf16[32,64,256]{2,1,0:T(8,128)(2,1)} %bitcast.2), calls=%async_computation.1 | async-start | bytes 2097152 | tf_op jit(solution)/shard_map/all_to_all | solution.py:241
  80.0 1.3 %copy-start.1 = (bf16[1024,640]{1,0:T(8,128)(2,1)S(1)}, bf16[1024,640]{1,0:T(8,128)(2,1)}, u32[]{:S(2)}) copy-start(bf16[1024,640]{1,0:T(8,128)(2,1)} %all-gather.2.cloned.1.call-done.strips) | copy-start | bytes 3932164
  81.7 16.8 %collective-permute-start.2 = (bf16[1024,1024]{1,0:T(8,128)(2,1)S(1)}, bf16[1024,1024]{1,0:T(8,128)(2,1)}, u32[]{:S(2)}, u32[]{:S(2)}) collective-permute-start(bf16[1024,1024]{1,0:T(8,128)(2,1)S(1)} %shard_map.105.root), channel_id=1, source_target_pairs={{0,32},{32,0},{1,33},{33,1},{2,34},{34,2},{3,35},{35,3},{4,36},{36... | collective-permute-start | bytes 6291464 | tf_op jit(solution)/shard_map/ppermute | solution.py:240
  95.3 5.5 %collective-permute-start.1 = (bf16[4,512,256]{2,1,0:T(8,128)(2,1)S(1)}, bf16[4,512,256]{2,1,0:T(8,128)(2,1)S(1)}, u32[]{:S(2)}, u32[]{:S(2)}) collective-permute-start(bf16[4,512,256]{2,1,0:T(8,128)(2,1)S(1)} %bitcast.10), channel_id=1, source_target_pairs={{0,32},{32,0},{1,33},{33,1},{2,34},{34,2},{3,35},{35,3},{4,36},{36... | collective-permute-start | bytes 3145736 | tf_op jit(solution)/shard_map/ppermute | solution.py:244
  109.0 1.3 %copy-start = (bf16[1024,1024]{1,0:T(8,128)(2,1)}, bf16[1024,1024]{1,0:T(8,128)(2,1)S(1)}, u32[]{:S(2)}) copy-start(bf16[1024,1024]{1,0:T(8,128)(2,1)S(1)} %get-tuple-element.19.stored) | copy-start | bytes 6291460
  110.4 10.8 %all-to-all-start.2 = ((bf16[4,64,256]{2,1,0:T(8,128)(2,1)}), bf16[4,64,256]{2,1,0:T(8,128)(2,1)S(1)}, u32[]{:S(2)}, u32[]{:S(2)}) async-start(bf16[4,64,256]{2,1,0:T(8,128)(2,1)} %get-tuple-element.24), calls=%async_computation.2 | async-start | bytes 262144 | tf_op jit(solution)/shard_map/all_to_all | solution.py:259
Sparse Core Ops, SparseCore 0:
  30.0 49.9 all-gather.1

commit v6 on v5

--- a/solution.py
+++ b/solution.py
@@ -148,22 +148,24 @@
         for copy in bring(far_root, root):
             copy.start()
 
-    for copy in pieces + bring(root, far_root):
+    applies, follows = bring(root, far_root)
+    for copy in pieces + [applies]:
         copy.wait()
     store = pltpu.make_async_copy(whole, stored, sems.at[2, 2])
     store.start()
 
-    def tile(i, total):
-        rows = at(i * TILE, TILE, TILE)
-        precond = dot(dot(left[rows], whole[...]).astype(BF16), right[...])
+    total = jnp.zeros((1, BS), F32)
+    for i in range(BS // TILE):
+        applied = dot(left[i * TILE : (i + 1) * TILE], whole[...]).astype(BF16)
+        if i == 0:
+            follows.wait()
+        precond = dot(applied, right[...])
+        total += jnp.sum(precond * precond, axis=0, keepdims=True)
 
         @pl.when(i == place // TILE)
-        def _():
+        def _(precond=precond):
             kept[...] = precond
 
-        return total + jnp.sum(precond * precond, axis=0, keepdims=True)
-
-    total = lax.fori_loop(0, BS // TILE, tile, jnp.zeros((1, BS), F32))
     scale = 1.0 / jnp.sqrt(jnp.sum(total) / (BS * BS) + EPS)
     scaled = kept[at(place % TILE, ROWS, ROWS)] * scale
     for x in range(NX):
@@ -171,8 +173,13 @@
     store.wait()
 
 
+def square_kernel(root, squared):
+    for i in range(0, BS, TILE):
+        squared[i : i + TILE] = dot(root[i : i + TILE], root[...]).astype(BF16)
+
+
 def factor_kernel(
-    stored, left_gram, right_gram, left_root, right_root, root, far_root,
+    stored, left_gram, right_gram, left_root, right_root, squared, far_squared, root, far_root,
     left_next, right_next, left_refined, right_refined, whole, columns, old, powers, sems,
 ):
     z, core = lax.axis_index("z"), lax.axis_index("core")
@@ -183,7 +190,7 @@
     ]
     both = [
         pltpu.make_async_copy(source, powers.at[k], sems.at[1, k])
-        for k, source in enumerate((root, far_root))
+        for k, source in enumerate((squared, far_squared, root, far_root))
     ]
     load = pltpu.make_async_copy(stored, whole, sems.at[2, 0])
     for copy in [load] + olds + both:
@@ -195,15 +202,18 @@
     left = dot(rows, whole[...], ((1,), (1,)))
     turned = columns[at(core * ROWS, ROWS, ROWS)].astype(BF16)
     right = dot(turned, whole[...])
-    for copy in olds + both:
+    for copy in olds + both[:2]:
         copy.wait()
     left = BETA * old[0] + left
     left_next[...] = left
     right = BETA * old[1] + right
     right_next[...] = right
     own, far = jnp.where(even, left, right), jnp.where(even, right, left)
-    for _ in range(5):
+    for _ in range(2):
         own, far = dot(own.astype(BF16), powers[0]), dot(far.astype(BF16), powers[1])
+    for copy in both[2:]:
+        copy.wait()
+    own, far = dot(own.astype(BF16), powers[2]), dot(far.astype(BF16), powers[3])
     left_refined[...] = (5.0 * old[2] - jnp.where(even, own, far)) / 4.0
     right_refined[...] = (5.0 * old[3] - jnp.where(even, far, own)) / 4.0
 
@@ -238,12 +248,16 @@
         root_kernel, jax.ShapeDtypeStruct((BS, BS), BF16), [VMEM], flops=1_000_000, moved=4_000_000
     )(strips)
     far_root = lax.ppermute(root, "core", SWAP)
+    squared = call(
+        square_kernel, jax.ShapeDtypeStruct((BS, BS), BF16), [VMEM], flops=2 * BS**3, moved=4_000_000
+    )(root)
+    far_squared = lax.ppermute(squared, "core", SWAP)
     mine = lax.all_to_all(
         copies.reshape(NX * NZ, ROWS, WIDTH), ("x", "z"), 0, 0, tiled=True
     ).reshape(NX, HALF, WIDTH)
     other = lax.ppermute(mine, "core", SWAP)
 
-    square = jax.ShapeDtypeStruct((BS, BS), BF16)
+    square = pltpu.HBM((BS, BS), BF16)
     precond, whole = call(
         precond_kernel, (jax.ShapeDtypeStruct((NX, ROWS, WIDTH), BF16), square), [ANY] * 4,
         places=(VMEM, HBM),
@@ -259,16 +273,16 @@
     arrived = lax.all_to_all(precond, "x", 0, 0, tiled=True)
     shape = jax.ShapeDtypeStruct((ROWS, BS), F32)
     outs = call(
-        factor_kernel, (shape,) * 4, [HBM] * 5 + [ANY] * 2,
+        factor_kernel, (shape,) * 4, [HBM] * 5 + [ANY] * 4,
         scratch=[
             pltpu.VMEM((BS, BS), BF16),
             pltpu.VMEM((SIDE, BS), F32),
             pltpu.VMEM((4, ROWS, BS), F32),
-            pltpu.VMEM((2, BS, BS), BF16),
+            pltpu.VMEM((4, BS, BS), BF16),
             pltpu.SemaphoreType.DMA((3, 4)),
         ],
-        flops=8 * 64 * 1024 * 1024, moved=8_000_000,
-    )(*map(in_hbm, (whole, left_gram, right_gram, left_root, right_root)), root, far_root)
+        flops=16 * 64 * 1024 * 1024, moved=8_000_000,
+    )(*map(in_hbm, (whole, left_gram, right_gram, left_root, right_root)), squared, far_squared, root, far_root)
     return (*(o[None] for o in outs), arrived.astype(F32))
 
 

time: 129 us -> 127 us (0.984)
  waiting for transfers between devices: 56.4 us -> 50.8 us
  Pallas kernels: 21.3 us -> 23.7 us
  starting transfers between devices: 33.6 us -> 35.5 us
  local copies, waits for them, and re-layouts: 2.64 us -> 1.32 us
    all_to_all x1, waiting for transfers between devices: 6.57 us -> 1.02 us  [on_device(): lax.all_to_all(copies.reshape(NX * NZ, ROWS, WIDTH), ('x', 'z'), 0, 0, ti...]
    pallas_call x1 -> x2, Pallas kernels: 7.43 us -> 10.2 us  [the longest x1 6.54 us: on_device(): call(factor_kernel, (shape,) * 4, [HBM] * 5 + [ANY] * 4, scratch=[pltpu.V...]
    ppermute x0 -> x1, starting transfers between devices: none -> 1.91 us  [on_device(): far_squared = lax.ppermute(squared, 'core', SWAP)]
    unnamed x4 -> x2, local copies, waits for them, and re-layouts: 2.64 us -> 1.32 us
  transfers between devices with their start and end apart: 7 -> 8, of which waited for: 5 -> 5; matrix products, arithmetic and copies ran while one was open for 0% -> 0% of each run, Pallas kernels for 7% -> 16%
where the time goes in v6:
time: 127 us; the launch traced here: 126 us
  waiting for transfers between devices  50.8 us (40%)
  starting transfers between devices  35.5 us (28%)
  Pallas kernels  23.7 us (19%)
  between operations  14.1 us (11%)
  local copies, waits for them, and re-layouts  1.32 us (1%)
    all_to_all x1, waiting for transfers between devices, on_device(): parts = lax.all_to_all(partial, 'z', 0, 0, tiled=True)  28.4 us
    all_gather x1, waiting for transfers between devices, on_device(): strips = lax.all_gather(strip, 'z', axis=0, tiled=True)  16.7 us
    ppermute x1, starting transfers between devices, on_device(): more = lax.ppermute(far, 'core', SWAP)  8.79 us
    pallas_call x1, Pallas kernels, on_device(): call(precond_kernel, (jax.ShapeDtypeStruct((NX, ROWS, WIDTH), BF16), squa...  7.82 us
    ppermute x1, starting transfers between devices, on_device(): far_root = lax.ppermute(root, 'core', SWAP)  6.88 us
    all_to_all x1, starting transfers between devices, on_device(): lax.all_to_all(copies.reshape(NX * NZ, ROWS, WIDTH), ('x', 'z'), 0, 0, ti...  6.58 us
    pallas_call x1, Pallas kernels, on_device(): call(factor_kernel, (shape,) * 4, [HBM] * 5 + [ANY] * 4, scratch=[pltpu.V...  6.54 us
    all_to_all x1, starting transfers between devices, on_device(): parts = lax.all_to_all(partial, 'z', 0, 0, tiled=True)  4.66 us
  transfers between devices with their start and end apart: 8, of which 5 were waited for; matrix products, arithmetic and copies ran while one was open for 0% of the time, Pallas kernels for 16%

profile of v6, /device:TPU:1, one launch (start us, length us, event | category | flops | bytes accessed | tf_op | source)
XLA Modules:
  0.0 126.1 jit_solution(6208380437668301711)
XLA Ops:
  7.2 1.6 %shard_map.101 = (bf16[128,2816]{1,0:T(8,128)(2,1)S(1)}, bf16[128,2816]{1,0:T(8,128)(2,1)S(1)}) custom-call(bf16[128,4096]{1,0:T(8,128)(2,1)} %act.1, bf16[128,256]{1,0:T(8,128)(2,1)} %cot.1, f32[64,1024]{1,0:T(8,128)} %bitcast.12, f32[64,1024]{1,0:T(8,128)} %bitcast.14), custom_call_target="tpu_custom_call" | custom-call | flops 100000 | bytes 1500000 | tf_op jit(solution)/shard_map/pallas_call | solution.py:226
  8.8 8.8 %collective-permute-start = (bf16[128,2816]{1,0:T(8,128)(2,1)S(1)}, bf16[128,2816]{1,0:T(8,128)(2,1)S(1)}, u32[]{:S(2)}, u32[]{:S(2)}) collective-permute-start(bf16[128,2816]{1,0:T(8,128)(2,1)S(1)} %get-tuple-element.16), channel_id=1, source_target_pairs={{0,32},{32,0},{1,33},{33,1},{2,34},{34,2},{3,35},{35,3},{4,36},{36... | collective-permute-start | bytes 2162696 | tf_op jit(solution)/shard_map/ppermute | solution.py:231
  17.6 1.8 %collective-permute-done.more = bf16[128,2816]{1,0:T(8,128)(2,1)S(1)} collective-permute-done((bf16[128,2816]{1,0:T(8,128)(2,1)S(1)}, bf16[128,2816]{1,0:T(8,128)(2,1)S(1)}, u32[]{:S(2)}, u32[]{:S(2)}) %collective-permute-start) | collective-permute-done | bytes 720928 | tf_op jit(solution)/shard_map/ppermute | solution.py:231
  19.4 0.7 shard_map.102
  20.1 1.7 %shard_map.103 = bf16[8,256,256]{2,1,0:T(8,128)(2,1)} custom-call(bf16[128,2816]{1,0:T(8,128)(2,1)S(1)} %get-tuple-element.15.own, bf16[128,2816]{1,0:T(8,128)(2,1)S(1)} %collective-permute-done.more), custom_call_target="tpu_custom_call" | custom-call | flops 268435456 | bytes 3000000 | tf_op jit(solution)/shard_map/pallas_call | solution.py:238
  21.9 4.7 %all-to-all-start = ((bf16[8,256,256]{2,1,0:T(8,128)(2,1)}), bf16[8,256,256]{2,1,0:T(8,128)(2,1)S(1)}, u32[]{:S(2)}, u32[]{:S(2)}) async-start(bf16[8,256,256]{2,1,0:T(8,128)(2,1)} %shard_map.103), calls=%async_computation | async-start | bytes 2097152 | tf_op jit(solution)/shard_map/all_to_all | solution.py:242
  26.5 0.0 all-gather.2.cloned.1.call-start
  26.6 0.7 all-gather.2.cloned.1.call-update
  27.2 28.4 %all-to-all-done.parts = bf16[8,256,256]{2,1,0:T(8,128)(2,1)S(1)} async-done(((bf16[8,256,256]{2,1,0:T(8,128)(2,1)}), bf16[8,256,256]{2,1,0:T(8,128)(2,1)S(1)}, u32[]{:S(2)}, u32[]{:S(2)}) %all-to-all-start) | async-done | bytes 1048608 | tf_op jit(solution)/shard_map/all_to_all | solution.py:242
  55.6 1.1 shard_map.104
  56.8 6.6 %all-to-all-start.1 = ((bf16[32,64,256]{2,1,0:T(8,128)(2,1)}), bf16[32,64,256]{2,1,0:T(8,128)(2,1)S(1)}, u32[]{:S(2)}, u32[]{:S(2)}) async-start(bf16[32,64,256]{2,1,0:T(8,128)(2,1)} %bitcast.2), calls=%async_computation.1 | async-start | bytes 2097152 | tf_op jit(solution)/shard_map/all_to_all | solution.py:255
  63.3 16.7 %all-gather.2.cloned.1.call-done.strips = bf16[1024,640]{1,0:T(8,128)(2,1)} async-done(((bf16[128,640]{1,0:T(8,128)(2,1)}), bf16[1024,640]{1,0:T(8,128)(2,1)}) %all-gather.2.cloned.1.call-update) | async-done | bytes 1310736 | tf_op jit(solution)/shard_map/all_gather | solution.py:237
  80.0 1.3 %copy-done = bf16[1024,640]{1,0:T(8,128)(2,1)S(1)} copy-done((bf16[1024,640]{1,0:T(8,128)(2,1)S(1)}, bf16[1024,640]{1,0:T(8,128)(2,1)}, u32[]{:S(2)}) %copy-start) | copy-done | bytes 1310744
  81.3 0.4 shard_map.105.root
  81.7 6.9 %collective-permute-start.2 = (bf16[1024,1024]{1,0:T(8,128)(2,1)S(1)}, bf16[1024,1024]{1,0:T(8,128)(2,1)}, u32[]{:S(2)}, u32[]{:S(2)}) collective-permute-start(bf16[1024,1024]{1,0:T(8,128)(2,1)S(1)} %shard_map.105.root), channel_id=1, source_target_pairs={{0,32},{32,0},{1,33},{33,1},{2,34},{34,2},{3,35},{35,3},{4,36},{36... | collective-permute-start | bytes 6291464 | tf_op jit(solution)/shard_map/ppermute | solution.py:250
  88.6 3.7 %shard_map.107.squared = bf16[1024,1024]{1,0:T(8,128)(2,1)} custom-call(bf16[1024,1024]{1,0:T(8,128)(2,1)S(1)} %shard_map.105.root), custom_call_target="tpu_custom_call" | custom-call | flops 2147483648 | bytes 4000000 | tf_op jit(solution)/shard_map/pallas_call | solution.py:251
  92.3 1.9 %collective-permute-start.3 = (bf16[1024,1024]{1,0:T(8,128)(2,1)}, bf16[1024,1024]{1,0:T(8,128)(2,1)}, u32[]{:S(2)}, u32[]{:S(2)}) collective-permute-start(bf16[1024,1024]{1,0:T(8,128)(2,1)} %shard_map.107.squared), channel_id=1, source_target_pairs={{0,32},{32,0},{1,33},{33,1},{2,34},{34,2},{3,35},{35,3},{4,36},{36... | collective-permute-start | bytes 6291464 | tf_op jit(solution)/shard_map/ppermute | solution.py:254
  94.2 1.0 all-to-all-done.1
  95.2 3.3 %collective-permute-start.1 = (bf16[4,512,256]{2,1,0:T(8,128)(2,1)S(1)}, bf16[4,512,256]{2,1,0:T(8,128)(2,1)S(1)}, u32[]{:S(2)}, u32[]{:S(2)}) collective-permute-start(bf16[4,512,256]{2,1,0:T(8,128)(2,1)S(1)} %bitcast.10), channel_id=1, source_target_pairs={{0,32},{32,0},{1,33},{33,1},{2,34},{34,2},{3,35},{35,3},{4,36},{36... | collective-permute-start | bytes 3145736 | tf_op jit(solution)/shard_map/ppermute | solution.py:258
  98.6 2.3 %collective-permute-done.1.other = bf16[4,512,256]{2,1,0:T(8,128)(2,1)S(1)} collective-permute-done((bf16[4,512,256]{2,1,0:T(8,128)(2,1)S(1)}, bf16[4,512,256]{2,1,0:T(8,128)(2,1)S(1)}, u32[]{:S(2)}, u32[]{:S(2)}) %collective-permute-start.1) | collective-permute-done | bytes 1048608 | tf_op jit(solution)/shard_map/ppermute | solution.py:258
  100.8 7.8 %shard_map.106 = (bf16[4,64,256]{2,1,0:T(8,128)(2,1)}, bf16[1024,1024]{1,0:T(8,128)(2,1)}) custom-call(bf16[4,512,256]{2,1,0:T(8,128)(2,1)S(1)} %bitcast.11, bf16[4,512,256]{2,1,0:T(8,128)(2,1)S(1)} %collective-permute-done.1.other, bf16[1024,1024]{1,0:T(8,128)(2,1)S(1)} %shard_map.105.root, bf16[1024,1024]{1,0:T(8,128)(2,1)} %collective-permute-done.2.far_root), custom_call_target="tpu_custom_call" | custom-call | flops 4294967296 | bytes 6000000 | tf_op jit(solution)/shard_map/pallas_call | solution.py:261
  108.6 3.3 %all-to-all-start.2 = ((bf16[4,64,256]{2,1,0:T(8,128)(2,1)}), bf16[4,64,256]{2,1,0:T(8,128)(2,1)S(1)}, u32[]{:S(2)}, u32[]{:S(2)}) async-start(bf16[4,64,256]{2,1,0:T(8,128)(2,1)} %get-tuple-element.24), calls=%async_computation.2 | async-start | bytes 262144 | tf_op jit(solution)/shard_map/all_to_all | solution.py:273
  112.0 6.5 %shard_map.108 = (f32[64,1024]{1,0:T(8,128)}, f32[64,1024]{1,0:T(8,128)}, f32[64,1024]{1,0:T(8,128)}, f32[64,1024]{1,0:T(8,128)}) custom-call(bf16[1024,1024]{1,0:T(8,128)(2,1)} %get-tuple-element.19.stored, f32[64,1024]{1,0:T(8,128)} %bitcast.16, f32[64,1024]{1,0:T(8,128)} %bitcast.17, f32[64,1024]{1,0:T(8,128)} %bitcast.13, f32[64,1024]{1,0:T(8,128)} %bitcast.15, ...), custom_call_target="tpu_custom_call" | custom-call | flops 1073741824 | bytes 8000000 | tf_op jit(solution)/shard_map/pallas_call | solution.py:275
  118.5 0.7 convert_element_type.3
  (4 shorter events, 0.0 us)
Async XLA Ops:
  8.8 10.6 %collective-permute-start = (bf16[128,2816]{1,0:T(8,128)(2,1)S(1)}, bf16[128,2816]{1,0:T(8,128)(2,1)S(1)}, u32[]{:S(2)}, u32[]{:S(2)}) collective-permute-start(bf16[128,2816]{1,0:T(8,128)(2,1)S(1)} %get-tuple-element.16), channel_id=1, source_target_pairs={{0,32},{32,0},{1,33},{33,1},{2,34},{34,2},{3,35},{35,3},{4,36},{36... | collective-permute-start | bytes 2162696 | tf_op jit(solution)/shard_map/ppermute | solution.py:231
  21.9 33.8 %all-to-all-start = ((bf16[8,256,256]{2,1,0:T(8,128)(2,1)}), bf16[8,256,256]{2,1,0:T(8,128)(2,1)S(1)}, u32[]{:S(2)}, u32[]{:S(2)}) async-start(bf16[8,256,256]{2,1,0:T(8,128)(2,1)} %shard_map.103), calls=%async_computation | async-start | bytes 2097152 | tf_op jit(solution)/shard_map/all_to_all | solution.py:242
  26.5 53.5 %all-gather.2.cloned.1.call-start = ((), (), s32[]{:S(2)}) async-start(), calls=%async_computation.3 | async-start | bytes 1474560 | tf_op jit(solution)/shard_map/all_gather | solution.py:237
  56.8 38.5 %all-to-all-start.1 = ((bf16[32,64,256]{2,1,0:T(8,128)(2,1)}), bf16[32,64,256]{2,1,0:T(8,128)(2,1)S(1)}, u32[]{:S(2)}, u32[]{:S(2)}) async-start(bf16[32,64,256]{2,1,0:T(8,128)(2,1)} %bitcast.2), calls=%async_computation.1 | async-start | bytes 2097152 | tf_op jit(solution)/shard_map/all_to_all | solution.py:255
  80.0 1.3 %copy-start = (bf16[1024,640]{1,0:T(8,128)(2,1)S(1)}, bf16[1024,640]{1,0:T(8,128)(2,1)}, u32[]{:S(2)}) copy-start(bf16[1024,640]{1,0:T(8,128)(2,1)} %all-gather.2.cloned.1.call-done.strips) | copy-start | bytes 3932164
  81.7 16.8 %collective-permute-start.2 = (bf16[1024,1024]{1,0:T(8,128)(2,1)S(1)}, bf16[1024,1024]{1,0:T(8,128)(2,1)}, u32[]{:S(2)}, u32[]{:S(2)}) collective-permute-start(bf16[1024,1024]{1,0:T(8,128)(2,1)S(1)} %shard_map.105.root), channel_id=1, source_target_pairs={{0,32},{32,0},{1,33},{33,1},{2,34},{34,2},{3,35},{35,3},{4,36},{36... | collective-permute-start | bytes 6291464 | tf_op jit(solution)/shard_map/ppermute | solution.py:250
  92.3 19.7 %collective-permute-start.3 = (bf16[1024,1024]{1,0:T(8,128)(2,1)}, bf16[1024,1024]{1,0:T(8,128)(2,1)}, u32[]{:S(2)}, u32[]{:S(2)}) collective-permute-start(bf16[1024,1024]{1,0:T(8,128)(2,1)} %shard_map.107.squared), channel_id=1, source_target_pairs={{0,32},{32,0},{1,33},{33,1},{2,34},{34,2},{3,35},{35,3},{4,36},{36... | collective-permute-start | bytes 6291464 | tf_op jit(solution)/shard_map/ppermute | solution.py:254
  95.2 5.6 %collective-permute-start.1 = (bf16[4,512,256]{2,1,0:T(8,128)(2,1)S(1)}, bf16[4,512,256]{2,1,0:T(8,128)(2,1)S(1)}, u32[]{:S(2)}, u32[]{:S(2)}) collective-permute-start(bf16[4,512,256]{2,1,0:T(8,128)(2,1)S(1)} %bitcast.10), channel_id=1, source_target_pairs={{0,32},{32,0},{1,33},{33,1},{2,34},{34,2},{3,35},{35,3},{4,36},{36... | collective-permute-start | bytes 3145736 | tf_op jit(solution)/shard_map/ppermute | solution.py:258
  108.6 9.9 %all-to-all-start.2 = ((bf16[4,64,256]{2,1,0:T(8,128)(2,1)}), bf16[4,64,256]{2,1,0:T(8,128)(2,1)S(1)}, u32[]{:S(2)}, u32[]{:S(2)}) async-start(bf16[4,64,256]{2,1,0:T(8,128)(2,1)} %get-tuple-element.24), calls=%async_computation.2 | async-start | bytes 262144 | tf_op jit(solution)/shard_map/all_to_all | solution.py:273
Sparse Core Ops, SparseCore 0:
  30.0 49.9 all-gather.1

commit v7 on v6

--- a/solution.py
+++ b/solution.py
@@ -1,3 +1,5 @@
+import functools
+
 import jax
 import jax.numpy as jnp
 from jax import lax
@@ -56,25 +58,27 @@
     return pl.ds(pl.multiple_of(start, unit), size)
 
 
-def pack_kernel(act, cot, left_root, right_root, own, far, roots, sems):
+def pack_kernel(mate, act, cot, left_root, right_root, out, root, sems):
     core = lax.axis_index("core")
-    copies = []
-    for k, (out, side) in enumerate(((far, 1 - core), (own, core))):
-        for r in range(NX):
-            source = act.at[:, at(r * BS + side * HALF, HALF, 128)]
-            target = out.at[:, pl.ds(r * HALF, HALF)]
-            copies.append(pltpu.make_async_copy(source, target, sems.at[k, r]))
-        copies.append(pltpu.make_async_copy(cot, out.at[:, pl.ds(COT, WIDTH)], sems.at[k, NX]))
-    copies.append(pltpu.make_async_copy(left_root, roots.at[0], sems.at[0, NX + 1]))
-    copies.append(pltpu.make_async_copy(right_root, roots.at[1], sems.at[1, NX + 1]))
+    side = 1 - core if mate else core
+    copies = [pltpu.make_async_copy(cot, out.at[:, pl.ds(COT, WIDTH)], sems.at[NX])]
+    for r in range(NX):
+        source = act.at[:, at(r * BS + side * HALF, HALF, 128)]
+        copies.append(pltpu.make_async_copy(source, out.at[:, pl.ds(r * HALF, HALF)], sems.at[r]))
+    for k, source in enumerate((left_root, right_root)):
+
+        @pl.when(side == k)
+        def _(source=source):
+            pltpu.make_async_copy(source, root, sems.at[NX + 1]).start()
+
     for copy in copies:
         copy.start()
+    pltpu.make_async_copy(left_root, root, sems.at[NX + 1]).wait()
+    low = root[...].astype(BF16)
+    out[:ROWS, ROOT:] = low[:, :HALF]
+    out[ROWS:, ROOT:] = low[:, HALF:]
     for copy in copies:
         copy.wait()
-    for out, side in ((far, 1 - core), (own, core)):
-        low = roots[side].astype(BF16)
-        out[:ROWS, ROOT:] = low[:, :HALF]
-        out[ROWS:, ROOT:] = low[:, HALF:]
 
 
 def strip_kernel(own, more, strip, shard):
@@ -120,13 +124,38 @@
                 root[there, own] = piece.T
 
 
-def precond_kernel(mine, other, root, far_root, out, stored, whole, left, right, kept, sems):
+def first_kernel(mine, root, far_root, out, upper, left, sems):
+    core = lax.axis_index("core")
+    cols = at(core * HALF, HALF, 128)
+    pieces = [
+        pltpu.make_async_copy(mine.at[x], upper.at[:, pl.ds(x * WIDTH, WIDTH)], sems.at[x])
+        for x in range(NX)
+    ]
+    for copy in pieces:
+        copy.start()
+    for side, source in enumerate((root, far_root)):
+
+        @pl.when(core == side)
+        def _(source=source):
+            pltpu.make_async_copy(source.at[:, cols], left, sems.at[NX]).start()
+
+    for copy in pieces + [pltpu.make_async_copy(root.at[:, cols], left, sems.at[NX])]:
+        copy.wait()
+    for i in range(0, BS, TILE):
+        out[i : i + TILE] = dot(left[i : i + TILE], upper[...])
+
+
+def precond_kernel(
+    mine, other, root, far_root, first, out, stored, whole, left, right, kept, sems
+):
     z, core = lax.axis_index("z"), lax.axis_index("core")
     place = (z * NC + core) * ROWS
 
-    def bring(first, second):
+    cols = at((1 - core) * HALF, HALF, 128)
+
+    def bring(applied_by, second):
         return [
-            pltpu.make_async_copy(first, left, sems.at[2, 0]),
+            pltpu.make_async_copy(applied_by.at[:, cols], left, sems.at[2, 0]),
             pltpu.make_async_copy(second, right, sems.at[2, 1]),
         ]
 
@@ -156,7 +185,9 @@
 
     total = jnp.zeros((1, BS), F32)
     for i in range(BS // TILE):
-        applied = dot(left[i * TILE : (i + 1) * TILE], whole[...]).astype(BF16)
+        part = slice(i * TILE, (i + 1) * TILE)
+        lower = whole[at((1 - core) * HALF, HALF, HALF)]
+        applied = (first[part] + dot(left[part], lower)).astype(BF16)
         if i == 0:
             follows.wait()
         precond = dot(applied, right[...])
@@ -222,13 +253,18 @@
     left_gram, right_gram = left_gram[0], right_gram[0]
     left_root, right_root = left_root[0], right_root[0]
 
-    half = jax.ShapeDtypeStruct((TOKENS, ROOT + HALF), BF16)
-    own, far = call(
-        pack_kernel, (half, half), [HBM] * 4,
-        scratch=[pltpu.VMEM((2, ROWS, BS), F32), pltpu.SemaphoreType.DMA((2, NX + 2))],
-        flops=100_000, moved=1_500_000,
-    )(*map(in_hbm, (activations, cotangent, left_root, right_root)))
+    def pack(mate):
+        return call(
+            functools.partial(pack_kernel, mate),
+            jax.ShapeDtypeStruct((TOKENS, ROOT + HALF), BF16), [HBM] * 4,
+            scratch=[pltpu.VMEM((ROWS, BS), F32), pltpu.SemaphoreType.DMA((NX + 2,))],
+            flops=100_000, moved=1_000_000,
+        )(*map(in_hbm, (activations, cotangent, left_root, right_root)))
+
+    far = pack(1)
     more = lax.ppermute(far, "core", SWAP)
+    own = pack(0)
+    more, own = lax.optimization_barrier((more, own))
     strip = call(
         strip_kernel, jax.ShapeDtypeStruct((SIDE, STRIP), BF16), [VMEM, VMEM],
         scratch=[pltpu.VMEM((SIDE, BS), BF16)], moved=500_000,
@@ -257,19 +293,29 @@
     ).reshape(NX, HALF, WIDTH)
     other = lax.ppermute(mine, "core", SWAP)
 
+    first = call(
+        first_kernel, jax.ShapeDtypeStruct((BS, BS), F32), [ANY] * 3,
+        scratch=[
+            pltpu.VMEM((HALF, BS), BF16),
+            pltpu.VMEM((BS, HALF), BF16),
+            pltpu.SemaphoreType.DMA((NX + 1,)),
+        ],
+        flops=BS**3, moved=3_000_000,
+    )(mine, root, far_root)
+    other, first = lax.optimization_barrier((other, first))
     square = pltpu.HBM((BS, BS), BF16)
     precond, whole = call(
-        precond_kernel, (jax.ShapeDtypeStruct((NX, ROWS, WIDTH), BF16), square), [ANY] * 4,
+        precond_kernel, (jax.ShapeDtypeStruct((NX, ROWS, WIDTH), BF16), square), [ANY] * 4 + [VMEM],
         places=(VMEM, HBM),
         scratch=[
             pltpu.VMEM((BS, BS), BF16),
-            pltpu.VMEM((BS, BS), BF16),
+            pltpu.VMEM((BS, HALF), BF16),
             pltpu.VMEM((BS, BS), BF16),
             pltpu.VMEM((TILE, BS), F32),
             pltpu.SemaphoreType.DMA((3, 4)),
         ],
         flops=4 * BS**3, moved=6_000_000,
-    )(mine, other, root, far_root)
+    )(mine, other, root, far_root, first)
     arrived = lax.all_to_all(precond, "x", 0, 0, tiled=True)
     shape = jax.ShapeDtypeStruct((ROWS, BS), F32)
     outs = call(

time: 127 us -> 125 us (0.984)
  waiting for transfers between devices: 50.8 us -> 47.3 us
  Pallas kernels: 23.7 us -> 25.7 us
    pallas_call x1 -> x3, Pallas kernels: 1.64 us -> 5.18 us  [the longest x1 2.68 us: on_device(): call(first_kernel, jax.ShapeDtypeStruct((BS, BS), F32), [ANY] * 3, scratc...]
    ppermute x1, waiting for transfers between devices: 2.25 us -> 0.01 us  [on_device(): other = lax.ppermute(mine, 'core', SWAP)]
    pallas_call x1, Pallas kernels: 7.82 us -> 6.39 us  [on_device(): call(precond_kernel, (jax.ShapeDtypeStruct((NX, ROWS, WIDTH), BF16), squa...]
  transfers between devices with their start and end apart: 8 -> 8, of which waited for: 5 -> 4; matrix products, arithmetic and copies ran while one was open for 0% -> 0% of each run, Pallas kernels for 16% -> 18%
where the time goes in v7:
time: 125 us
  waiting for transfers between devices  47.3 us (38%)
  starting transfers between devices  35.5 us (28%)
  Pallas kernels  25.7 us (21%)
  between operations  14.2 us (11%)
  local copies, waits for them, and re-layouts  1.32 us (1%)
    all_to_all x1, waiting for transfers between devices, on_device(): parts = lax.all_to_all(partial, 'z', 0, 0, tiled=True)  28.4 us
    all_gather x1, waiting for transfers between devices, on_device(): strips = lax.all_gather(strip, 'z', axis=0, tiled=True)  16.6 us
    ppermute x1, starting transfers between devices, on_device(): more = lax.ppermute(far, 'core', SWAP)  8.79 us
    ppermute x1, starting transfers between devices, on_device(): far_root = lax.ppermute(root, 'core', SWAP)  6.84 us
    all_to_all x1, starting transfers between devices, on_device(): lax.all_to_all(copies.reshape(NX * NZ, ROWS, WIDTH), ('x', 'z'), 0, 0, ti...  6.58 us
    pallas_call x1, Pallas kernels, on_device(): call(factor_kernel, (shape,) * 4, [HBM] * 5 + [ANY] * 4, scratch=[pltpu.V...  6.54 us
    pallas_call x1, Pallas kernels, on_device(): call(precond_kernel, (jax.ShapeDtypeStruct((NX, ROWS, WIDTH), BF16), squa...  6.39 us
    all_to_all x1, starting transfers between devices, on_device(): parts = lax.all_to_all(partial, 'z', 0, 0, tiled=True)  4.66 us
  transfers between devices with their start and end apart: 8, of which 4 were waited for; matrix products, arithmetic and copies ran while one was open for 0% of the time, Pallas kernels for 18%

profile of v7, /device:TPU:1, one launch (start us, length us, event | category | flops | bytes accessed | tf_op | source)
XLA Modules:
  0.0 124.7 jit_solution(6864552730069480823)
XLA Ops:
  7.2 1.2 shard_map.101
  8.4 8.8 %collective-permute-start = (bf16[128,2816]{1,0:T(8,128)(2,1)S(1)}, bf16[128,2816]{1,0:T(8,128)(2,1)S(1)}, u32[]{:S(2)}, u32[]{:S(2)}) collective-permute-start(bf16[128,2816]{1,0:T(8,128)(2,1)S(1)} %shard_map.101), channel_id=1, source_target_pairs={{0,32},{32,0},{1,33},{33,1},{2,34},{34,2},{3,35},{35,3},{4,36},{36... | collective-permute-start | bytes 2162696 | tf_op jit(solution)/shard_map/ppermute | solution.py:265
  17.2 1.2 shard_map.102.own
  18.5 0.5 collective-permute-done.more
  19.0 0.7 shard_map.103
  19.7 1.7 %shard_map.104 = bf16[8,256,256]{2,1,0:T(8,128)(2,1)} custom-call(bf16[128,2816]{1,0:T(8,128)(2,1)S(1)} %shard_map.102.own, bf16[128,2816]{1,0:T(8,128)(2,1)S(1)} %collective-permute-done.more), custom_call_target="tpu_custom_call" | custom-call | flops 268435456 | bytes 3000000 | tf_op jit(solution)/shard_map/pallas_call | solution.py:274
  21.4 4.7 %all-to-all-start = ((bf16[8,256,256]{2,1,0:T(8,128)(2,1)}), bf16[8,256,256]{2,1,0:T(8,128)(2,1)S(1)}, u32[]{:S(2)}, u32[]{:S(2)}) async-start(bf16[8,256,256]{2,1,0:T(8,128)(2,1)} %shard_map.104), calls=%async_computation | async-start | bytes 2097152 | tf_op jit(solution)/shard_map/all_to_all | solution.py:278
  26.2 0.7 all-gather.2.cloned.1.call-update
  26.8 28.4 %all-to-all-done.parts = bf16[8,256,256]{2,1,0:T(8,128)(2,1)S(1)} async-done(((bf16[8,256,256]{2,1,0:T(8,128)(2,1)}), bf16[8,256,256]{2,1,0:T(8,128)(2,1)S(1)}, u32[]{:S(2)}, u32[]{:S(2)}) %all-to-all-start) | async-done | bytes 1048608 | tf_op jit(solution)/shard_map/all_to_all | solution.py:278
  55.2 1.1 shard_map.105
  56.4 6.6 %all-to-all-start.1 = ((bf16[32,64,256]{2,1,0:T(8,128)(2,1)}), bf16[32,64,256]{2,1,0:T(8,128)(2,1)S(1)}, u32[]{:S(2)}, u32[]{:S(2)}) async-start(bf16[32,64,256]{2,1,0:T(8,128)(2,1)} %bitcast.2), calls=%async_computation.1 | async-start | bytes 2097152 | tf_op jit(solution)/shard_map/all_to_all | solution.py:291
  63.0 16.6 %all-gather.2.cloned.1.call-done.strips = bf16[1024,640]{1,0:T(8,128)(2,1)} async-done(((bf16[128,640]{1,0:T(8,128)(2,1)}), bf16[1024,640]{1,0:T(8,128)(2,1)}) %all-gather.2.cloned.1.call-update) | async-done | bytes 1310736 | tf_op jit(solution)/shard_map/all_gather | solution.py:273
  79.6 1.3 %copy-done = bf16[1024,640]{1,0:T(8,128)(2,1)S(1)} copy-done((bf16[1024,640]{1,0:T(8,128)(2,1)S(1)}, bf16[1024,640]{1,0:T(8,128)(2,1)}, u32[]{:S(2)}) %copy-start) | copy-done | bytes 1310744
  80.9 0.4 shard_map.106.root
  81.3 6.8 %collective-permute-start.2 = (bf16[1024,1024]{1,0:T(8,128)(2,1)S(1)}, bf16[1024,1024]{1,0:T(8,128)(2,1)}, u32[]{:S(2)}, u32[]{:S(2)}) collective-permute-start(bf16[1024,1024]{1,0:T(8,128)(2,1)S(1)} %shard_map.106.root), channel_id=1, source_target_pairs={{0,32},{32,0},{1,33},{33,1},{2,34},{34,2},{3,35},{35,3},{4,36},{36... | collective-permute-start | bytes 6291464 | tf_op jit(solution)/shard_map/ppermute | solution.py:286
  88.2 3.7 %shard_map.109.squared = bf16[1024,1024]{1,0:T(8,128)(2,1)} custom-call(bf16[1024,1024]{1,0:T(8,128)(2,1)S(1)} %shard_map.106.root), custom_call_target="tpu_custom_call" | custom-call | flops 2147483648 | bytes 4000000 | tf_op jit(solution)/shard_map/pallas_call | solution.py:287
  91.8 1.9 %collective-permute-start.3 = (bf16[1024,1024]{1,0:T(8,128)(2,1)}, bf16[1024,1024]{1,0:T(8,128)(2,1)}, u32[]{:S(2)}, u32[]{:S(2)}) collective-permute-start(bf16[1024,1024]{1,0:T(8,128)(2,1)} %shard_map.109.squared), channel_id=1, source_target_pairs={{0,32},{32,0},{1,33},{33,1},{2,34},{34,2},{3,35},{35,3},{4,36},{36... | collective-permute-start | bytes 6291464 | tf_op jit(solution)/shard_map/ppermute | solution.py:290
  93.7 1.1 all-to-all-done.1
  94.8 3.3 %collective-permute-start.1 = (bf16[4,512,256]{2,1,0:T(8,128)(2,1)S(1)}, bf16[4,512,256]{2,1,0:T(8,128)(2,1)S(1)}, u32[]{:S(2)}, u32[]{:S(2)}) collective-permute-start(bf16[4,512,256]{2,1,0:T(8,128)(2,1)S(1)} %bitcast.10), channel_id=1, source_target_pairs={{0,32},{32,0},{1,33},{33,1},{2,34},{34,2},{3,35},{35,3},{4,36},{36... | collective-permute-start | bytes 3145736 | tf_op jit(solution)/shard_map/ppermute | solution.py:294
  98.1 2.7 %shard_map.107.first = f32[1024,1024]{1,0:T(8,128)S(1)} custom-call(bf16[4,512,256]{2,1,0:T(8,128)(2,1)S(1)} %bitcast.11, bf16[1024,1024]{1,0:T(8,128)(2,1)S(1)} %shard_map.106.root, bf16[1024,1024]{1,0:T(8,128)(2,1)} %collective-permute-done.2.far_root), custom_call_target="tpu_custom_call" | custom-call | flops 1073741824 | bytes 3000000 | tf_op jit(solution)/shard_map/pallas_call | solution.py:296
  100.8 6.4 %shard_map.108 = (bf16[4,64,256]{2,1,0:T(8,128)(2,1)}, bf16[1024,1024]{1,0:T(8,128)(2,1)}) custom-call(bf16[4,512,256]{2,1,0:T(8,128)(2,1)S(1)} %bitcast.12, bf16[4,512,256]{2,1,0:T(8,128)(2,1)S(1)} %collective-permute-done.1.other, bf16[1024,1024]{1,0:T(8,128)(2,1)S(1)} %shard_map.106.root, bf16[1024,1024]{1,0:T(8,128)(2,1)} %collective-permute-done.2.far_root, ...), custom_call_target="tpu_custom_call" | custom-call | flops 4294967296 | bytes 6000000 | tf_op jit(solution)/shard_map/pallas_call | solution.py:307
  107.2 3.3 %all-to-all-start.2 = ((bf16[4,64,256]{2,1,0:T(8,128)(2,1)}), bf16[4,64,256]{2,1,0:T(8,128)(2,1)S(1)}, u32[]{:S(2)}, u32[]{:S(2)}) async-start(bf16[4,64,256]{2,1,0:T(8,128)(2,1)} %get-tuple-element.28), calls=%async_computation.2 | async-start | bytes 262144 | tf_op jit(solution)/shard_map/all_to_all | solution.py:319
  110.6 6.5 %shard_map.110 = (f32[64,1024]{1,0:T(8,128)}, f32[64,1024]{1,0:T(8,128)}, f32[64,1024]{1,0:T(8,128)}, f32[64,1024]{1,0:T(8,128)}) custom-call(bf16[1024,1024]{1,0:T(8,128)(2,1)} %get-tuple-element.23.stored, f32[64,1024]{1,0:T(8,128)} %bitcast.19, f32[64,1024]{1,0:T(8,128)} %bitcast.20, f32[64,1024]{1,0:T(8,128)} %bitcast.15, f32[64,1024]{1,0:T(8,128)} %bitcast.18, ...), custom_call_target="tpu_custom_call" | custom-call | flops 1073741824 | bytes 8000000 | tf_op jit(solution)/shard_map/pallas_call | solution.py:321
  117.1 0.7 convert_element_type.3
  (6 shorter events, 0.0 us)
Async XLA Ops:
  8.4 10.6 %collective-permute-start = (bf16[128,2816]{1,0:T(8,128)(2,1)S(1)}, bf16[128,2816]{1,0:T(8,128)(2,1)S(1)}, u32[]{:S(2)}, u32[]{:S(2)}) collective-permute-start(bf16[128,2816]{1,0:T(8,128)(2,1)S(1)} %shard_map.101), channel_id=1, source_target_pairs={{0,32},{32,0},{1,33},{33,1},{2,34},{34,2},{3,35},{35,3},{4,36},{36... | collective-permute-start | bytes 2162696 | tf_op jit(solution)/shard_map/ppermute | solution.py:265
  21.4 33.8 %all-to-all-start = ((bf16[8,256,256]{2,1,0:T(8,128)(2,1)}), bf16[8,256,256]{2,1,0:T(8,128)(2,1)S(1)}, u32[]{:S(2)}, u32[]{:S(2)}) async-start(bf16[8,256,256]{2,1,0:T(8,128)(2,1)} %shard_map.104), calls=%async_computation | async-start | bytes 2097152 | tf_op jit(solution)/shard_map/all_to_all | solution.py:278
  26.1 53.5 %all-gather.2.cloned.1.call-start = ((), (), s32[]{:S(2)}) async-start(), calls=%async_computation.3 | async-start | bytes 1474560 | tf_op jit(solution)/shard_map/all_gather | solution.py:273
  56.4 38.5 %all-to-all-start.1 = ((bf16[32,64,256]{2,1,0:T(8,128)(2,1)}), bf16[32,64,256]{2,1,0:T(8,128)(2,1)S(1)}, u32[]{:S(2)}, u32[]{:S(2)}) async-start(bf16[32,64,256]{2,1,0:T(8,128)(2,1)} %bitcast.2), calls=%async_computation.1 | async-start | bytes 2097152 | tf_op jit(solution)/shard_map/all_to_all | solution.py:291
  79.6 1.3 %copy-start = (bf16[1024,640]{1,0:T(8,128)(2,1)S(1)}, bf16[1024,640]{1,0:T(8,128)(2,1)}, u32[]{:S(2)}) copy-start(bf16[1024,640]{1,0:T(8,128)(2,1)} %all-gather.2.cloned.1.call-done.strips) | copy-start | bytes 3932164
  81.3 16.8 %collective-permute-start.2 = (bf16[1024,1024]{1,0:T(8,128)(2,1)S(1)}, bf16[1024,1024]{1,0:T(8,128)(2,1)}, u32[]{:S(2)}, u32[]{:S(2)}) collective-permute-start(bf16[1024,1024]{1,0:T(8,128)(2,1)S(1)} %shard_map.106.root), channel_id=1, source_target_pairs={{0,32},{32,0},{1,33},{33,1},{2,34},{34,2},{3,35},{35,3},{4,36},{36... | collective-permute-start | bytes 6291464 | tf_op jit(solution)/shard_map/ppermute | solution.py:286
  91.8 18.8 %collective-permute-start.3 = (bf16[1024,1024]{1,0:T(8,128)(2,1)}, bf16[1024,1024]{1,0:T(8,128)(2,1)}, u32[]{:S(2)}, u32[]{:S(2)}) collective-permute-start(bf16[1024,1024]{1,0:T(8,128)(2,1)} %shard_map.109.squared), channel_id=1, source_target_pairs={{0,32},{32,0},{1,33},{33,1},{2,34},{34,2},{3,35},{35,3},{4,36},{36... | collective-permute-start | bytes 6291464 | tf_op jit(solution)/shard_map/ppermute | solution.py:290
  94.8 6.0 %collective-permute-start.1 = (bf16[4,512,256]{2,1,0:T(8,128)(2,1)S(1)}, bf16[4,512,256]{2,1,0:T(8,128)(2,1)S(1)}, u32[]{:S(2)}, u32[]{:S(2)}) collective-permute-start(bf16[4,512,256]{2,1,0:T(8,128)(2,1)S(1)} %bitcast.10), channel_id=1, source_target_pairs={{0,32},{32,0},{1,33},{33,1},{2,34},{34,2},{3,35},{35,3},{4,36},{36... | collective-permute-start | bytes 3145736 | tf_op jit(solution)/shard_map/ppermute | solution.py:294
  107.2 9.9 %all-to-all-start.2 = ((bf16[4,64,256]{2,1,0:T(8,128)(2,1)}), bf16[4,64,256]{2,1,0:T(8,128)(2,1)S(1)}, u32[]{:S(2)}, u32[]{:S(2)}) async-start(bf16[4,64,256]{2,1,0:T(8,128)(2,1)} %get-tuple-element.28), calls=%async_computation.2 | async-start | bytes 262144 | tf_op jit(solution)/shard_map/all_to_all | solution.py:319
Sparse Core Ops, SparseCore 0:
  29.6 49.9 all-gather.1

commit v8 on v7

--- a/solution.py
+++ b/solution.py
@@ -24,7 +24,9 @@
 SIDE = NC * ROWS
 OFF = 3
 SLABS = NX * ROWS
-STRIP = (OFF + 2) * SIDE
+STRIP = (OFF + 1) * SIDE
+EXTRA = ROWS * SIDE // STRIP
+TALL = SIDE + EXTRA
 TOK = ("z", "core")
 HID = ("y", "x")
 SWAP = [(0, 1), (1, 0)]
@@ -87,8 +89,16 @@
         rows = at(side * ROWS, ROWS, ROWS)
         shard[rows, :HALF] = given[:ROWS, ROOT:]
         shard[rows, HALF:] = given[ROWS:, ROOT:]
-    for k in range(OFF + 2):
-        strip[:, k * SIDE : (k + 1) * SIDE] = shard[:, at(lax.rem(z + k, NZ) * SIDE, SIDE, SIDE)]
+    def block(k):
+        return shard[:, at(lax.rem(z + k, NZ) * SIDE, SIDE, SIDE)]
+
+    for k in range(OFF + 1):
+        strip[:SIDE, k * SIDE : (k + 1) * SIDE] = block(k)
+
+    across = block(OFF + 1).astype(F32)
+    half = jnp.where(z < NZ // 2, across.T[:ROWS], across[ROWS:]).astype(BF16)
+    for k in range(OFF + 1):
+        strip[SIDE:, k * SIDE : (k + 1) * SIDE] = half[k * EXTRA : (k + 1) * EXTRA]
 
 
 def partial_kernel(own, more, out):
@@ -113,15 +123,25 @@
 
 
 def root_kernel(strips, root):
+    def cut(z):
+        return slice(z * SIDE, (z + 1) * SIDE)
+
     for z in range(NZ):
-        own = slice(z * SIDE, (z + 1) * SIDE)
-        for k in range(OFF + 2):
-            j = (z + k) % NZ
-            there = slice(j * SIDE, (j + 1) * SIDE)
-            piece = strips[own, k * SIDE : (k + 1) * SIDE]
-            root[own, there] = piece
-            if 0 < k <= OFF:
-                root[there, own] = piece.T
+        for k in range(OFF + 1):
+            there = cut((z + k) % NZ)
+            piece = strips[z * TALL : z * TALL + SIDE, k * SIDE : (k + 1) * SIDE]
+            root[cut(z), there] = piece
+            if k:
+                root[there, cut(z)] = piece.T
+    for z in range(NZ // 2):
+        pieces = [
+            strips[home * TALL + SIDE : (home + 1) * TALL, k * SIDE : (k + 1) * SIDE]
+            for home in (z, z + NZ // 2)
+            for k in range(OFF + 1)
+        ]
+        whole = jnp.concatenate(pieces, axis=0)
+        root[cut(z + NZ // 2), cut(z)] = whole
+        root[cut(z), cut(z + NZ // 2)] = whole.T
 
 
 def first_kernel(mine, root, far_root, out, upper, left, sems):
@@ -266,7 +286,7 @@
     own = pack(0)
     more, own = lax.optimization_barrier((more, own))
     strip = call(
-        strip_kernel, jax.ShapeDtypeStruct((SIDE, STRIP), BF16), [VMEM, VMEM],
+        strip_kernel, jax.ShapeDtypeStruct((TALL, STRIP), BF16), [VMEM, VMEM],
         scratch=[pltpu.VMEM((SIDE, BS), BF16)], moved=500_000,
     )(own, more)
     strip, more = lax.optimization_barrier((strip, more))

time: 125 us -> 124 us (level)
  waiting for transfers between devices: 47.3 us -> 43.9 us
    all_gather x1, waiting for transfers between devices: 16.6 us -> 14.1 us  [on_device(): strips = lax.all_gather(strip, 'z', axis=0, tiled=True)]
where the time goes in v8:
time: 124 us; the launch traced here: 122 us
  waiting for transfers between devices  43.9 us (35%)
  starting transfers between devices  36.7 us (30%)
  Pallas kernels  25.8 us (21%)
  between operations  14.1 us (11%)
  local copies, waits for them, and re-layouts  1.27 us (1%)
    all_to_all x1, waiting for transfers between devices, on_device(): parts = lax.all_to_all(partial, 'z', 0, 0, tiled=True)  28.4 us
    all_gather x1, waiting for transfers between devices, on_device(): strips = lax.all_gather(strip, 'z', axis=0, tiled=True)  14.1 us
    ppermute x1, starting transfers between devices, on_device(): more = lax.ppermute(far, 'core', SWAP)  8.79 us
    ppermute x1, starting transfers between devices, on_device(): far_root = lax.ppermute(root, 'core', SWAP)  6.68 us
    all_to_all x1, starting transfers between devices, on_device(): lax.all_to_all(copies.reshape(NX * NZ, ROWS, WIDTH), ('x', 'z'), 0, 0, ti...  6.59 us
    pallas_call x1, Pallas kernels, on_device(): call(factor_kernel, (shape,) * 4, [HBM] * 5 + [ANY] * 4, scratch=[pltpu.V...  6.53 us
    pallas_call x1, Pallas kernels, on_device(): call(precond_kernel, (jax.ShapeDtypeStruct((NX, ROWS, WIDTH), BF16), squa...  6.39 us
    all_to_all x1, starting transfers between devices, on_device(): parts = lax.all_to_all(partial, 'z', 0, 0, tiled=True)  4.66 us
  transfers between devices with their start and end apart: 8, of which 4 were waited for; matrix products, arithmetic and copies ran while one was open for 0% of the time, Pallas kernels for 18%

profile of v8, /device:TPU:1, one launch (start us, length us, event | category | flops | bytes accessed | tf_op | source)
XLA Modules:
  0.0 122.5 jit_solution(9284983256761637650)
XLA Ops:
  7.2 1.2 %shard_map.101 = bf16[128,2816]{1,0:T(8,128)(2,1)S(1)} custom-call(bf16[128,4096]{1,0:T(8,128)(2,1)} %act.3, bf16[128,256]{1,0:T(8,128)(2,1)} %cot.3, f32[64,1024]{1,0:T(8,128)} %bitcast.13, f32[64,1024]{1,0:T(8,128)} %bitcast.16), custom_call_target="tpu_custom_call" | custom-call | flops 100000 | bytes 1000000 | tf_op jit(solution)/shard_map/pallas_call | solution.py:277
  8.4 8.8 %collective-permute-start = (bf16[128,2816]{1,0:T(8,128)(2,1)S(1)}, bf16[128,2816]{1,0:T(8,128)(2,1)S(1)}, u32[]{:S(2)}, u32[]{:S(2)}) collective-permute-start(bf16[128,2816]{1,0:T(8,128)(2,1)S(1)} %shard_map.101), channel_id=1, source_target_pairs={{0,32},{32,0},{1,33},{33,1},{2,34},{34,2},{3,35},{35,3},{4,36},{36... | collective-permute-start | bytes 2162696 | tf_op jit(solution)/shard_map/ppermute | solution.py:285
  17.2 1.2 %shard_map.102.own = bf16[128,2816]{1,0:T(8,128)(2,1)S(1)} custom-call(bf16[128,4096]{1,0:T(8,128)(2,1)} %act.3, bf16[128,256]{1,0:T(8,128)(2,1)} %cot.3, f32[64,1024]{1,0:T(8,128)} %bitcast.14, f32[64,1024]{1,0:T(8,128)} %bitcast.17), custom_call_target="tpu_custom_call" | custom-call | flops 100000 | bytes 1000000 | tf_op jit(solution)/shard_map/pallas_call | solution.py:277
  18.5 0.5 collective-permute-done.more
  19.0 0.8 shard_map.103
  19.8 1.7 %shard_map.104 = bf16[8,256,256]{2,1,0:T(8,128)(2,1)} custom-call(bf16[128,2816]{1,0:T(8,128)(2,1)S(1)} %shard_map.102.own, bf16[128,2816]{1,0:T(8,128)(2,1)S(1)} %collective-permute-done.more), custom_call_target="tpu_custom_call" | custom-call | flops 268435456 | bytes 3000000 | tf_op jit(solution)/shard_map/pallas_call | solution.py:294
  21.5 4.7 %all-to-all-start = ((bf16[8,256,256]{2,1,0:T(8,128)(2,1)}), bf16[8,256,256]{2,1,0:T(8,128)(2,1)S(1)}, u32[]{:S(2)}, u32[]{:S(2)}) async-start(bf16[8,256,256]{2,1,0:T(8,128)(2,1)} %shard_map.104), calls=%async_computation | async-start | bytes 2097152 | tf_op jit(solution)/shard_map/all_to_all | solution.py:298
  26.2 0.7 all-gather.2.cloned.1.call-update
  26.9 28.4 %all-to-all-done.parts = bf16[8,256,256]{2,1,0:T(8,128)(2,1)S(1)} async-done(((bf16[8,256,256]{2,1,0:T(8,128)(2,1)}), bf16[8,256,256]{2,1,0:T(8,128)(2,1)S(1)}, u32[]{:S(2)}, u32[]{:S(2)}) %all-to-all-start) | async-done | bytes 1048608 | tf_op jit(solution)/shard_map/all_to_all | solution.py:298
  55.3 1.1 shard_map.105
  56.4 6.6 %all-to-all-start.1 = ((bf16[32,64,256]{2,1,0:T(8,128)(2,1)}), bf16[32,64,256]{2,1,0:T(8,128)(2,1)S(1)}, u32[]{:S(2)}, u32[]{:S(2)}) async-start(bf16[32,64,256]{2,1,0:T(8,128)(2,1)} %bitcast.2), calls=%async_computation.1 | async-start | bytes 2097152 | tf_op jit(solution)/shard_map/all_to_all | solution.py:311
  63.0 14.1 %all-gather.2.cloned.1.call-done.strips = bf16[1152,512]{1,0:T(8,128)(2,1)} async-done(((bf16[144,512]{1,0:T(8,128)(2,1)}), bf16[1152,512]{1,0:T(8,128)(2,1)}) %all-gather.2.cloned.1.call-update) | async-done | bytes 1179664 | tf_op jit(solution)/shard_map/all_gather | solution.py:293
  77.1 1.3 %copy-done = bf16[1152,512]{1,0:T(8,128)(2,1)S(1)} copy-done((bf16[1152,512]{1,0:T(8,128)(2,1)S(1)}, bf16[1152,512]{1,0:T(8,128)(2,1)}, u32[]{:S(2)}) %copy-start) | copy-done | bytes 1179672
  78.3 0.4 shard_map.106.root
  78.8 6.7 %collective-permute-start.2 = (bf16[1024,1024]{1,0:T(8,128)(2,1)S(1)}, bf16[1024,1024]{1,0:T(8,128)(2,1)}, u32[]{:S(2)}, u32[]{:S(2)}) collective-permute-start(bf16[1024,1024]{1,0:T(8,128)(2,1)S(1)} %shard_map.106.root), channel_id=1, source_target_pairs={{0,32},{32,0},{1,33},{33,1},{2,34},{34,2},{3,35},{35,3},{4,36},{36... | collective-permute-start | bytes 6291464 | tf_op jit(solution)/shard_map/ppermute | solution.py:306
  85.4 3.7 %shard_map.109.squared = bf16[1024,1024]{1,0:T(8,128)(2,1)} custom-call(bf16[1024,1024]{1,0:T(8,128)(2,1)S(1)} %shard_map.106.root), custom_call_target="tpu_custom_call" | custom-call | flops 2147483648 | bytes 4000000 | tf_op jit(solution)/shard_map/pallas_call | solution.py:307
  89.1 1.9 %collective-permute-start.3 = (bf16[1024,1024]{1,0:T(8,128)(2,1)}, bf16[1024,1024]{1,0:T(8,128)(2,1)}, u32[]{:S(2)}, u32[]{:S(2)}) collective-permute-start(bf16[1024,1024]{1,0:T(8,128)(2,1)} %shard_map.109.squared), channel_id=1, source_target_pairs={{0,32},{32,0},{1,33},{33,1},{2,34},{34,2},{3,35},{35,3},{4,36},{36... | collective-permute-start | bytes 6291464 | tf_op jit(solution)/shard_map/ppermute | solution.py:310
  91.0 0.2 all-to-all-done.1
  91.2 4.4 %collective-permute-start.1 = (bf16[4,512,256]{2,1,0:T(8,128)(2,1)S(1)}, bf16[4,512,256]{2,1,0:T(8,128)(2,1)S(1)}, u32[]{:S(2)}, u32[]{:S(2)}) collective-permute-start(bf16[4,512,256]{2,1,0:T(8,128)(2,1)S(1)} %bitcast.10), channel_id=1, source_target_pairs={{0,32},{32,0},{1,33},{33,1},{2,34},{34,2},{3,35},{35,3},{4,36},{36... | collective-permute-start | bytes 3145736 | tf_op jit(solution)/shard_map/ppermute | solution.py:314
  95.7 2.7 %shard_map.107.first = f32[1024,1024]{1,0:T(8,128)S(1)} custom-call(bf16[4,512,256]{2,1,0:T(8,128)(2,1)S(1)} %bitcast.11, bf16[1024,1024]{1,0:T(8,128)(2,1)S(1)} %shard_map.106.root, bf16[1024,1024]{1,0:T(8,128)(2,1)} %collective-permute-done.2.far_root), custom_call_target="tpu_custom_call" | custom-call | flops 1073741824 | bytes 3000000 | tf_op jit(solution)/shard_map/pallas_call | solution.py:316
  98.4 6.4 %shard_map.108 = (bf16[4,64,256]{2,1,0:T(8,128)(2,1)}, bf16[1024,1024]{1,0:T(8,128)(2,1)}) custom-call(bf16[4,512,256]{2,1,0:T(8,128)(2,1)S(1)} %bitcast.12, bf16[4,512,256]{2,1,0:T(8,128)(2,1)S(1)} %collective-permute-done.1.other, bf16[1024,1024]{1,0:T(8,128)(2,1)S(1)} %shard_map.106.root, bf16[1024,1024]{1,0:T(8,128)(2,1)} %collective-permute-done.2.far_root, ...), custom_call_target="tpu_custom_call" | custom-call | flops 4294967296 | bytes 6000000 | tf_op jit(solution)/shard_map/pallas_call | solution.py:327
  104.8 3.6 %all-to-all-start.2 = ((bf16[4,64,256]{2,1,0:T(8,128)(2,1)}), bf16[4,64,256]{2,1,0:T(8,128)(2,1)S(1)}, u32[]{:S(2)}, u32[]{:S(2)}) async-start(bf16[4,64,256]{2,1,0:T(8,128)(2,1)} %get-tuple-element.28), calls=%async_computation.2 | async-start | bytes 262144 | tf_op jit(solution)/shard_map/all_to_all | solution.py:339
  108.4 6.5 %shard_map.110 = (f32[64,1024]{1,0:T(8,128)}, f32[64,1024]{1,0:T(8,128)}, f32[64,1024]{1,0:T(8,128)}, f32[64,1024]{1,0:T(8,128)}) custom-call(bf16[1024,1024]{1,0:T(8,128)(2,1)} %get-tuple-element.23.stored, f32[64,1024]{1,0:T(8,128)} %bitcast.19, f32[64,1024]{1,0:T(8,128)} %bitcast.20, f32[64,1024]{1,0:T(8,128)} %bitcast.15, f32[64,1024]{1,0:T(8,128)} %bitcast.18, ...), custom_call_target="tpu_custom_call" | custom-call | flops 1073741824 | bytes 8000000 | tf_op jit(solution)/shard_map/pallas_call | solution.py:341
  114.9 0.7 convert_element_type.3
  (6 shorter events, 0.0 us)
Async XLA Ops:
  8.4 10.6 %collective-permute-start = (bf16[128,2816]{1,0:T(8,128)(2,1)S(1)}, bf16[128,2816]{1,0:T(8,128)(2,1)S(1)}, u32[]{:S(2)}, u32[]{:S(2)}) collective-permute-start(bf16[128,2816]{1,0:T(8,128)(2,1)S(1)} %shard_map.101), channel_id=1, source_target_pairs={{0,32},{32,0},{1,33},{33,1},{2,34},{34,2},{3,35},{35,3},{4,36},{36... | collective-permute-start | bytes 2162696 | tf_op jit(solution)/shard_map/ppermute | solution.py:285
  21.5 33.8 %all-to-all-start = ((bf16[8,256,256]{2,1,0:T(8,128)(2,1)}), bf16[8,256,256]{2,1,0:T(8,128)(2,1)S(1)}, u32[]{:S(2)}, u32[]{:S(2)}) async-start(bf16[8,256,256]{2,1,0:T(8,128)(2,1)} %shard_map.104), calls=%async_computation | async-start | bytes 2097152 | tf_op jit(solution)/shard_map/all_to_all | solution.py:298
  26.1 50.9 %all-gather.2.cloned.1.call-start = ((), (), s32[]{:S(2)}) async-start(), calls=%async_computation.3 | async-start | bytes 1327104 | tf_op jit(solution)/shard_map/all_gather | solution.py:293
  56.4 34.8 %all-to-all-start.1 = ((bf16[32,64,256]{2,1,0:T(8,128)(2,1)}), bf16[32,64,256]{2,1,0:T(8,128)(2,1)S(1)}, u32[]{:S(2)}, u32[]{:S(2)}) async-start(bf16[32,64,256]{2,1,0:T(8,128)(2,1)} %bitcast.2), calls=%async_computation.1 | async-start | bytes 2097152 | tf_op jit(solution)/shard_map/all_to_all | solution.py:311
  77.1 1.3 %copy-start = (bf16[1152,512]{1,0:T(8,128)(2,1)S(1)}, bf16[1152,512]{1,0:T(8,128)(2,1)}, u32[]{:S(2)}) copy-start(bf16[1152,512]{1,0:T(8,128)(2,1)} %all-gather.2.cloned.1.call-done.strips) | copy-start | bytes 3538948
  78.8 16.9 %collective-permute-start.2 = (bf16[1024,1024]{1,0:T(8,128)(2,1)S(1)}, bf16[1024,1024]{1,0:T(8,128)(2,1)}, u32[]{:S(2)}, u32[]{:S(2)}) collective-permute-start(bf16[1024,1024]{1,0:T(8,128)(2,1)S(1)} %shard_map.106.root), channel_id=1, source_target_pairs={{0,32},{32,0},{1,33},{33,1},{2,34},{34,2},{3,35},{35,3},{4,36},{36... | collective-permute-start | bytes 6291464 | tf_op jit(solution)/shard_map/ppermute | solution.py:306
  89.1 19.3 %collective-permute-start.3 = (bf16[1024,1024]{1,0:T(8,128)(2,1)}, bf16[1024,1024]{1,0:T(8,128)(2,1)}, u32[]{:S(2)}, u32[]{:S(2)}) collective-permute-start(bf16[1024,1024]{1,0:T(8,128)(2,1)} %shard_map.109.squared), channel_id=1, source_target_pairs={{0,32},{32,0},{1,33},{33,1},{2,34},{34,2},{3,35},{35,3},{4,36},{36... | collective-permute-start | bytes 6291464 | tf_op jit(solution)/shard_map/ppermute | solution.py:310
  91.2 7.1 %collective-permute-start.1 = (bf16[4,512,256]{2,1,0:T(8,128)(2,1)S(1)}, bf16[4,512,256]{2,1,0:T(8,128)(2,1)S(1)}, u32[]{:S(2)}, u32[]{:S(2)}) collective-permute-start(bf16[4,512,256]{2,1,0:T(8,128)(2,1)S(1)} %bitcast.10), channel_id=1, source_target_pairs={{0,32},{32,0},{1,33},{33,1},{2,34},{34,2},{3,35},{35,3},{4,36},{36... | collective-permute-start | bytes 3145736 | tf_op jit(solution)/shard_map/ppermute | solution.py:314
  104.8 10.1 %all-to-all-start.2 = ((bf16[4,64,256]{2,1,0:T(8,128)(2,1)}), bf16[4,64,256]{2,1,0:T(8,128)(2,1)S(1)}, u32[]{:S(2)}, u32[]{:S(2)}) async-start(bf16[4,64,256]{2,1,0:T(8,128)(2,1)} %get-tuple-element.28), calls=%async_computation.2 | async-start | bytes 262144 | tf_op jit(solution)/shard_map/all_to_all | solution.py:339
Sparse Core Ops, SparseCore 0:
  29.6 47.3 all-gather.1

commit v9 on v8

--- a/solution.py
+++ b/solution.py
@@ -285,16 +285,16 @@
     more = lax.ppermute(far, "core", SWAP)
     own = pack(0)
     more, own = lax.optimization_barrier((more, own))
+    partial = call(
+        partial_kernel, jax.ShapeDtypeStruct((NZ, SLABS, WIDTH), BF16), [VMEM, VMEM],
+        flops=2 * 256 * 2048 * 256, moved=3_000_000,
+    )(own, more)
+    partial, more = lax.optimization_barrier((partial, more))
     strip = call(
         strip_kernel, jax.ShapeDtypeStruct((TALL, STRIP), BF16), [VMEM, VMEM],
         scratch=[pltpu.VMEM((SIDE, BS), BF16)], moved=500_000,
     )(own, more)
-    strip, more = lax.optimization_barrier((strip, more))
     strips = lax.all_gather(strip, "z", axis=0, tiled=True)
-    partial = call(
-        partial_kernel, jax.ShapeDtypeStruct((NZ, SLABS, WIDTH), BF16), [VMEM, VMEM],
-        flops=2 * 256 * 2048 * 256, moved=3_000_000,
-    )(own, more)
     parts = lax.all_to_all(partial, "z", 0, 0, tiled=True)
     copies = call(
         sum_kernel, jax.ShapeDtypeStruct((NX, NZ, ROWS, WIDTH), BF16), [VMEM],

time: 124 us -> 123 us (level)
  transfers between devices with their start and end apart: 8 -> 8, of which waited for: 4 -> 4; matrix products, arithmetic and copies ran while one was open for 0% -> 0% of each run, Pallas kernels for 18% -> 19%
where the time goes in v9:
time: 123 us; the launch traced here: 122 us
  waiting for transfers between devices  43.2 us (35%)
  starting transfers between devices  36.5 us (30%)
  Pallas kernels  25.8 us (21%)
  between operations  14.1 us (11%)
  local copies, waits for them, and re-layouts  1.27 us (1%)
    all_to_all x1, waiting for transfers between devices, on_device(): parts = lax.all_to_all(partial, 'z', 0, 0, tiled=True)  28.2 us
    all_gather x1, waiting for transfers between devices, on_device(): strips = lax.all_gather(strip, 'z', axis=0, tiled=True)  14.1 us
    ppermute x1, starting transfers between devices, on_device(): more = lax.ppermute(far, 'core', SWAP)  8.79 us
    ppermute x1, starting transfers between devices, on_device(): far_root = lax.ppermute(root, 'core', SWAP)  6.72 us
    all_to_all x1, starting transfers between devices, on_device(): lax.all_to_all(copies.reshape(NX * NZ, ROWS, WIDTH), ('x', 'z'), 0, 0, ti...  6.59 us
    pallas_call x1, Pallas kernels, on_device(): call(factor_kernel, (shape,) * 4, [HBM] * 5 + [ANY] * 4, scratch=[pltpu.V...  6.53 us
    pallas_call x1, Pallas kernels, on_device(): call(precond_kernel, (jax.ShapeDtypeStruct((NX, ROWS, WIDTH), BF16), squa...  6.38 us
    all_to_all x1, starting transfers between devices, on_device(): parts = lax.all_to_all(partial, 'z', 0, 0, tiled=True)  4.66 us
  transfers between devices with their start and end apart: 8, of which 4 were waited for; matrix products, arithmetic and copies ran while one was open for 0% of the time, Pallas kernels for 19%

profile of v9, /device:TPU:1, one launch (start us, length us, event | category | flops | bytes accessed | tf_op | source)
XLA Modules:
  0.0 121.7 jit_solution(13326308561646983661)
XLA Ops:
  7.2 1.2 %shard_map.101 = bf16[128,2816]{1,0:T(8,128)(2,1)S(1)} custom-call(bf16[128,4096]{1,0:T(8,128)(2,1)} %act.3, bf16[128,256]{1,0:T(8,128)(2,1)} %cot.3, f32[64,1024]{1,0:T(8,128)} %bitcast.13, f32[64,1024]{1,0:T(8,128)} %bitcast.16), custom_call_target="tpu_custom_call" | custom-call | flops 100000 | bytes 1000000 | tf_op jit(solution)/shard_map/pallas_call | solution.py:277
  8.4 8.8 %collective-permute-start = (bf16[128,2816]{1,0:T(8,128)(2,1)S(1)}, bf16[128,2816]{1,0:T(8,128)(2,1)S(1)}, u32[]{:S(2)}, u32[]{:S(2)}) collective-permute-start(bf16[128,2816]{1,0:T(8,128)(2,1)S(1)} %shard_map.101), channel_id=1, source_target_pairs={{0,32},{32,0},{1,33},{33,1},{2,34},{34,2},{3,35},{35,3},{4,36},{36... | collective-permute-start | bytes 2162696 | tf_op jit(solution)/shard_map/ppermute | solution.py:285
  17.2 1.2 %shard_map.102.own = bf16[128,2816]{1,0:T(8,128)(2,1)S(1)} custom-call(bf16[128,4096]{1,0:T(8,128)(2,1)} %act.3, bf16[128,256]{1,0:T(8,128)(2,1)} %cot.3, f32[64,1024]{1,0:T(8,128)} %bitcast.14, f32[64,1024]{1,0:T(8,128)} %bitcast.17), custom_call_target="tpu_custom_call" | custom-call | flops 100000 | bytes 1000000 | tf_op jit(solution)/shard_map/pallas_call | solution.py:277
  18.5 0.5 collective-permute-done.more
  19.0 1.7 %shard_map.103 = bf16[8,256,256]{2,1,0:T(8,128)(2,1)} custom-call(bf16[128,2816]{1,0:T(8,128)(2,1)S(1)} %shard_map.102.own, bf16[128,2816]{1,0:T(8,128)(2,1)S(1)} %collective-permute-done.more), custom_call_target="tpu_custom_call" | custom-call | flops 268435456 | bytes 3000000 | tf_op jit(solution)/shard_map/pallas_call | solution.py:288
  20.7 4.7 %all-to-all-start = ((bf16[8,256,256]{2,1,0:T(8,128)(2,1)}), bf16[8,256,256]{2,1,0:T(8,128)(2,1)S(1)}, u32[]{:S(2)}, u32[]{:S(2)}) async-start(bf16[8,256,256]{2,1,0:T(8,128)(2,1)} %shard_map.103), calls=%async_computation | async-start | bytes 2097152 | tf_op jit(solution)/shard_map/all_to_all | solution.py:298
  25.4 0.0 all-gather.2.cloned.1.call-start
  25.4 0.8 shard_map.105
  26.2 28.2 %all-to-all-done.parts = bf16[8,256,256]{2,1,0:T(8,128)(2,1)S(1)} async-done(((bf16[8,256,256]{2,1,0:T(8,128)(2,1)}), bf16[8,256,256]{2,1,0:T(8,128)(2,1)S(1)}, u32[]{:S(2)}, u32[]{:S(2)}) %all-to-all-start) | async-done | bytes 1048608 | tf_op jit(solution)/shard_map/all_to_all | solution.py:298
  54.5 1.1 shard_map.104
  55.6 6.6 %all-to-all-start.1 = ((bf16[32,64,256]{2,1,0:T(8,128)(2,1)}), bf16[32,64,256]{2,1,0:T(8,128)(2,1)S(1)}, u32[]{:S(2)}, u32[]{:S(2)}) async-start(bf16[32,64,256]{2,1,0:T(8,128)(2,1)} %bitcast.2), calls=%async_computation.1 | async-start | bytes 2097152 | tf_op jit(solution)/shard_map/all_to_all | solution.py:311
  62.2 14.1 %all-gather.2.cloned.1.call-done.strips = bf16[1152,512]{1,0:T(8,128)(2,1)} async-done(((bf16[144,512]{1,0:T(8,128)(2,1)}), bf16[1152,512]{1,0:T(8,128)(2,1)}) %all-gather.2.cloned.1.call-update) | async-done | bytes 1179664 | tf_op jit(solution)/shard_map/all_gather | solution.py:297
  76.3 1.3 %copy-done = bf16[1152,512]{1,0:T(8,128)(2,1)S(1)} copy-done((bf16[1152,512]{1,0:T(8,128)(2,1)S(1)}, bf16[1152,512]{1,0:T(8,128)(2,1)}, u32[]{:S(2)}) %copy-start) | copy-done | bytes 1179672
  77.5 0.4 shard_map.106.root
  78.0 6.7 %collective-permute-start.2 = (bf16[1024,1024]{1,0:T(8,128)(2,1)S(1)}, bf16[1024,1024]{1,0:T(8,128)(2,1)}, u32[]{:S(2)}, u32[]{:S(2)}) collective-permute-start(bf16[1024,1024]{1,0:T(8,128)(2,1)S(1)} %shard_map.106.root), channel_id=1, source_target_pairs={{0,32},{32,0},{1,33},{33,1},{2,34},{34,2},{3,35},{35,3},{4,36},{36... | collective-permute-start | bytes 6291464 | tf_op jit(solution)/shard_map/ppermute | solution.py:306
  84.7 3.7 %shard_map.109.squared = bf16[1024,1024]{1,0:T(8,128)(2,1)} custom-call(bf16[1024,1024]{1,0:T(8,128)(2,1)S(1)} %shard_map.106.root), custom_call_target="tpu_custom_call" | custom-call | flops 2147483648 | bytes 4000000 | tf_op jit(solution)/shard_map/pallas_call | solution.py:307
  88.4 1.9 %collective-permute-start.3 = (bf16[1024,1024]{1,0:T(8,128)(2,1)}, bf16[1024,1024]{1,0:T(8,128)(2,1)}, u32[]{:S(2)}, u32[]{:S(2)}) collective-permute-start(bf16[1024,1024]{1,0:T(8,128)(2,1)} %shard_map.109.squared), channel_id=1, source_target_pairs={{0,32},{32,0},{1,33},{33,1},{2,34},{34,2},{3,35},{35,3},{4,36},{36... | collective-permute-start | bytes 6291464 | tf_op jit(solution)/shard_map/ppermute | solution.py:310
  90.3 0.4 all-to-all-done.1
  90.6 4.2 %collective-permute-start.1 = (bf16[4,512,256]{2,1,0:T(8,128)(2,1)S(1)}, bf16[4,512,256]{2,1,0:T(8,128)(2,1)S(1)}, u32[]{:S(2)}, u32[]{:S(2)}) collective-permute-start(bf16[4,512,256]{2,1,0:T(8,128)(2,1)S(1)} %bitcast.10), channel_id=1, source_target_pairs={{0,32},{32,0},{1,33},{33,1},{2,34},{34,2},{3,35},{35,3},{4,36},{36... | collective-permute-start | bytes 3145736 | tf_op jit(solution)/shard_map/ppermute | solution.py:314
  94.9 2.7 %shard_map.107.first = f32[1024,1024]{1,0:T(8,128)S(1)} custom-call(bf16[4,512,256]{2,1,0:T(8,128)(2,1)S(1)} %bitcast.11, bf16[1024,1024]{1,0:T(8,128)(2,1)S(1)} %shard_map.106.root, bf16[1024,1024]{1,0:T(8,128)(2,1)} %collective-permute-done.2.far_root), custom_call_target="tpu_custom_call" | custom-call | flops 1073741824 | bytes 3000000 | tf_op jit(solution)/shard_map/pallas_call | solution.py:316
  97.6 6.4 %shard_map.108 = (bf16[4,64,256]{2,1,0:T(8,128)(2,1)}, bf16[1024,1024]{1,0:T(8,128)(2,1)}) custom-call(bf16[4,512,256]{2,1,0:T(8,128)(2,1)S(1)} %bitcast.12, bf16[4,512,256]{2,1,0:T(8,128)(2,1)S(1)} %collective-permute-done.1.other, bf16[1024,1024]{1,0:T(8,128)(2,1)S(1)} %shard_map.106.root, bf16[1024,1024]{1,0:T(8,128)(2,1)} %collective-permute-done.2.far_root, ...), custom_call_target="tpu_custom_call" | custom-call | flops 4294967296 | bytes 6000000 | tf_op jit(solution)/shard_map/pallas_call | solution.py:327
  104.0 3.6 %all-to-all-start.2 = ((bf16[4,64,256]{2,1,0:T(8,128)(2,1)}), bf16[4,64,256]{2,1,0:T(8,128)(2,1)S(1)}, u32[]{:S(2)}, u32[]{:S(2)}) async-start(bf16[4,64,256]{2,1,0:T(8,128)(2,1)} %get-tuple-element.28), calls=%async_computation.2 | async-start | bytes 262144 | tf_op jit(solution)/shard_map/all_to_all | solution.py:339
  107.6 6.5 %shard_map.110 = (f32[64,1024]{1,0:T(8,128)}, f32[64,1024]{1,0:T(8,128)}, f32[64,1024]{1,0:T(8,128)}, f32[64,1024]{1,0:T(8,128)}) custom-call(bf16[1024,1024]{1,0:T(8,128)(2,1)} %get-tuple-element.23.stored, f32[64,1024]{1,0:T(8,128)} %bitcast.19, f32[64,1024]{1,0:T(8,128)} %bitcast.20, f32[64,1024]{1,0:T(8,128)} %bitcast.15, f32[64,1024]{1,0:T(8,128)} %bitcast.18, ...), custom_call_target="tpu_custom_call" | custom-call | flops 1073741824 | bytes 8000000 | tf_op jit(solution)/shard_map/pallas_call | solution.py:341
  114.1 0.7 convert_element_type.3
  (6 shorter events, 0.0 us)
Async XLA Ops:
  8.4 10.6 %collective-permute-start = (bf16[128,2816]{1,0:T(8,128)(2,1)S(1)}, bf16[128,2816]{1,0:T(8,128)(2,1)S(1)}, u32[]{:S(2)}, u32[]{:S(2)}) collective-permute-start(bf16[128,2816]{1,0:T(8,128)(2,1)S(1)} %shard_map.101), channel_id=1, source_target_pairs={{0,32},{32,0},{1,33},{33,1},{2,34},{34,2},{3,35},{35,3},{4,36},{36... | collective-permute-start | bytes 2162696 | tf_op jit(solution)/shard_map/ppermute | solution.py:285
  20.7 33.8 %all-to-all-start = ((bf16[8,256,256]{2,1,0:T(8,128)(2,1)}), bf16[8,256,256]{2,1,0:T(8,128)(2,1)S(1)}, u32[]{:S(2)}, u32[]{:S(2)}) async-start(bf16[8,256,256]{2,1,0:T(8,128)(2,1)} %shard_map.103), calls=%async_computation | async-start | bytes 2097152 | tf_op jit(solution)/shard_map/all_to_all | solution.py:298
  25.4 50.9 %all-gather.2.cloned.1.call-start = ((), (), s32[]{:S(2)}) async-start(), calls=%async_computation.3 | async-start | bytes 1327104 | tf_op jit(solution)/shard_map/all_gather | solution.py:297
  55.6 35.0 %all-to-all-start.1 = ((bf16[32,64,256]{2,1,0:T(8,128)(2,1)}), bf16[32,64,256]{2,1,0:T(8,128)(2,1)S(1)}, u32[]{:S(2)}, u32[]{:S(2)}) async-start(bf16[32,64,256]{2,1,0:T(8,128)(2,1)} %bitcast.2), calls=%async_computation.1 | async-start | bytes 2097152 | tf_op jit(solution)/shard_map/all_to_all | solution.py:311
  76.3 1.3 %copy-start = (bf16[1152,512]{1,0:T(8,128)(2,1)S(1)}, bf16[1152,512]{1,0:T(8,128)(2,1)}, u32[]{:S(2)}) copy-start(bf16[1152,512]{1,0:T(8,128)(2,1)} %all-gather.2.cloned.1.call-done.strips) | copy-start | bytes 3538948
  78.0 16.9 %collective-permute-start.2 = (bf16[1024,1024]{1,0:T(8,128)(2,1)S(1)}, bf16[1024,1024]{1,0:T(8,128)(2,1)}, u32[]{:S(2)}, u32[]{:S(2)}) collective-permute-start(bf16[1024,1024]{1,0:T(8,128)(2,1)S(1)} %shard_map.106.root), channel_id=1, source_target_pairs={{0,32},{32,0},{1,33},{33,1},{2,34},{34,2},{3,35},{35,3},{4,36},{36... | collective-permute-start | bytes 6291464 | tf_op jit(solution)/shard_map/ppermute | solution.py:306
  88.4 19.2 %collective-permute-start.3 = (bf16[1024,1024]{1,0:T(8,128)(2,1)}, bf16[1024,1024]{1,0:T(8,128)(2,1)}, u32[]{:S(2)}, u32[]{:S(2)}) collective-permute-start(bf16[1024,1024]{1,0:T(8,128)(2,1)} %shard_map.109.squared), channel_id=1, source_target_pairs={{0,32},{32,0},{1,33},{33,1},{2,34},{34,2},{3,35},{35,3},{4,36},{36... | collective-permute-start | bytes 6291464 | tf_op jit(solution)/shard_map/ppermute | solution.py:310
  90.6 6.9 %collective-permute-start.1 = (bf16[4,512,256]{2,1,0:T(8,128)(2,1)S(1)}, bf16[4,512,256]{2,1,0:T(8,128)(2,1)S(1)}, u32[]{:S(2)}, u32[]{:S(2)}) collective-permute-start(bf16[4,512,256]{2,1,0:T(8,128)(2,1)S(1)} %bitcast.10), channel_id=1, source_target_pairs={{0,32},{32,0},{1,33},{33,1},{2,34},{34,2},{3,35},{35,3},{4,36},{36... | collective-permute-start | bytes 3145736 | tf_op jit(solution)/shard_map/ppermute | solution.py:314
  104.0 10.2 %all-to-all-start.2 = ((bf16[4,64,256]{2,1,0:T(8,128)(2,1)}), bf16[4,64,256]{2,1,0:T(8,128)(2,1)S(1)}, u32[]{:S(2)}, u32[]{:S(2)}) async-start(bf16[4,64,256]{2,1,0:T(8,128)(2,1)} %get-tuple-element.28), calls=%async_computation.2 | async-start | bytes 262144 | tf_op jit(solution)/shard_map/all_to_all | solution.py:339
Sparse Core Ops, SparseCore 0:
  28.9 47.3 all-gather.1
